TPU v7x, 32 devices: a whole 2x2x4 slice. The times are simulated.
32 devices in a mesh: dp: 4 (over x, core), ctx: 8 (over z, y).
Axes of the slice: x: 2, y: 2, z: 4, core: 2. Of those that a mesh axis runs over, the one named last changes fastest.
Arguments:
- tokens: bfloat16 [8, 512, 2048], P('dp', 'ctx'), may hold values from -43 to 43
- cotangent: bfloat16 [8, 512, 2048], P('dp', 'ctx'), may hold values from -6 to 6
- attn_gain: bfloat16 [2048], P(('dp', 'ctx')), may hold values from 0.5 to 1.5
- query_weight: bfloat16 [2048, 2048], P(('dp', 'ctx')), may hold values from -0.1875 to 0.1875
- key_weight: bfloat16 [2048, 256], P(('dp', 'ctx')), may hold values from -0.1875 to 0.1875
- value_weight: bfloat16 [2048, 256], P(('dp', 'ctx')), may hold values from -0.125 to 0.125
- output_weight: bfloat16 [2048, 2048], P(('dp', 'ctx')), may hold values from -0.75 to 0.75
- mlp_gain: bfloat16 [2048], P(('dp', 'ctx')), may hold values from 0.5 to 1.5
- gate_weight: bfloat16 [2048, 5632], P(('dp', 'ctx')), may hold values from -0.125 to 0.125
- up_weight: bfloat16 [2048, 5632], P(('dp', 'ctx')), may hold values from -0.125 to 0.125
- down_weight: bfloat16 [5632, 2048], P(None, ('dp', 'ctx')), may hold values from -0.078125 to 0.078125
Outputs:
- block_out: bfloat16 [8, 512, 2048], P('dp', 'ctx')
- tokens_grad: float32 [8, 512, 2048], P('dp', 'ctx')
- attn_gain_grad: float32 [2048], P(('dp', 'ctx'))
- query_grad: float32 [2048, 2048], P(('dp', 'ctx'))
- key_grad: float32 [2048, 256], P(('dp', 'ctx'))
- value_grad: float32 [2048, 256], P(('dp', 'ctx'))
- output_grad: float32 [2048, 2048], P(('dp', 'ctx'))
- mlp_gain_grad: float32 [2048], P(('dp', 'ctx'))
- gate_grad: float32 [2048, 5632], P(('dp', 'ctx'))
- up_grad: float32 [2048, 5632], P(('dp', 'ctx'))
- down_grad: float32 [5632, 2048], P(None, ('dp', 'ctx'))
All inputs are finite; a program needn't handle non-finite values.
Results may differ from a plain program's by a relative error of at most 0.023.
Values may be sent and summed in bfloat16 or wider, within the bound.
No kernel may reach another device: no remote copies, remote signals or barrier semaphores. Data moves between devices by JAX's collectives and lax.ppermute only.
A program may use at most 384 MiB of HBM per device.

v0:
```python
import math

import jax
import jax.numpy as jnp
from jax import lax
from jax.sharding import PartitionSpec as P

HEADS = 32
KV_HEADS = 4
HEAD_DIM = 64


norm_eps = 1e-05
rope_base = 10000.0


def rope_tables(positions):
    half = HEAD_DIM // 2
    freqs = rope_base ** (-(jnp.arange(half, dtype=jnp.float32) * 2.0) / HEAD_DIM)
    angles = positions.astype(jnp.float32)[:, None] * freqs[None, :]
    cosine = jnp.cos(angles)
    sine = jnp.sin(angles)
    return (jnp.concatenate([cosine, cosine], -1), jnp.concatenate([sine, sine], -1))


def rotate(values, cosine, sine):
    half = values.shape[-1] // 2
    turned = jnp.concatenate([-values[..., half:], values[..., :half]], -1)
    return values * cosine[:, None, :] + turned * sine[:, None, :]


def rotate_back(grads, cosine, sine):
    half = grads.shape[-1] // 2
    scaled = grads * sine[:, None, :]
    turned = jnp.concatenate([-scaled[..., half:], scaled[..., :half]], -1)
    return grads * cosine[:, None, :] - turned


def norm_back(grad_normed, normed, inverse, gain):
    scaled = grad_normed * gain
    return inverse * (scaled - normed * jnp.mean(scaled * normed, -1, keepdims=True))


def key_weights(grouped, key_block, first, positions, factor):
    scores = (
        jnp.einsum("sqgjd,skgd->sgjqk", grouped, key_block, preferred_element_type=jnp.float32)
        * factor
    )
    key_positions = first + jnp.arange(key_block.shape[1], dtype=jnp.int32)
    visible = positions[:, None] >= key_positions[None, :]
    return jnp.where(visible, jnp.exp(scores), 0.0)


def split_blocks(array, block):
    seqs, count, width = array.shape
    return jnp.moveaxis(array.reshape(seqs, count // block, block, KV_HEADS, HEAD_DIM), 1, 0)


def shards(
    tokens,
    cotangent,
    attn_gain,
    query_weight,
    key_weight,
    value_weight,
    output_weight,
    mlp_gain,
    gate_weight,
    up_weight,
    down_weight,
):
    seqs, seq_dev, width = tokens.shape
    rows = seqs * seq_dev
    groups = HEADS // KV_HEADS
    kv_width = KV_HEADS * HEAD_DIM
    factor = 1.0 / math.sqrt(HEAD_DIM)
    positions = lax.axis_index("ctx") * seq_dev + jnp.arange(seq_dev, dtype=jnp.int32)
    cosine, sine = rope_tables(positions)
    stream = tokens.astype(jnp.float32).reshape(rows, width)
    attn_full = (
        lax.all_gather(attn_gain, ("dp", "ctx"), axis=0, tiled=True),
        lax.all_gather(query_weight, ("dp", "ctx"), axis=0, tiled=True),
        lax.all_gather(key_weight, ("dp", "ctx"), axis=0, tiled=True),
        lax.all_gather(value_weight, ("dp", "ctx"), axis=0, tiled=True),
        lax.all_gather(output_weight, ("dp", "ctx"), axis=0, tiled=True),
    )
    gain_one, full_query, full_key, full_value, full_output = attn_full
    inverse_one = lax.rsqrt(jnp.mean(stream * stream, -1, keepdims=True) + norm_eps)
    normed_one = stream * inverse_one
    inputs_one = (normed_one * gain_one.astype(jnp.float32)).astype(jnp.bfloat16)
    query_raw = jnp.dot(inputs_one, full_query, preferred_element_type=jnp.float32)
    key_raw = jnp.dot(inputs_one, full_key, preferred_element_type=jnp.float32)
    values_low = (
        jnp.dot(inputs_one, full_value, preferred_element_type=jnp.float32)
        .astype(jnp.bfloat16)
        .reshape(seqs, seq_dev, kv_width)
    )
    queries = rotate(query_raw.reshape(seqs, seq_dev, HEADS, HEAD_DIM), cosine, sine).astype(
        jnp.bfloat16
    )
    keys_low = (
        rotate(key_raw.reshape(seqs, seq_dev, KV_HEADS, HEAD_DIM), cosine, sine)
        .astype(jnp.bfloat16)
        .reshape(seqs, seq_dev, kv_width)
    )
    grouped = queries.reshape(seqs, seq_dev, KV_HEADS, groups, HEAD_DIM)
    empty_totals = jnp.zeros((seqs, KV_HEADS, groups, seq_dev), jnp.float32)
    empty_mixed = jnp.zeros((seqs, KV_HEADS, groups, seq_dev, HEAD_DIM), jnp.float32)
    key_piece = lax.all_gather(keys_low, "ctx", axis=1, tiled=True)
    value_piece = lax.all_gather(values_low, "ctx", axis=1, tiled=True)
    count = key_piece.shape[1]
    absorb_block = math.gcd(count, 512)
    firsts = jnp.arange(count // absorb_block, dtype=jnp.int32) * absorb_block

    def inner(state, block_items):
        key_block, value_block, first = block_items
        totals, mixed = state
        weights = key_weights(grouped, key_block, first, positions, factor)
        totals = totals + jnp.sum(weights, -1)
        mixed = mixed + jnp.einsum(
            "sgjqk,skgd->sgjqd",
            weights.astype(jnp.bfloat16),
            value_block,
            preferred_element_type=jnp.float32,
        )
        return ((totals, mixed), None)

    result, unused = lax.scan(
        inner,
        (empty_totals, empty_mixed),
        (split_blocks(key_piece, absorb_block), split_blocks(value_piece, absorb_block), firsts),
    )
    totals, mixed = result
    attended = mixed / totals[..., None]
    heads_low = (
        jnp.transpose(attended, (0, 3, 1, 2, 4))
        .reshape(rows, HEADS * HEAD_DIM)
        .astype(jnp.bfloat16)
    )
    middle = stream + jnp.dot(heads_low, full_output, preferred_element_type=jnp.float32)
    mlp_full = (
        lax.all_gather(mlp_gain, ("dp", "ctx"), axis=0, tiled=True),
        lax.all_gather(gate_weight, ("dp", "ctx"), axis=0, tiled=True),
        lax.all_gather(up_weight, ("dp", "ctx"), axis=0, tiled=True),
        lax.all_gather(down_weight, ("dp", "ctx"), axis=1, tiled=True),
    )
    gain_two, full_gate, full_up, full_down = mlp_full
    inverse_two = lax.rsqrt(jnp.mean(middle * middle, -1, keepdims=True) + norm_eps)
    normed_two = middle * inverse_two
    inputs_two = (normed_two * gain_two.astype(jnp.float32)).astype(jnp.bfloat16)
    gate_values = jnp.dot(inputs_two, full_gate, preferred_element_type=jnp.float32)
    up_values = jnp.dot(inputs_two, full_up, preferred_element_type=jnp.float32)
    sigmoid_gate = jax.nn.sigmoid(gate_values)
    activated = gate_values * sigmoid_gate
    hidden_low = (activated * up_values).astype(jnp.bfloat16)
    result_out = (
        middle + jnp.dot(hidden_low, full_down, preferred_element_type=jnp.float32)
    ).astype(jnp.bfloat16)
    mlp_back = (
        lax.all_gather(mlp_gain, ("dp", "ctx"), axis=0, tiled=True),
        lax.all_gather(gate_weight, ("dp", "ctx"), axis=0, tiled=True),
        lax.all_gather(up_weight, ("dp", "ctx"), axis=0, tiled=True),
        lax.all_gather(down_weight, ("dp", "ctx"), axis=1, tiled=True),
    )
    back_gain_two, back_gate, back_up, back_down = mlp_back
    grad_out = cotangent.astype(jnp.float32).reshape(rows, width)
    grad_low = grad_out.astype(jnp.bfloat16)
    down_total = jnp.dot(hidden_low.T, grad_low, preferred_element_type=jnp.float32)
    grad_hidden = jnp.dot(grad_low, back_down.T, preferred_element_type=jnp.float32)
    grad_gate = (
        grad_hidden * up_values * sigmoid_gate * (1.0 + gate_values * (1.0 - sigmoid_gate))
    ).astype(jnp.bfloat16)
    grad_up = (grad_hidden * activated).astype(jnp.bfloat16)
    grad_inputs_two = jnp.dot(grad_gate, back_gate.T, preferred_element_type=jnp.float32) + jnp.dot(
        grad_up, back_up.T, preferred_element_type=jnp.float32
    )
    gain_two_total = jnp.sum(grad_inputs_two * normed_two, 0)
    grad_middle = grad_out + norm_back(
        grad_inputs_two, normed_two, inverse_two, back_gain_two.astype(jnp.float32)
    )
    gate_total = jnp.dot(inputs_two.T, grad_gate, preferred_element_type=jnp.float32)
    up_total = jnp.dot(inputs_two.T, grad_up, preferred_element_type=jnp.float32)
    mlp_grads = (
        lax.psum_scatter(gain_two_total, ("dp", "ctx"), scatter_dimension=0, tiled=True),
        lax.psum_scatter(gate_total, ("dp", "ctx"), scatter_dimension=0, tiled=True),
        lax.psum_scatter(up_total, ("dp", "ctx"), scatter_dimension=0, tiled=True),
        lax.psum_scatter(down_total, ("dp", "ctx"), scatter_dimension=1, tiled=True),
    )
    gain_two_grad, gate_grad_out, up_grad_out, down_grad_out = mlp_grads
    attn_back = (
        lax.all_gather(attn_gain, ("dp", "ctx"), axis=0, tiled=True),
        lax.all_gather(query_weight, ("dp", "ctx"), axis=0, tiled=True),
        lax.all_gather(key_weight, ("dp", "ctx"), axis=0, tiled=True),
        lax.all_gather(value_weight, ("dp", "ctx"), axis=0, tiled=True),
        lax.all_gather(output_weight, ("dp", "ctx"), axis=0, tiled=True),
    )
    back_gain_one, back_query, back_key, back_value, back_output = attn_back
    grad_branch = grad_middle.astype(jnp.bfloat16)
    output_total = jnp.dot(heads_low.T, grad_branch, preferred_element_type=jnp.float32)
    grad_heads = jnp.dot(grad_branch, back_output.T, preferred_element_type=jnp.float32)
    grad_attended = jnp.transpose(
        grad_heads.reshape(seqs, seq_dev, KV_HEADS, groups, HEAD_DIM), (0, 2, 3, 1, 4)
    )
    deltas = jnp.sum(grad_attended * attended, -1) / totals
    grad_mixed = (grad_attended / totals[..., None]).astype(jnp.bfloat16)
    all_keys, all_values = (
        lax.all_gather(keys_low, "ctx", axis=1, tiled=True),
        lax.all_gather(values_low, "ctx", axis=1, tiled=True),
    )
    length = all_keys.shape[1]
    block = math.gcd(length, 512)
    firsts = jnp.arange(length // block, dtype=jnp.int32) * block

    def backward_block(grad_query, block_items):
        key_block, value_block, first = block_items
        weights = key_weights(grouped, key_block, first, positions, factor)
        through = jnp.einsum(
            "sgjqd,skgd->sgjqk", grad_mixed, value_block, preferred_element_type=jnp.float32
        )
        grad_scores = (weights * (through - deltas[..., None])).astype(jnp.bfloat16)
        grad_query = (
            grad_query
            + jnp.einsum(
                "sgjqk,skgd->sgjqd", grad_scores, key_block, preferred_element_type=jnp.float32
            )
            * factor
        )
        grad_key = (
            jnp.einsum(
                "sgjqk,sqgjd->skgd", grad_scores, grouped, preferred_element_type=jnp.float32
            )
            * factor
        )
        grad_value = jnp.einsum(
            "sgjqk,sgjqd->skgd",
            weights.astype(jnp.bfloat16),
            grad_mixed,
            preferred_element_type=jnp.float32,
        )
        joined = jnp.concatenate(
            [grad_key.reshape(seqs, block, kv_width), grad_value.reshape(seqs, block, kv_width)], -1
        )
        return (grad_query, joined)

    grad_grouped, kv_terms = lax.scan(
        backward_block,
        jnp.zeros((seqs, KV_HEADS, groups, seq_dev, HEAD_DIM), jnp.float32),
        (split_blocks(all_keys, block), split_blocks(all_values, block), firsts),
    )
    kv_terms = jnp.moveaxis(kv_terms, 0, 1).reshape(seqs, length, 2 * kv_width)
    kv_grads = lax.psum_scatter(
        kv_terms.astype(jnp.bfloat16), "ctx", scatter_dimension=1, tiled=True
    ).astype(jnp.float32)
    grad_queries = jnp.transpose(grad_grouped, (0, 3, 1, 2, 4)).reshape(
        seqs, seq_dev, HEADS, HEAD_DIM
    )
    grad_query_low = (
        rotate_back(grad_queries, cosine, sine).astype(jnp.bfloat16).reshape(rows, HEADS * HEAD_DIM)
    )
    grad_key_low = (
        rotate_back(
            kv_grads[..., :kv_width].reshape(seqs, seq_dev, KV_HEADS, HEAD_DIM), cosine, sine
        )
        .astype(jnp.bfloat16)
        .reshape(rows, kv_width)
    )
    grad_value_low = kv_grads[..., kv_width:].astype(jnp.bfloat16).reshape(rows, kv_width)
    query_total = jnp.dot(inputs_one.T, grad_query_low, preferred_element_type=jnp.float32)
    key_total = jnp.dot(inputs_one.T, grad_key_low, preferred_element_type=jnp.float32)
    value_total = jnp.dot(inputs_one.T, grad_value_low, preferred_element_type=jnp.float32)
    grad_inputs_one = jnp.dot(grad_query_low, back_query.T, preferred_element_type=jnp.float32)
    grad_inputs_one = grad_inputs_one + jnp.dot(
        grad_key_low, back_key.T, preferred_element_type=jnp.float32
    )
    grad_inputs_one = grad_inputs_one + jnp.dot(
        grad_value_low, back_value.T, preferred_element_type=jnp.float32
    )
    gain_one_total = jnp.sum(grad_inputs_one * normed_one, 0)
    grad_tokens = grad_middle + norm_back(
        grad_inputs_one, normed_one, inverse_one, back_gain_one.astype(jnp.float32)
    )
    attn_grads = (
        lax.psum_scatter(gain_one_total, ("dp", "ctx"), scatter_dimension=0, tiled=True),
        lax.psum_scatter(query_total, ("dp", "ctx"), scatter_dimension=0, tiled=True),
        lax.psum_scatter(key_total, ("dp", "ctx"), scatter_dimension=0, tiled=True),
        lax.psum_scatter(value_total, ("dp", "ctx"), scatter_dimension=0, tiled=True),
        lax.psum_scatter(output_total, ("dp", "ctx"), scatter_dimension=0, tiled=True),
    )
    return (
        result_out.reshape(seqs, seq_dev, width),
        grad_tokens.reshape(seqs, seq_dev, width),
        attn_grads[0],
        attn_grads[1],
        attn_grads[2],
        attn_grads[3],
        attn_grads[4],
        gain_two_grad,
        gate_grad_out,
        up_grad_out,
        down_grad_out,
    )


def solution(mesh):
    placed = (
        P("dp", "ctx", None),
        P("dp", "ctx", None),
        P(("dp", "ctx")),
        P(("dp", "ctx"), None),
        P(("dp", "ctx"), None),
        P(("dp", "ctx"), None),
        P(("dp", "ctx"), None),
        P(("dp", "ctx")),
        P(("dp", "ctx"), None),
        P(("dp", "ctx"), None),
        P(None, ("dp", "ctx")),
    )
    return jax.shard_map(
        shards,
        mesh=mesh,
        in_specs=placed,
        out_specs=(
            P("dp", "ctx", None),
            P("dp", "ctx", None),
            P(("dp", "ctx")),
            P(("dp", "ctx"), None),
            P(("dp", "ctx"), None),
            P(("dp", "ctx"), None),
            P(("dp", "ctx"), None),
            P(("dp", "ctx")),
            P(("dp", "ctx"), None),
            P(("dp", "ctx"), None),
            P(None, ("dp", "ctx")),
        ),
        check_vma=False,
    )
```

profile of v0, /device:TPU:0, one launch (start us, length us, event | category | flops | bytes accessed | tf_op | source)
XLA Modules:
  0.0 4774.6 jit_solution(8322731844851056100)
XLA Ops:
  13.7 42.2 all-reduce.5
  56.8 10.9 all-gather.8.cloned.1.call-done
  69.9 31.9 all_gather.46
  102.5 21.3 all-gather.12.cloned.1.call-done
  125.3 32.0 all_gather.49
  157.6 46.6 all-gather.10.cloned.1.call-done
  204.1 12.3 copy.50
  232.4 50.5 %all-gather.14.cloned.1.call-done = bf16[2048,2048]{1,0:T(8,128)(2,1)} async-done(((bf16[64,2048]{1,0:T(8,128)(2,1)}), bf16[2048,2048]{1,0:T(8,128)(2,1)}) %all-gather.14.cloned.1.call-update) | async-done | bytes 8388624 | tf_op jit(solution)/shard_map/all_gather | solution.py:85
  287.8 141.0 %all-gather.16.cloned.1.call-done = bf16[2048,5632]{1,0:T(8,128)(2,1)} async-done(((bf16[64,5632]{1,0:T(8,128)(2,1)}), bf16[2048,5632]{1,0:T(8,128)(2,1)}) %all-gather.16.cloned.1.call-update) | async-done | bytes 23068688 | tf_op jit(solution)/shard_map/all_gather | solution.py:143
  428.9 12.3 fusion.37
  441.2 133.3 %all-gather.18.cloned.1.call-done = bf16[2048,5632]{1,0:T(8,128)(2,1)} async-done(((bf16[64,5632]{1,0:T(8,128)(2,1)}), bf16[2048,5632]{1,0:T(8,128)(2,1)}) %all-gather.18.cloned.1.call-update) | async-done | bytes 23068688 | tf_op jit(solution)/shard_map/all_gather | solution.py:144
  574.5 12.4 fusion.38
  586.8 133.4 %all-gather.20.cloned.1.call-done = bf16[5632,2048]{0,1:T(8,128)(2,1)} async-done(((bf16[5632,64]{0,1:T(8,128)(2,1)}), bf16[5632,2048]{0,1:T(8,128)(2,1)}) %all-gather.20.cloned.1.call-update) | async-done | bytes 23068688 | tf_op jit(solution)/shard_map/all_gather | solution.py:145
  720.2 15.1 multiply_convert_fusion.1
  735.3 13.8 fusion.39
  749.2 13.1 multiply_reduce_fusion
  776.4 6.4 fusion.11
  799.4 61.5 %reduce-scatter.9.cloned.1.call-done = bf16[2,64,512]{2,1,0:T(8,128)(2,1)} async-done(((bf16[2,512,512]{2,1,0:T(8,128)(2,1)}), bf16[2,64,512]{2,1,0:T(8,128)(2,1)}) %reduce-scatter.9.cloned.1.call-update) | async-done | bytes 131088 | tf_op jit(solution)/shard_map/reduce_scatter | solution.py:251
  880.5 9.3 fusion.40
  889.9 9.6 fusion.22
  899.5 19.2 fusion.42
  918.8 19.4 fusion.43
  938.5 19.4 fusion.44
  976.2 7.7 fusion.15
  984.0 12.9 fusion.3
  1001.0 40.6 all-reduce.4
  1045.4 94.7 %reduce-scatter.15.cloned.1.call-done = f32[64,256]{1,0:T(8,128)} async-done(((f32[2048,256]{1,0:T(8,128)}), f32[64,256]{1,0:T(8,128)}) %reduce-scatter.15.cloned.1.call-update) | async-done | bytes 65552 | tf_op jit(solution)/shard_map/reduce_scatter | solution.py:286
  1140.1 357.4 %reduce-scatter.11.cloned.1.call-done = f32[64,2048]{1,0:T(8,128)} async-done(((f32[2048,2048]{1,0:T(8,128)}), f32[64,2048]{1,0:T(8,128)}) %reduce-scatter.11.cloned.1.call-update) | async-done | bytes 524304 | tf_op jit(solution)/shard_map/reduce_scatter | solution.py:284
  1497.5 360.2 %reduce-scatter.17.cloned.1.call-done = f32[64,2048]{1,0:T(8,128)} async-done(((f32[2048,2048]{1,0:T(8,128)}), f32[64,2048]{1,0:T(8,128)}) %reduce-scatter.17.cloned.1.call-update) | async-done | bytes 524304 | tf_op jit(solution)/shard_map/reduce_scatter | solution.py:287
  1857.7 969.6 %reduce-scatter.19.cloned.1.call-done = f32[64,5632]{1,0:T(8,128)} async-done(((f32[2048,5632]{1,0:T(8,128)}), f32[64,5632]{1,0:T(8,128)}) %reduce-scatter.19.cloned.1.call-update) | async-done | bytes 1441808 | tf_op jit(solution)/shard_map/reduce_scatter | solution.py:185
  2827.3 970.2 %reduce-scatter.21.cloned.1.call-done = f32[64,5632]{1,0:T(8,128)} async-done(((f32[2048,5632]{1,0:T(8,128)}), f32[64,5632]{1,0:T(8,128)}) %reduce-scatter.21.cloned.1.call-update) | async-done | bytes 1441808 | tf_op jit(solution)/shard_map/reduce_scatter | solution.py:186
  3797.5 970.2 %reduce-scatter.23.cloned.1.call-done = f32[5632,64]{0,1:T(8,128)} async-done(((f32[5632,2048]{0,1:T(8,128)}), f32[5632,64]{0,1:T(8,128)}) %reduce-scatter.23.cloned.1.call-update) | async-done | bytes 1441808 | tf_op jit(solution)/shard_map/reduce_scatter | solution.py:187
  (173 shorter events, 109.4 us)
Async XLA Ops:
  7.2 48.6 %copy-start = (bf16[2,64,2048]{2,1,0:T(8,128)(2,1)S(1)}, bf16[2,64,2048]{2,1,0:T(8,128)(2,1)}, u32[]{:S(2)}) copy-start(bf16[2,64,2048]{2,1,0:T(8,128)(2,1)} %param.11) | copy-start | bytes 1572868
  7.2 60.5 %all-gather.8.cloned.1.call-start = ((), (), s32[]{:S(2)}) async-start(), calls=%async_computation.8 | async-start | bytes 1081344 | tf_op jit(solution)/shard_map/all_gather | solution.py:83
  7.9 115.9 %all-gather.12.cloned.1.call-start = ((), (), s32[]{:S(2)}) async-start(), calls=%async_computation.10 | async-start | bytes 1081344 | tf_op jit(solution)/shard_map/all_gather | solution.py:84
  8.7 195.5 %all-gather.10.cloned.1.call-start = ((), (), s32[]{:S(2)}) async-start(), calls=%async_computation.9 | async-start | bytes 8650752 | tf_op jit(solution)/shard_map/all_gather | solution.py:82
  9.4 273.5 %all-gather.14.cloned.1.call-start = ((), (), s32[]{:S(2)}) async-start(), calls=%async_computation.11 | async-start | bytes 8650752 | tf_op jit(solution)/shard_map/all_gather | solution.py:85
  10.0 418.9 %all-gather.16.cloned.1.call-start = ((), (), s32[]{:S(2)}) async-start(), calls=%async_computation.12 | async-start | bytes 23789568 | tf_op jit(solution)/shard_map/all_gather | solution.py:143
  10.6 563.9 %all-gather.18.cloned.1.call-start = ((), (), s32[]{:S(2)}) async-start(), calls=%async_computation.13 | async-start | bytes 23789568 | tf_op jit(solution)/shard_map/all_gather | solution.py:144
  11.1 709.1 %all-gather.20.cloned.1.call-start = ((), (), s32[]{:S(2)}) async-start(), calls=%async_computation.14 | async-start | bytes 23789568 | tf_op jit(solution)/shard_map/all_gather | solution.py:145
  11.9 849.1 %reduce-scatter.9.cloned.1.call-start = ((), (), s32[]{:S(2)}) async-start(), calls=%async_computation.15 | async-start | bytes 1179648 | tf_op jit(solution)/shard_map/reduce_scatter | solution.py:251
  55.8 13.4 copy-start.25
  56.1 13.6 copy-start.28
  56.8 808.8 %copy-start.8 = (bf16[2,64,2048]{2,1,0:T(8,128)(2,1)}, bf16[2,64,2048]{2,1,0:T(8,128)(2,1)S(1)}, u32[]{:S(2)}) copy-start(bf16[2,64,2048]{2,1,0:T(8,128)(2,1)S(1)} %multiply_convert_fusion.6) | copy-start | bytes 1572868
  102.5 119.7 %copy-start.17 = (bf16[2,512,256]{1,2,0:T(8,128)(2,1)}, bf16[2,512,256]{1,2,0:T(8,128)(2,1)S(1)}, u32[]{:S(2)}) copy-start(bf16[2,512,256]{1,2,0:T(8,128)(2,1)S(1)} %copy.49) | copy-start | bytes 1572868
  157.6 66.8 %copy-start.20 = (bf16[2,512,256]{1,2,0:T(8,128)(2,1)}, bf16[2,512,256]{1,2,0:T(8,128)(2,1)S(1)}, u32[]{:S(2)}) copy-start(bf16[2,512,256]{1,2,0:T(8,128)(2,1)S(1)} %copy.52) | copy-start | bytes 1572868
  232.4 55.3 %copy-start.10 = (bf16[128,2048]{1,0:T(8,128)(2,1)}, bf16[128,2048]{1,0:T(8,128)(2,1)S(1)}, u32[]{:S(2)}) copy-start(bf16[128,2048]{1,0:T(8,128)(2,1)S(1)} %convert_element_type.121) | copy-start | bytes 1572868
  287.8 286.6 %copy-start.4 = (bf16[128,2048]{1,0:T(8,128)(2,1)}, bf16[128,2048]{1,0:T(8,128)(2,1)S(1)}, u32[]{:S(2)}) copy-start(bf16[128,2048]{1,0:T(8,128)(2,1)S(1)} %multiply_convert_fusion.4) | copy-start | bytes 1572868
  735.3 13.8 copy-start.7
  735.3 13.8 copy-start.6
  776.4 6.4 copy-start.9
  776.4 6.4 copy-start.16
  783.9 8.1 copy-start.12
  799.2 246.2 %reduce-scatter.13.cloned.1.call-start = ((), (), s32[]{:S(2)}) async-start(), calls=%async_computation.17 | async-start | bytes 2162688 | tf_op jit(solution)/shard_map/reduce_scatter | solution.py:285
  865.6 274.5 %reduce-scatter.15.cloned.1.call-start = ((), (), s32[]{:S(2)}) async-start(), calls=%async_computation.18 | async-start | bytes 2162688 | tf_op jit(solution)/shard_map/reduce_scatter | solution.py:286
  867.4 630.1 %reduce-scatter.11.cloned.1.call-start = ((), (), s32[]{:S(2)}) async-start(), calls=%async_computation.16 | async-start | bytes 17301504 | tf_op jit(solution)/shard_map/reduce_scatter | solution.py:284
  889.8 967.9 %reduce-scatter.17.cloned.1.call-start = ((), (), s32[]{:S(2)}) async-start(), calls=%async_computation.19 | async-start | bytes 17301504 | tf_op jit(solution)/shard_map/reduce_scatter | solution.py:287
  899.5 1927.9 %reduce-scatter.19.cloned.1.call-start = ((), (), s32[]{:S(2)}) async-start(), calls=%async_computation.20 | async-start | bytes 47579136 | tf_op jit(solution)/shard_map/reduce_scatter | solution.py:185
  918.7 2878.8 %reduce-scatter.21.cloned.1.call-start = ((), (), s32[]{:S(2)}) async-start(), calls=%async_computation.21 | async-start | bytes 47579136 | tf_op jit(solution)/shard_map/reduce_scatter | solution.py:186
  938.2 3829.5 %reduce-scatter.23.cloned.1.call-start = ((), (), s32[]{:S(2)}) async-start(), calls=%async_computation.22 | async-start | bytes 47579136 | tf_op jit(solution)/shard_map/reduce_scatter | solution.py:187
  976.2 7.7 copy-start.5
  984.0 12.9 copy-start.18
  984.0 13.3 copy-start.19
  997.3 45.5 copy-start.3
  (14 other events, 35.7 us)
Sparse Core Ops, SparseCore 0:
  11.1 56.5 all-gather.7
  70.8 52.9 all-gather.11
  126.8 77.3 all-gather.9
  207.0 75.8 all-gather.13
  285.6 143.1 all-gather.15
  431.7 142.7 all-gather.17
  577.4 142.7 all-gather.19
  799.3 61.5 reduce-scatter.8
  865.7 136.8 reduce-scatter.12
  1005.2 134.7 reduce-scatter.14
  1143.0 354.4 reduce-scatter.10
  1500.3 357.3 reduce-scatter.16
  1860.7 966.5 reduce-scatter.18
  2830.2 967.3 reduce-scatter.20
  3800.4 967.3 reduce-scatter.22
where the time goes:
time: 4780 us; the launch traced here: 4770 us
  waiting for transfers between devices  4330 us (91%)
  matrix products  217 us (5%)
  blocking collectives  147 us (3%)
  local copies, waits for them, and re-layouts  56.6 us (1%)
    reduce_scatter x1, waiting for transfers between devices, shards(): lax.psum_scatter(up_total, ('dp', 'ctx'), scatter_dimension=0, tiled=True)  970 us
    reduce_scatter x1, waiting for transfers between devices, shards(): lax.psum_scatter(down_total, ('dp', 'ctx'), scatter_dimension=1, tiled=True)  970 us
    reduce_scatter x1, waiting for transfers between devices, shards(): lax.psum_scatter(gate_total, ('dp', 'ctx'), scatter_dimension=0, tiled=True)  970 us
    reduce_scatter x1, waiting for transfers between devices, shards(): lax.psum_scatter(output_total, ('dp', 'ctx'), scatter_dimension=0, tiled=...  360 us
    reduce_scatter x1, waiting for transfers between devices, shards(): lax.psum_scatter(query_total, ('dp', 'ctx'), scatter_dimension=0, tiled=T...  357 us
    all_gather x1, waiting for transfers between devices, shards(): lax.all_gather(gate_weight, ('dp', 'ctx'), axis=0, tiled=True)  141 us
    all_gather x1, waiting for transfers between devices, shards(): lax.all_gather(down_weight, ('dp', 'ctx'), axis=1, tiled=True)  133 us
    all_gather x1, waiting for transfers between devices, shards(): lax.all_gather(up_weight, ('dp', 'ctx'), axis=0, tiled=True)  133 us
  transfers between devices with their start and end apart: 15, of which 14 were waited for; matrix products, arithmetic and copies ran while one was open for 4% of the time, Pallas kernels for 0%

commit v1 on v0

v1 whole, which is shorter than its diff:
```python
import math

import jax
import jax.numpy as jnp
from jax import lax
from jax.sharding import PartitionSpec as P

HEADS = 32
KV_HEADS = 4
HEAD_DIM = 64
GROUPS = HEADS // KV_HEADS

norm_eps = 1e-05
rope_base = 10000.0

BF = jnp.bfloat16
F32 = jnp.float32


def dot(left, right):
    return jnp.dot(left, right, preferred_element_type=F32)


def dot_nt(left, right):
    return lax.dot_general(left, right, (((1,), (1,)), ((), ())), preferred_element_type=F32)


def dot_tn(left, right):
    return lax.dot_general(left, right, (((0,), (0,)), ((), ())), preferred_element_type=F32)


class Bit:
    def __init__(self, axis, bit, size):
        self.axis, self.bit = axis, bit
        self.pairs = [(i, i ^ (1 << bit)) for i in range(size)]

    def mine(self):
        return (lax.axis_index(self.axis) >> self.bit) & 1

    def swap(self, value):
        return lax.ppermute(value, self.axis, self.pairs)


def rope_tables(positions):
    half = HEAD_DIM // 2
    freqs = rope_base ** (-(jnp.arange(half, dtype=F32) * 2.0) / HEAD_DIM)
    angles = positions.astype(F32)[:, None] * freqs[None, :]
    cosine = jnp.cos(angles)
    sine = jnp.sin(angles)
    return (jnp.concatenate([cosine, cosine], -1), jnp.concatenate([sine, sine], -1))


def turn(values):
    half = values.shape[-1] // 2
    return jnp.concatenate([-values[..., half:], values[..., :half]], -1)


def rotate(values, cosine, sine):
    return values * cosine[:, None, :] + turn(values) * sine[:, None, :]


def rotate_back(grads, cosine, sine):
    return grads * cosine[:, None, :] - turn(grads * sine[:, None, :])


def norm_back(grad_normed, normed, inverse, gain):
    scaled = grad_normed * gain
    return inverse * (scaled - normed * jnp.mean(scaled * normed, -1, keepdims=True))


def gather_bits(value, bits):
    acc = value[None]
    for bit in bits:
        acc = jnp.concatenate([acc, bit.swap(acc)], 0)
    return acc


def reduce_bits(blocks, bits):
    acc = blocks
    for bit in reversed(bits):
        half = acc.shape[0] // 2
        got = bit.swap(acc[half:].astype(BF))
        acc = acc[:half].astype(F32) + got.astype(F32)
    return acc[0]


def trade(value, dim, bit):
    mine = bit.mine()
    got = bit.swap(lax.dynamic_index_in_dim(value, 1 - mine, dim, True))
    keep = lax.dynamic_index_in_dim(value, mine, dim, True)
    low = jnp.where(mine == 0, keep, got)
    high = jnp.where(mine == 0, got, keep)
    return jnp.concatenate([low, high], dim)


def absolute(blocks, index, bits):
    def one(j):
        other = index ^ j
        slot = sum(((other >> b.bit) & 1) << i for i, b in enumerate(bits))
        return lax.dynamic_index_in_dim(blocks, slot, 0, False)

    return [one(j) for j in range(blocks.shape[0])]


def relative(blocks, index, bits):
    def one(r):
        code = sum(((r >> i) & 1) << b.bit for i, b in enumerate(bits))
        return lax.dynamic_index_in_dim(blocks, index ^ code, 0, False)

    return jnp.stack([one(r) for r in range(blocks.shape[0])])


def shards(
    dp,
    ctx,
    tokens,
    cotangent,
    attn_gain,
    query_weight,
    key_weight,
    value_weight,
    output_weight,
    mlp_gain,
    gate_weight,
    up_weight,
    down_weight,
):
    seqs, seq_dev, width = tokens.shape
    rows = seqs * seq_dev
    depth = query_weight.shape[0]
    ff = gate_weight.shape[1]
    factor = 1.0 / math.sqrt(HEAD_DIM)
    head_cols = GROUPS * HEAD_DIM

    bit_x, bit_core = Bit("dp", 1, dp), Bit("dp", 0, dp)
    ctx_bits = [Bit("ctx", b, ctx) for b in reversed(range(ctx.bit_length() - 1))]
    near = ctx_bits[-2]
    far = [b for b in ctx_bits if b is not near]
    team = [bit_x, near, bit_core]
    dp_bits = [bit_x, bit_core]
    d_index = lax.axis_index("dp")
    c_index = lax.axis_index("ctx")

    levels = len(ctx_bits)
    split_shape = (2, 2) + (2,) * levels + (depth,)
    near_dim = 2 + levels - 2
    far_dims = [2 + k for k in range(levels) if ctx_bits[k] is not near]
    order = far_dims + [0, near_dim, 1, 2 + levels]
    back_order = [order.index(k) for k in range(len(order))]
    pieces = 1 << len(far)
    piece = width // pieces

    def to_pieces(array):
        count = array.shape[0]
        out = array.reshape((count,) + split_shape)
        for k, bit in zip(far_dims, far):
            out = jnp.where(bit.mine() == 1, jnp.flip(out, k + 1), out)
        return out.transpose([0] + [k + 1 for k in order]).reshape(count, width)

    def from_pieces(array):
        count = array.shape[0]
        out = array.reshape([count] + [split_shape[k] for k in order])
        out = out.transpose([0] + [k + 1 for k in back_order])
        for k, bit in zip(far_dims, far):
            out = jnp.where(bit.mine() == 1, jnp.flip(out, k + 1), out)
        return out.reshape(count, width)

    gains = jnp.stack([attn_gain, mlp_gain])
    gains = jnp.stack(absolute(gather_bits(gains, dp_bits), d_index, dp_bits))
    gains = jnp.stack(absolute(gather_bits(gains, ctx_bits), c_index, ctx_bits))
    gains = gains.transpose(2, 1, 0, 3).reshape(2, width).astype(F32)
    gain_one, gain_two = gains[0], gains[1]

    own_qkv = jnp.concatenate(
        [
            query_weight.reshape(depth, dp, head_cols),
            key_weight.reshape(depth, dp, HEAD_DIM),
            value_weight.reshape(depth, dp, HEAD_DIM),
        ],
        -1,
    ).transpose(1, 0, 2)
    qkv_cols = own_qkv.shape[-1]
    own_qkv = own_qkv.reshape(2, 2, depth, qkv_cols)
    own_qkv = trade(trade(own_qkv, 0, bit_x), 1, bit_core).reshape(dp, depth, qkv_cols)
    qkv_rel = gather_bits(own_qkv, ctx_bits)
    qkv = jnp.stack(absolute(qkv_rel, c_index, ctx_bits), 1).reshape(width, qkv_cols)
    out_rel = gather_bits(output_weight, ctx_bits)
    out_full = jnp.concatenate(absolute(out_rel, c_index, ctx_bits), 0)

    def mlp_slices(weight):
        own = weight.reshape(depth, 2, 2, 2, ff // 8).transpose(1, 2, 3, 0, 4)
        own = trade(own, 2, bit_core)
        own = trade(own, 0, bit_x)
        own = trade(own, 1, near)
        own = own.reshape(piece, ff // 8)
        parts = [own]
        for bit in far:
            parts = parts + [bit.swap(p) for p in parts]
        return parts

    gate_parts = mlp_slices(gate_weight)
    up_parts = mlp_slices(up_weight)
    down_parts = mlp_slices(down_weight.T)
    digit = [sum(((k >> i) & 1) << (len(far) - 1 - i) for i in range(len(far))) for k in range(pieces)]

    def part_cols(array, k):
        return array[:, digit[k] * piece : (digit[k] + 1) * piece]

    positions = c_index * seq_dev + jnp.arange(seq_dev, dtype=jnp.int32)
    cosine, sine = rope_tables(positions)
    stream = tokens.astype(F32).reshape(rows, width)
    inverse_one = lax.rsqrt(jnp.mean(stream * stream, -1, keepdims=True) + norm_eps)
    normed_one = stream * inverse_one
    inputs_one = (normed_one * gain_one).astype(BF)
    a1 = gather_bits(inputs_one, dp_bits).reshape(dp * rows, width)
    all_seqs = dp * seqs
    raw = dot(a1, qkv)
    queries = rotate(
        raw[:, :head_cols].reshape(all_seqs, seq_dev, GROUPS, HEAD_DIM), cosine, sine
    ).astype(BF)
    keys_own = rotate(
        raw[:, head_cols : head_cols + HEAD_DIM].reshape(all_seqs, seq_dev, 1, HEAD_DIM), cosine, sine
    ).astype(BF)
    values_own = raw[:, head_cols + HEAD_DIM :].astype(BF).reshape(all_seqs, seq_dev, HEAD_DIM)
    kv_own = jnp.concatenate([keys_own[:, :, 0, :], values_own], -1)
    kv = gather_bits(kv_own, ctx_bits)
    rel = jnp.arange(ctx, dtype=jnp.int32)
    rel_abs = sum(((rel >> i) & 1) << b.bit for i, b in enumerate(ctx_bits)) ^ c_index
    key_positions = (rel_abs[:, None] * seq_dev + jnp.arange(seq_dev, dtype=jnp.int32)[None]).reshape(-1)
    kv = kv.transpose(1, 0, 2, 3).reshape(all_seqs, ctx * seq_dev, 2 * HEAD_DIM)
    keys, values = kv[..., :HEAD_DIM], kv[..., HEAD_DIM:]
    scores = jnp.einsum("sqjd,skd->sjqk", queries, keys, preferred_element_type=F32) * factor
    visible = positions[:, None] >= key_positions[None, :]
    weights = jnp.where(visible, jnp.exp(scores), 0.0)
    weights_low = weights.astype(BF)
    totals = jnp.sum(weights, -1)
    mixed = jnp.einsum("sjqk,skd->sjqd", weights_low, values, preferred_element_type=F32)
    attended = mixed / totals[..., None]
    heads_low = attended.transpose(0, 2, 1, 3).reshape(dp * rows, head_cols).astype(BF)
    branch = dot(heads_low, out_full)
    middle = stream + reduce_bits(branch.reshape(dp, rows, width), dp_bits)

    inverse_two = lax.rsqrt(jnp.mean(middle * middle, -1, keepdims=True) + norm_eps)
    normed_two = middle * inverse_two
    inputs_two = to_pieces((normed_two * gain_two).astype(BF))
    grad_low = to_pieces(cotangent.reshape(rows, width))
    crowd = 8 * rows
    a2 = gather_bits(inputs_two, team).reshape(crowd, width)
    gb = gather_bits(grad_low, team).reshape(crowd, width)

    def through(array, parts):
        total = None
        for k in range(pieces):
            term = dot(part_cols(array, k), parts[k])
            total = term if total is None else total + term
        return total

    gate_values = through(a2, gate_parts)
    up_values = through(a2, up_parts)
    sigmoid_gate = jax.nn.sigmoid(gate_values)
    activated = gate_values * sigmoid_gate
    hidden = (activated * up_values).astype(BF)
    by_digit = sorted(range(pieces), key=lambda k: digit[k])
    down_out = jnp.concatenate([dot_nt(hidden, down_parts[k]) for k in by_digit], -1)
    result = middle + from_pieces(reduce_bits(down_out.reshape(8, rows, width), team))

    grad_hidden = through(gb, down_parts)
    grad_gate = (
        grad_hidden * up_values * sigmoid_gate * (1.0 + gate_values * (1.0 - sigmoid_gate))
    ).astype(BF)
    grad_up = (grad_hidden * activated).astype(BF)
    grad_a2 = jnp.concatenate(
        [dot_nt(grad_gate, gate_parts[k]) + dot_nt(grad_up, up_parts[k]) for k in by_digit], -1
    )
    grad_inputs_two = from_pieces(reduce_bits(grad_a2.reshape(8, rows, width), team))

    def mlp_return(left, right):
        terms = [dot_tn(part_cols(left, k), right) for k in range(pieces)]
        for bit in reversed(far):
            half = len(terms) // 2
            got = [bit.swap(t.astype(BF)) for t in terms[half:]]
            terms = [t + g.astype(F32) for t, g in zip(terms[:half], got)]
        own = terms[0].astype(BF).reshape(2, 2, 2, depth, ff // 8)
        own = trade(own, 1, near)
        own = trade(own, 0, bit_x)
        own = trade(own, 2, bit_core)
        return own.transpose(3, 0, 1, 2, 4).reshape(depth, ff).astype(F32)

    gate_grad = mlp_return(a2, grad_gate)
    up_grad = mlp_return(a2, grad_up)
    down_grad = mlp_return(gb, hidden).T

    grad_out = cotangent.astype(F32).reshape(rows, width)
    gain_two_total = jnp.sum(grad_inputs_two * normed_two, 0)
    grad_middle = grad_out + norm_back(grad_inputs_two, normed_two, inverse_two, gain_two)

    grad_branch = gather_bits(grad_middle.astype(BF), dp_bits).reshape(dp * rows, width)
    output_total = dot_tn(heads_low, grad_branch)
    grad_heads = dot_nt(grad_branch, out_full)
    grad_attended = grad_heads.reshape(all_seqs, seq_dev, GROUPS, HEAD_DIM).transpose(0, 2, 1, 3)
    deltas = jnp.sum(grad_attended * attended, -1) / totals
    grad_mixed = (grad_attended / totals[..., None]).astype(BF)
    through_values = jnp.einsum("sjqd,skd->sjqk", grad_mixed, values, preferred_element_type=F32)
    grad_scores = (weights * (through_values - deltas[..., None])).astype(BF)
    grad_queries = jnp.einsum("sjqk,skd->sqjd", grad_scores, keys, preferred_element_type=F32) * factor
    grad_keys = jnp.einsum("sjqk,sqjd->skd", grad_scores, queries, preferred_element_type=F32) * factor
    grad_values = jnp.einsum("sjqk,sjqd->skd", weights_low, grad_mixed, preferred_element_type=F32)
    grad_kv = jnp.concatenate([grad_keys, grad_values], -1)
    grad_kv = grad_kv.reshape(all_seqs, ctx, seq_dev, 2 * HEAD_DIM).transpose(1, 0, 2, 3)
    grad_kv = reduce_bits(grad_kv, ctx_bits)
    grad_query_low = rotate_back(grad_queries, cosine, sine).astype(BF).reshape(dp * rows, head_cols)
    grad_key_low = rotate_back(grad_kv[:, :, None, :HEAD_DIM], cosine, sine).astype(BF)
    grad_key_low = grad_key_low.reshape(dp * rows, HEAD_DIM)
    grad_value_low = grad_kv[..., HEAD_DIM:].astype(BF).reshape(dp * rows, HEAD_DIM)
    grad_raw = jnp.concatenate([grad_query_low, grad_key_low, grad_value_low], -1)
    qkv_total = dot_tn(a1, grad_raw)
    grad_a1 = dot_nt(grad_raw, qkv)
    grad_inputs_one = reduce_bits(grad_a1.reshape(dp, rows, width), dp_bits)
    gain_one_total = jnp.sum(grad_inputs_one * normed_one, 0)
    grad_tokens = grad_middle + norm_back(grad_inputs_one, normed_one, inverse_one, gain_one)

    qkv_blocks = qkv_total.reshape(dp, ctx, depth, qkv_cols).transpose(1, 0, 2, 3)
    qkv_own = reduce_bits(relative(qkv_blocks, c_index, ctx_bits), ctx_bits).astype(BF).reshape(2, 2, depth, qkv_cols)
    qkv_own = trade(trade(qkv_own, 1, bit_core), 0, bit_x).reshape(dp, depth, qkv_cols).astype(F32)
    query_grad = qkv_own[..., :head_cols].transpose(1, 0, 2).reshape(depth, dp * head_cols)
    key_grad = qkv_own[..., head_cols : head_cols + HEAD_DIM].transpose(1, 0, 2).reshape(depth, dp * HEAD_DIM)
    value_grad = qkv_own[..., head_cols + HEAD_DIM :].transpose(1, 0, 2).reshape(depth, dp * HEAD_DIM)
    out_blocks = output_total.reshape(ctx, depth, width)
    output_grad = reduce_bits(relative(out_blocks, c_index, ctx_bits), ctx_bits)

    gain_totals = lax.psum_scatter(
        jnp.stack([gain_one_total, gain_two_total]), ("dp", "ctx"), scatter_dimension=1, tiled=True
    )
    return (
        result.astype(BF).reshape(seqs, seq_dev, width),
        grad_tokens.reshape(seqs, seq_dev, width),
        gain_totals[0],
        query_grad,
        key_grad,
        value_grad,
        output_grad,
        gain_totals[1],
        gate_grad,
        up_grad,
        down_grad,
    )


def solution(mesh):
    dp, ctx = mesh.shape["dp"], mesh.shape["ctx"]

    def local(*args):
        return shards(dp, ctx, *args)

    weight = P(("dp", "ctx"), None)
    flat = P(("dp", "ctx"))
    acts = P("dp", "ctx", None)
    down = P(None, ("dp", "ctx"))
    return jax.shard_map(
        local,
        mesh=mesh,
        in_specs=(acts, acts, flat, weight, weight, weight, weight, flat, weight, weight, down),
        out_specs=(acts, acts, flat, weight, weight, weight, weight, flat, weight, weight, down),
        check_vma=False,
    )
```

time: 4780 us -> 1010 us (0.21)
  waiting for transfers between devices: 4330 us -> 449 us
  other arithmetic: 13.6 us -> 181 us
  blocking collectives: 147 us -> 0 us
  local copies, waits for them, and re-layouts: 56.6 us -> 181 us
  matrix products: 217 us -> 99.8 us
  starting transfers between devices: 0.98 us -> 71.7 us
    reduce_scatter x8 -> x0, waiting for transfers between devices: 3780 us -> none  [the longest x1 970 us: shards(): lax.psum_scatter(up_total, ('dp', 'ctx'), scatter_dimension=0, tiled=True)]
    all_gather x7 -> x0, waiting for transfers between devices: 537 us -> none  [the longest x1 141 us: shards(): lax.all_gather(gate_weight, ('dp', 'ctx'), axis=0, tiled=True)]
    ppermute x0 -> x83, waiting for transfers between devices: none -> 334 us  [swap(): return lax.ppermute(value, self.axis, self.pairs)]
    dot_general x27 -> x48, matrix products: 217 us -> 99.8 us  [the longest x14 29.8 us: dot(): return jnp.dot(left, right, preferred_element_type=F32)]
    unnamed x15 -> x2, waiting for transfers between devices: 4.46 us -> 114 us
    unnamed x2 -> x0, blocking collectives: 82.8 us -> none
    ppermute x0 -> x83, starting transfers between devices: none -> 71.7 us  [swap(): return lax.ppermute(value, self.axis, self.pairs)]
    all_gather x2 -> x0, blocking collectives: 63.9 us -> none  [the longest x1 32 us: shards(): value_piece = lax.all_gather(values_low, 'ctx', axis=1, tiled=True)]
  transfers between devices with their start and end apart: 15 -> 84, of which waited for: 14 -> 38; matrix products, arithmetic and copies ran while one was open for 4% -> 39% of each run, Pallas kernels for 0% -> 0%
where the time goes in v1:
time: 1010 us; the launch traced here: 1000 us
  waiting for transfers between devices  449 us (44%)
  local copies, waits for them, and re-layouts  181 us (18%)
  other arithmetic  181 us (18%)
  matrix products  99.8 us (10%)
  starting transfers between devices  71.7 us (7%)
  between operations  17.1 us (2%)
    ppermute x83, waiting for transfers between devices, swap(): return lax.ppermute(value, self.axis, self.pairs)  334 us
    unnamed x2, waiting for transfers between devices  114 us
    ppermute x83, starting transfers between devices, swap(): return lax.ppermute(value, self.axis, self.pairs)  71.7 us
    dot_general x14, matrix products, dot(): return jnp.dot(left, right, preferred_element_type=F32)  29.8 us
    select_n x20, other arithmetic, trade(): high = jnp.where(mine == 0, got, keep)  27.4 us
    dot_general x14, matrix products, dot_nt(): lax.dot_general(left, right, (((1,), (1,)), ((), ())), preferred_element_...  26.8 us
    concatenate x24, other arithmetic, gather_bits(): acc = jnp.concatenate([acc, bit.swap(acc)], 0)  26.5 us
    dot_general x14, matrix products, dot_tn(): lax.dot_general(left, right, (((0,), (0,)), ((), ())), preferred_element_...  23.5 us
  transfers between devices with their start and end apart: 84, of which 38 were waited for; matrix products, arithmetic and copies ran while one was open for 39% of the time, Pallas kernels for 0%

profile of v1, /device:TPU:0, one launch (start us, length us, event | category | flops | bytes accessed | tf_op | source)
XLA Modules:
  0.0 999.7 jit_solution(16435638964067834225)
XLA Ops:
  23.7 10.3 %rev.33 = bf16[128,2,2,2,2,2,64]{6,5,4,3,2,1,0:T(2,128)(2,1)} reverse(bf16[128,2,2,2,2,2,64]{6,5,4,3,2,1,0:T(2,128)(2,1)} %broadcast_select_fusion), dimensions={5} | reverse | bytes 1048576 | tf_op jit(solution)/shard_map/jit(_flip)/rev | solution.py:157
  110.4 9.2 collective-permute-done.10
  121.5 8.2 collective-permute-done.17
  131.1 26.3 %collective-permute-done.11 = bf16[4,4,64,640]{3,2,1,0:T(8,128)(2,1)S(1)} collective-permute-done((bf16[4,4,64,640]{3,2,1,0:T(8,128)(2,1)S(1)}, bf16[4,4,64,640]{3,2,1,0:T(8,128)(2,1)S(1)}, u32[]{:S(2)}, u32[]{:S(2)}) %collective-permute-start.11) | collective-permute-done | bytes 1310752 | tf_op jit(solution)/shard_map/ppermute | solution.py:41
  161.5 8.0 collective-permute-done.12
  180.8 9.2 collective-permute-done.14
  219.2 7.6 collective-permute-done.19
  236.4 7.6 rev.29
  275.7 34.2 %collective-permute-done.21 = bf16[2,128,2048]{1,2,0:T(8,128)(2,1)S(1)} collective-permute-done((bf16[2,128,2048]{1,2,0:T(8,128)(2,1)}, bf16[2,128,2048]{1,2,0:T(8,128)(2,1)S(1)}, u32[]{:S(2)}, u32[]{:S(2)}) %collective-permute-start.21) | collective-permute-done | bytes 1048608 | tf_op jit(solution)/shard_map/ppermute | solution.py:41
  326.2 6.6 copy.178
  342.0 13.4 %collective-permute-done.26 = bf16[512,704]{0,1:T(8,128)(2,1)S(1)} collective-permute-done((bf16[512,704]{0,1:T(8,128)(2,1)}, bf16[512,704]{0,1:T(8,128)(2,1)S(1)}, u32[]{:S(2)}, u32[]{:S(2)}) %collective-permute-start.26) | collective-permute-done | bytes 720928 | tf_op jit(solution)/shard_map/ppermute | solution.py:41
  364.6 6.5 copy.155
  379.9 6.5 collective-permute-done.34
  388.6 13.0 %collective-permute-done.28 = bf16[512,704]{0,1:T(8,128)(2,1)} collective-permute-done((bf16[512,704]{0,1:T(8,128)(2,1)S(1)}, bf16[512,704]{0,1:T(8,128)(2,1)}, u32[]{:S(2)}, u32[]{:S(2)}) %collective-permute-start.28) | collective-permute-done | bytes 720928 | tf_op jit(solution)/shard_map/ppermute | solution.py:41
  455.1 8.1 collective-permute-done.66
  468.6 10.1 %collective-permute-done.72 = bf16[512,704]{0,1:T(8,128)(2,1)S(1)} collective-permute-done((bf16[512,704]{0,1:T(8,128)(2,1)S(1)}, bf16[512,704]{0,1:T(8,128)(2,1)S(1)}, u32[]{:S(2)}, u32[]{:S(2)}) %collective-permute-start.72) | collective-permute-done | bytes 720928 | tf_op jit(solution)/shard_map/ppermute | solution.py:41
  482.2 27.4 %collective-permute-done.78 = bf16[512,704]{0,1:T(8,128)(2,1)S(1)} collective-permute-done((bf16[512,704]{0,1:T(8,128)(2,1)S(1)}, bf16[512,704]{0,1:T(8,128)(2,1)S(1)}, u32[]{:S(2)}, u32[]{:S(2)}) %collective-permute-start.78) | collective-permute-done | bytes 720928 | tf_op jit(solution)/shard_map/ppermute | solution.py:41
  517.9 7.3 collective-permute-done.71
  525.2 33.0 %collective-permute-done.73 = bf16[512,704]{0,1:T(8,128)(2,1)} collective-permute-done((bf16[512,704]{0,1:T(8,128)(2,1)}, bf16[512,704]{0,1:T(8,128)(2,1)}, u32[]{:S(2)}, u32[]{:S(2)}) %collective-permute-start.73) | collective-permute-done | bytes 720928 | tf_op jit(solution)/shard_map/ppermute | solution.py:41
  562.7 10.3 %collective-permute-done.79 = bf16[512,704]{0,1:T(8,128)(2,1)} collective-permute-done((bf16[512,704]{0,1:T(8,128)(2,1)}, bf16[512,704]{0,1:T(8,128)(2,1)}, u32[]{:S(2)}, u32[]{:S(2)}) %collective-permute-start.79) | collective-permute-done | bytes 720928 | tf_op jit(solution)/shard_map/ppermute | solution.py:41
  592.0 6.1 collective-permute-done.80
  638.9 6.1 collective-permute-done.49
  649.7 11.0 %rev.35 = f32[128,2,2,2,2,2,64]{6,5,4,3,2,1,0:T(2,128)} reverse(f32[128,2,2,2,2,2,64]{6,5,4,3,2,1,0:T(2,128)} %reverse_select_fusion), dimensions={5} | reverse | bytes 2097152 | tf_op jit(solution)/shard_map/jit(_flip)/rev | solution.py:165
  660.8 7.8 multiply_reduce_fusion
  681.4 9.1 collective-permute-done.50
  720.9 11.1 %rev.31 = f32[128,2,2,2,2,2,64]{6,5,4,3,2,1,0:T(2,128)} reverse(f32[128,2,2,2,2,2,64]{6,5,4,3,2,1,0:T(2,128)} %reverse_select_fusion.1), dimensions={5} | reverse | bytes 2097152 | tf_op jit(solution)/shard_map/jit(_flip)/rev | solution.py:165
  765.4 7.1 collective-permute-done.52
  774.3 6.5 collective-permute-done.53
  825.8 5.9 collective-permute-done.57
  837.6 11.5 %collective-permute-done.58 = bf16[2,4,64,640]{3,2,1,0:T(8,128)(2,1)S(1)} collective-permute-done((bf16[2,4,64,640]{3,2,1,0:T(8,128)(2,1)S(1)}, bf16[2,4,64,640]{3,2,1,0:T(8,128)(2,1)S(1)}, u32[]{:S(2)}, u32[]{:S(2)}) %collective-permute-start.58) | collective-permute-done | bytes 655392 | tf_op jit(solution)/shard_map/ppermute | solution.py:41
  852.7 15.2 %collective-permute-done.59 = bf16[1,4,64,640]{3,2,1,0:T(8,128)(2,1)S(1)} collective-permute-done((bf16[1,4,64,640]{3,2,1,0:T(8,128)(2,1)}, bf16[1,4,64,640]{3,2,1,0:T(8,128)(2,1)S(1)}, u32[]{:S(2)}, u32[]{:S(2)}) %collective-permute-start.59) | collective-permute-done | bytes 327712 | tf_op jit(solution)/shard_map/ppermute | solution.py:41
  873.0 114.2 %reduce-scatter.4.cloned.1.call-done = f32[64,2]{1,0:T(8,128)} async-done(((f32[2048,2]{1,0:T(8,128)}), f32[64,2]{1,0:T(8,128)}) %reduce-scatter.4.cloned.1.call-update) | async-done | bytes 528
  (715 shorter events, 508.2 us)
Async XLA Ops:
  7.2 980.0 %reduce-scatter.4.cloned.1.call-start = ((), (), s32[]{:S(2)}) async-start(), calls=%async_computation.1 | async-start | bytes 1081344
  8.0 44.1 %collective-permute-start = (bf16[1,2,64]{2,1,0:T(2,128)(2,1)S(1)}, bf16[1,2,64]{2,1,0:T(2,128)(2,1)S(1)}, u32[]{:S(2)}, u32[]{:S(2)}) collective-permute-start(bf16[1,2,64]{2,1,0:T(2,128)(2,1)S(1)} %maximum_bitcast_fusion.3), channel_id=1, source_target_pairs={{0,16},{8,24},{16,0},{24,8},{1,17},{9,25},{17,1},{25,9},{2,18},{10... | collective-permute-start | bytes 776 | tf_op jit(solution)/shard_map/ppermute | solution.py:41
  14.9 61.2 %collective-permute-start.7 = (bf16[1,2,64,640]{3,2,1,0:T(8,128)(2,1)}, bf16[1,2,64,640]{3,2,1,0:T(8,128)(2,1)}, u32[]{:S(2)}, u32[]{:S(2)}) collective-permute-start(bf16[1,2,64,640]{3,2,1,0:T(8,128)(2,1)} %constant_dynamic-slice_fusion.11), channel_id=1, source_target_pairs={{0,16},{8,24},{16,0},{24,8},{1,17},{9,25},{17,1},{25,9},{2,18},{10... | collective-permute-start | bytes 491528 | tf_op jit(solution)/shard_map/ppermute | solution.py:41
  14.9 62.8 %collective-permute-start.15 = (bf16[1,64,2048]{2,1,0:T(8,128)(2,1)}, bf16[1,64,2048]{2,1,0:T(8,128)(2,1)}, u32[]{:S(2)}, u32[]{:S(2)}) collective-permute-start(bf16[1,64,2048]{2,1,0:T(8,128)(2,1)} %bitcast.35), channel_id=1, source_target_pairs={{0,4},{1,5},{2,6},{3,7},{4,0},{5,1},{6,2},{7,3},{8,12},{9,13},{10,... | collective-permute-start | bytes 786440 | tf_op jit(solution)/shard_map/ppermute | solution.py:41
  20.6 59.2 %collective-permute-start.35 = (bf16[2,2,1,64,704]{4,3,2,1,0:T(8,128)(2,1)}, bf16[2,2,1,64,704]{4,3,2,1,0:T(8,128)(2,1)}, u32[]{:S(2)}, u32[]{:S(2)}) collective-permute-start(bf16[2,2,1,64,704]{4,3,2,1,0:T(8,128)(2,1)} %copy.168), channel_id=1, source_target_pairs={{0,8},{8,0},{16,24},{24,16},{1,9},{9,1},{17,25},{25,17},{2,10},{10... | collective-permute-start | bytes 1081352 | tf_op jit(solution)/shard_map/ppermute | solution.py:41
  39.1 64.6 %collective-permute-start.44 = (bf16[1,128,2048]{1,2,0:T(8,128)(2,1)S(1)}, bf16[1,128,2048]{1,2,0:T(8,128)(2,1)}, u32[]{:S(2)}, u32[]{:S(2)}) collective-permute-start(bf16[1,128,2048]{1,2,0:T(8,128)(2,1)S(1)} %bitcast.427), channel_id=1, source_target_pairs={{0,16},{8,24},{16,0},{24,8},{1,17},{9,25},{17,1},{25,9},{2,18},{10... | collective-permute-start | bytes 1572872 | tf_op jit(solution)/shard_map/ppermute | solution.py:41
  95.0 111.3 %collective-permute-start.30 = (bf16[1,2,2,64,704]{4,2,1,0,3:T(2,128)(2,1)}, bf16[1,2,2,64,704]{4,2,1,0,3:T(2,128)(2,1)}, u32[]{:S(2)}, u32[]{:S(2)}) collective-permute-start(bf16[1,2,2,64,704]{4,2,1,0,3:T(2,128)(2,1)} %fusion.78), channel_id=1, source_target_pairs={{0,16},{8,24},{16,0},{24,8},{1,17},{9,25},{17,1},{25,9},{2,18},{10... | collective-permute-start | bytes 1081352 | tf_op jit(solution)/shard_map/ppermute | solution.py:41
  105.9 105.1 %collective-permute-start.24 = (bf16[1,2,2,64,704]{4,2,1,0,3:T(2,128)(2,1)}, bf16[1,2,2,64,704]{4,2,1,0,3:T(2,128)(2,1)}, u32[]{:S(2)}, u32[]{:S(2)}) collective-permute-start(bf16[1,2,2,64,704]{4,2,1,0,3:T(2,128)(2,1)} %fusion.80), channel_id=1, source_target_pairs={{0,16},{8,24},{16,0},{24,8},{1,17},{9,25},{17,1},{25,9},{2,18},{10... | collective-permute-start | bytes 1081352 | tf_op jit(solution)/shard_map/ppermute | solution.py:41
  119.7 130.2 %collective-permute-start.45 = (bf16[2,128,2048]{1,2,0:T(8,128)(2,1)}, bf16[2,128,2048]{1,2,0:T(8,128)(2,1)}, u32[]{:S(2)}, u32[]{:S(2)}) collective-permute-start(bf16[2,128,2048]{1,2,0:T(8,128)(2,1)} %pad_maximum_fusion.17), channel_id=1, source_target_pairs={{0,2},{1,3},{2,0},{3,1},{4,6},{5,7},{6,4},{7,5},{8,10},{9,11},{10,... | collective-permute-start | bytes 3145736 | tf_op jit(solution)/shard_map/ppermute | solution.py:41
  210.3 54.7 %collective-permute-start.31 = (bf16[2,1,2,64,704]{4,2,1,0,3:T(2,128)(2,1)}, bf16[2,1,2,64,704]{4,2,1,0,3:T(2,128)(2,1)}, u32[]{:S(2)}, u32[]{:S(2)}) collective-permute-start(bf16[2,1,2,64,704]{4,2,1,0,3:T(2,128)(2,1)} %fusion.90), channel_id=1, source_target_pairs={{0,2},{1,3},{2,0},{3,1},{4,6},{5,7},{6,4},{7,5},{8,10},{9,11},{10,... | collective-permute-start | bytes 1081352 | tf_op jit(solution)/shard_map/ppermute | solution.py:41
  216.2 55.9 %collective-permute-start.25 = (bf16[2,1,2,64,704]{4,2,1,0,3:T(2,128)(2,1)}, bf16[2,1,2,64,704]{4,2,1,0,3:T(2,128)(2,1)}, u32[]{:S(2)}, u32[]{:S(2)}) collective-permute-start(bf16[2,1,2,64,704]{4,2,1,0,3:T(2,128)(2,1)} %fusion.92), channel_id=1, source_target_pairs={{0,2},{1,3},{2,0},{3,1},{4,6},{5,7},{6,4},{7,5},{8,10},{9,11},{10,... | collective-permute-start | bytes 1081352 | tf_op jit(solution)/shard_map/ppermute | solution.py:41
  252.7 67.9 %collective-permute-start.46 = (bf16[4,128,2048]{1,2,0:T(8,128)(2,1)}, bf16[4,128,2048]{1,2,0:T(8,128)(2,1)}, u32[]{:S(2)}, u32[]{:S(2)}) collective-permute-start(bf16[4,128,2048]{1,2,0:T(8,128)(2,1)} %pad_maximum_fusion.8), channel_id=1, source_target_pairs={{0,8},{8,0},{16,24},{24,16},{1,9},{9,1},{17,25},{25,17},{2,10},{10... | collective-permute-start | bytes 6291464 | tf_op jit(solution)/shard_map/ppermute | solution.py:41
  255.5 79.9 %collective-permute-start.38 = (bf16[512,704]{0,1:T(8,128)(2,1)}, bf16[512,704]{0,1:T(8,128)(2,1)}, u32[]{:S(2)}, u32[]{:S(2)}) collective-permute-start(bf16[512,704]{0,1:T(8,128)(2,1)} %copy.172), channel_id=1, source_target_pairs={{0,1},{1,0},{2,3},{3,2},{4,5},{5,4},{6,7},{7,6},{8,9},{9,8},{10,11... | collective-permute-start | bytes 2162696 | tf_op jit(solution)/shard_map/ppermute | solution.py:41
  261.5 59.2 %collective-permute-start.39 = (bf16[512,704]{0,1:T(8,128)(2,1)}, bf16[512,704]{0,1:T(8,128)(2,1)}, u32[]{:S(2)}, u32[]{:S(2)}) collective-permute-start(bf16[512,704]{0,1:T(8,128)(2,1)} %copy.172), channel_id=1, source_target_pairs={{0,4},{1,5},{2,6},{3,7},{4,0},{5,1},{6,2},{7,3},{8,12},{9,13},{10,... | collective-permute-start | bytes 2162696 | tf_op jit(solution)/shard_map/ppermute | solution.py:41
  265.0 44.9 %collective-permute-start.21 = (bf16[2,128,2048]{1,2,0:T(8,128)(2,1)}, bf16[2,128,2048]{1,2,0:T(8,128)(2,1)S(1)}, u32[]{:S(2)}, u32[]{:S(2)}) collective-permute-start(bf16[2,128,2048]{1,2,0:T(8,128)(2,1)} %pad_maximum_fusion.16), channel_id=1, source_target_pairs={{0,2},{1,3},{2,0},{3,1},{4,6},{5,7},{6,4},{7,5},{8,10},{9,11},{10,... | collective-permute-start | bytes 3145736 | tf_op jit(solution)/shard_map/ppermute | solution.py:41
  272.1 68.3 %collective-permute-start.32 = (bf16[512,704]{0,1:T(8,128)(2,1)}, bf16[512,704]{0,1:T(8,128)(2,1)}, u32[]{:S(2)}, u32[]{:S(2)}) collective-permute-start(bf16[512,704]{0,1:T(8,128)(2,1)} %copy.166), channel_id=1, source_target_pairs={{0,4},{1,5},{2,6},{3,7},{4,0},{5,1},{6,2},{7,3},{8,12},{9,13},{10,... | collective-permute-start | bytes 2162696 | tf_op jit(solution)/shard_map/ppermute | solution.py:41
  311.6 49.5 %collective-permute-start.22 = (bf16[4,128,2048]{1,2,0:T(8,128)(2,1)}, bf16[4,128,2048]{1,2,0:T(8,128)(2,1)}, u32[]{:S(2)}, u32[]{:S(2)}) collective-permute-start(bf16[4,128,2048]{1,2,0:T(8,128)(2,1)} %pad_maximum_fusion.7), channel_id=1, source_target_pairs={{0,8},{8,0},{16,24},{24,16},{1,9},{9,1},{17,25},{25,17},{2,10},{10... | collective-permute-start | bytes 6291464 | tf_op jit(solution)/shard_map/ppermute | solution.py:41
  335.4 40.4 %collective-permute-start.33 = (bf16[512,704]{0,1:T(8,128)(2,1)}, bf16[512,704]{0,1:T(8,128)(2,1)}, u32[]{:S(2)}, u32[]{:S(2)}) collective-permute-start(bf16[512,704]{0,1:T(8,128)(2,1)} %copy.166), channel_id=1, source_target_pairs={{0,1},{1,0},{2,3},{3,2},{4,5},{5,4},{6,7},{7,6},{8,9},{9,8},{10,11... | collective-permute-start | bytes 2162696 | tf_op jit(solution)/shard_map/ppermute | solution.py:41
  340.4 38.6 %collective-permute-start.27 = (bf16[512,704]{0,1:T(8,128)(2,1)}, bf16[512,704]{0,1:T(8,128)(2,1)S(1)}, u32[]{:S(2)}, u32[]{:S(2)}) collective-permute-start(bf16[512,704]{0,1:T(8,128)(2,1)} %copy.160), channel_id=1, source_target_pairs={{0,1},{1,0},{2,3},{3,2},{4,5},{5,4},{6,7},{7,6},{8,9},{9,8},{10,11... | collective-permute-start | bytes 2162696 | tf_op jit(solution)/shard_map/ppermute | solution.py:41
  357.1 44.4 %collective-permute-start.28 = (bf16[512,704]{0,1:T(8,128)(2,1)S(1)}, bf16[512,704]{0,1:T(8,128)(2,1)}, u32[]{:S(2)}, u32[]{:S(2)}) collective-permute-start(bf16[512,704]{0,1:T(8,128)(2,1)S(1)} %collective-permute-done.26), channel_id=1, source_target_pairs={{0,1},{1,0},{2,3},{3,2},{4,5},{5,4},{6,7},{7,6},{8,9},{9,8},{10,11... | collective-permute-start | bytes 2162696 | tf_op jit(solution)/shard_map/ppermute | solution.py:41
  431.9 168.2 %collective-permute-start.47 = (bf16[4,128,2048]{1,2,0:T(8,128)(2,1)}, bf16[4,128,2048]{1,2,0:T(8,128)(2,1)}, u32[]{:S(2)}, u32[]{:S(2)}) collective-permute-start(bf16[4,128,2048]{1,2,0:T(8,128)(2,1)} %copy_bitcast_fusion), channel_id=1, source_target_pairs={{0,8},{8,0},{16,24},{24,16},{1,9},{9,1},{17,25},{25,17},{2,10},{10... | collective-permute-start | bytes 6291464 | tf_op jit(solution)/shard_map/ppermute | solution.py:41
  453.1 60.9 %collective-permute-start.65 = (bf16[512,704]{0,1:T(8,128)(2,1)S(1)}, bf16[512,704]{0,1:T(8,128)(2,1)S(1)}, u32[]{:S(2)}, u32[]{:S(2)}) collective-permute-start(bf16[512,704]{0,1:T(8,128)(2,1)S(1)} %copy-done.110), channel_id=1, source_target_pairs={{0,1},{1,0},{2,3},{3,2},{4,5},{5,4},{6,7},{7,6},{8,9},{9,8},{10,11... | collective-permute-start | bytes 2162696 | tf_op jit(solution)/shard_map/ppermute | solution.py:41
  454.5 55.1 %collective-permute-start.78 = (bf16[512,704]{0,1:T(8,128)(2,1)S(1)}, bf16[512,704]{0,1:T(8,128)(2,1)S(1)}, u32[]{:S(2)}, u32[]{:S(2)}) collective-permute-start(bf16[512,704]{0,1:T(8,128)(2,1)S(1)} %convolution_convert_fusion), channel_id=1, source_target_pairs={{0,1},{1,0},{2,3},{3,2},{4,5},{5,4},{6,7},{7,6},{8,9},{9,8},{10,11... | collective-permute-start | bytes 2162696 | tf_op jit(solution)/shard_map/ppermute | solution.py:41
  464.2 51.6 %collective-permute-start.67 = (bf16[512,704]{0,1:T(8,128)(2,1)S(1)}, bf16[512,704]{0,1:T(8,128)(2,1)S(1)}, u32[]{:S(2)}, u32[]{:S(2)}) collective-permute-start(bf16[512,704]{0,1:T(8,128)(2,1)S(1)} %add_convert_fusion.5), channel_id=1, source_target_pairs={{0,4},{1,5},{2,6},{3,7},{4,0},{5,1},{6,2},{7,3},{8,12},{9,13},{10,... | collective-permute-start | bytes 2162696 | tf_op jit(solution)/shard_map/ppermute | solution.py:41
  478.7 46.5 %collective-permute-start.71 = (bf16[512,704]{0,1:T(8,128)(2,1)}, bf16[512,704]{0,1:T(8,128)(2,1)}, u32[]{:S(2)}, u32[]{:S(2)}) collective-permute-start(bf16[512,704]{0,1:T(8,128)(2,1)} %convolution_convert_fusion.3), channel_id=1, source_target_pairs={{0,1},{1,0},{2,3},{3,2},{4,5},{5,4},{6,7},{7,6},{8,9},{9,8},{10,11... | collective-permute-start | bytes 2162696 | tf_op jit(solution)/shard_map/ppermute | solution.py:41
  509.6 48.6 %collective-permute-start.73 = (bf16[512,704]{0,1:T(8,128)(2,1)}, bf16[512,704]{0,1:T(8,128)(2,1)}, u32[]{:S(2)}, u32[]{:S(2)}) collective-permute-start(bf16[512,704]{0,1:T(8,128)(2,1)} %add_convert_fusion.3), channel_id=1, source_target_pairs={{0,4},{1,5},{2,6},{3,7},{4,0},{5,1},{6,2},{7,3},{8,12},{9,13},{10,... | collective-permute-start | bytes 2162696 | tf_op jit(solution)/shard_map/ppermute | solution.py:41
  514.0 46.6 %collective-permute-start.77 = (bf16[512,704]{0,1:T(8,128)(2,1)}, bf16[512,704]{0,1:T(8,128)(2,1)}, u32[]{:S(2)}, u32[]{:S(2)}) collective-permute-start(bf16[512,704]{0,1:T(8,128)(2,1)} %convolution_convert_fusion.1), channel_id=1, source_target_pairs={{0,1},{1,0},{2,3},{3,2},{4,5},{5,4},{6,7},{7,6},{8,9},{9,8},{10,11... | collective-permute-start | bytes 2162696 | tf_op jit(solution)/shard_map/ppermute | solution.py:41
  515.8 57.3 %collective-permute-start.79 = (bf16[512,704]{0,1:T(8,128)(2,1)}, bf16[512,704]{0,1:T(8,128)(2,1)}, u32[]{:S(2)}, u32[]{:S(2)}) collective-permute-start(bf16[512,704]{0,1:T(8,128)(2,1)} %add_convert_fusion.1), channel_id=1, source_target_pairs={{0,4},{1,5},{2,6},{3,7},{4,0},{5,1},{6,2},{7,3},{8,12},{9,13},{10,... | collective-permute-start | bytes 2162696 | tf_op jit(solution)/shard_map/ppermute | solution.py:41
  525.2 78.6 %collective-permute-start.41 = (bf16[4,128,2048]{1,2,0:T(8,128)(2,1)}, bf16[4,128,2048]{1,2,0:T(8,128)(2,1)}, u32[]{:S(2)}, u32[]{:S(2)}) collective-permute-start(bf16[4,128,2048]{1,2,0:T(8,128)(2,1)} %copy_bitcast_fusion.1), channel_id=1, source_target_pairs={{0,8},{8,0},{16,24},{24,16},{1,9},{9,1},{17,25},{25,17},{2,10},{10... | collective-permute-start | bytes 6291464 | tf_op jit(solution)/shard_map/ppermute | solution.py:41
  607.1 69.8 %collective-permute-start.42 = (bf16[2,128,2048]{1,2,0:T(8,128)(2,1)}, bf16[2,128,2048]{1,2,0:T(8,128)(2,1)}, u32[]{:S(2)}, u32[]{:S(2)}) collective-permute-start(bf16[2,128,2048]{1,2,0:T(8,128)(2,1)} %slice.503), channel_id=1, source_target_pairs={{0,2},{1,3},{2,0},{3,1},{4,6},{5,7},{6,4},{7,5},{8,10},{9,11},{10,... | collective-permute-start | bytes 3145736 | tf_op jit(solution)/shard_map/ppermute | solution.py:41
  691.7 40.3 %collective-permute-start.51 = (bf16[2,128,2048]{2,1,0:T(8,128)(2,1)}, bf16[2,128,2048]{2,1,0:T(8,128)(2,1)}, u32[]{:S(2)}, u32[]{:S(2)}) collective-permute-start(bf16[2,128,2048]{2,1,0:T(8,128)(2,1)} %pad_maximum_fusion.18), channel_id=1, source_target_pairs={{0,8},{8,0},{16,24},{24,16},{1,9},{9,1},{17,25},{25,17},{2,10},{10... | collective-permute-start | bytes 3145736 | tf_op jit(solution)/shard_map/ppermute | solution.py:41
  872.3 116.9 %collective-permute-start.61 = (bf16[1,2,64,640]{3,2,1,0:T(8,128)(2,1)S(1)}, bf16[1,2,64,640]{3,2,1,0:T(8,128)(2,1)S(1)}, u32[]{:S(2)}, u32[]{:S(2)}) collective-permute-start(bf16[1,2,64,640]{3,2,1,0:T(8,128)(2,1)S(1)} %fusion.107), channel_id=1, source_target_pairs={{0,16},{8,24},{16,0},{24,8},{1,17},{9,25},{17,1},{25,9},{2,18},{10... | collective-permute-start | bytes 491528 | tf_op jit(solution)/shard_map/ppermute | solution.py:41
  (170 other events, 2114.4 us)
Sparse Core Ops, SparseCore 0:
  852.8 134.3 reduce-scatter.3

commit v2 on v1

v2 whole, which is shorter than its diff:
```python
import functools
import math

import jax
import jax.numpy as jnp
from jax import lax
from jax.experimental import pallas as pl
from jax.experimental.pallas import tpu as pltpu
from jax.sharding import PartitionSpec as P

HEADS = 32
KV_HEADS = 4
HEAD_DIM = 64
GROUPS = HEADS // KV_HEADS
HEAD_COLS = GROUPS * HEAD_DIM
FACTOR = 1.0 / math.sqrt(HEAD_DIM)

norm_eps = 1e-05
rope_base = 10000.0

BF = jnp.bfloat16
F32 = jnp.float32
MIB = 1 << 20


def dot(left, right):
    return jnp.dot(left, right, preferred_element_type=F32)


def dot_nt(left, right):
    return lax.dot_general(left, right, (((1,), (1,)), ((), ())), preferred_element_type=F32)


def dot_tn(left, right):
    return lax.dot_general(left, right, (((0,), (0,)), ((), ())), preferred_element_type=F32)


def shape_of(shape, kind):
    return jax.ShapeDtypeStruct(shape, kind)


def run(kernel, ins, outs, specs=None, out_specs=None, grid=None, vmem=32, scratch=(), flops=0):
    whole = pl.BlockSpec(memory_space=pltpu.VMEM)
    moved = sum(math.prod(a.shape) * a.dtype.itemsize for a in list(ins) + list(outs))
    extra = {} if grid is None else {"grid": grid}
    name = kernel.func.__name__ if isinstance(kernel, functools.partial) else kernel.__name__
    return pl.pallas_call(
        kernel,
        name=name,
        out_shape=list(outs),
        in_specs=specs or [whole] * len(ins),
        out_specs=out_specs or [whole] * len(outs),
        scratch_shapes=list(scratch),
        compiler_params=pltpu.CompilerParams(vmem_limit_bytes=vmem * MIB),
        cost_estimate=pl.CostEstimate(flops=0, bytes_accessed=0, transcendentals=0),
        **extra,
    )(*ins)


SMEM = pl.BlockSpec(memory_space=pltpu.SMEM)


class Bit:
    def __init__(self, axis, bit, size):
        self.axis, self.bit = axis, bit
        self.pairs = [(i, i ^ (1 << bit)) for i in range(size)]

    def mine(self):
        return (lax.axis_index(self.axis) >> self.bit) & 1

    def swap(self, value, what="rows"):
        with jax.named_scope(f"{what}_{self.axis}{self.bit}"):
            return lax.ppermute(value, self.axis, self.pairs)


def after(value, *others):
    return lax.optimization_barrier((value,) + others)[0]


class Order:
    def __init__(self, names, gathered, rest, depth):
        self.names, self.gathered, self.rest, self.depth = names, gathered, rest, depth
        self.rel = gathered + rest
        self.fast = depth == 64 and len(names) == 5 and names[-1] in gathered and rest[-1] is not names[-1]
        self.mine = jnp.stack(
            [b.mine() if b in gathered else jnp.zeros((), jnp.int32) for b in names]
        ).astype(jnp.int32)

    def to_tiles(self, read, write, mine):
        lanes = lax.broadcasted_iota(jnp.int32, (1, 128), 1)
        head = self.rel[:-1]
        last = self.rel[-1]
        for q in range(16):
            value = {b: (q >> (3 - i)) & 1 for i, b in enumerate(head)}

            def source(low):
                index = 0
                for i, b in enumerate(self.names[:-1]):
                    v = low if b is last else value[b]
                    if b in self.gathered:
                        v = v ^ mine[i]
                    index = index * 2 + v
                return read(index)

            a, b = source(0), source(1)
            side = value[self.names[-1]] ^ mine[4]
            first = jnp.where(lanes < 64, a, pltpu.roll(b, 64, 1))
            second = jnp.where(lanes < 64, pltpu.roll(a, 64, 1), b)
            write(q, jnp.where(side == 0, first, second))

    def from_tiles(self, read, write, mine):
        lanes = lax.broadcasted_iota(jnp.int32, (1, 128), 1)
        for t in range(16):
            value = {b: (t >> (3 - i)) & 1 for i, b in enumerate(self.names[:-1])}

            def source(y):
                index = 0
                for b in self.rel[:-1]:
                    v = y if b is self.names[-1] else value[b]
                    if b in self.gathered:
                        v = v ^ mine[self.names.index(b)]
                    index = index * 2 + v
                return read(index)

            low, high = source(0), source(1)
            if value[self.rel[-1]] == 0:
                write(t, jnp.where(lanes < 64, low, pltpu.roll(high, 64, 1)))
            else:
                write(t, jnp.where(lanes < 64, pltpu.roll(low, 64, 1), high))

    def to_rel(self, array):
        count, width = array.shape
        out = array.reshape((count,) + (2,) * len(self.names) + (self.depth,))
        for b in self.gathered:
            k = self.names.index(b) + 1
            out = jnp.where(b.mine() == 1, jnp.flip(out, k), out)
        axes = [self.names.index(b) + 1 for b in self.rel]
        return out.transpose([0] + axes + [len(self.names) + 1]).reshape(count, width)

    def from_rel(self, array):
        count, width = array.shape
        out = array.reshape((count,) + (2,) * len(self.names) + (self.depth,))
        axes = [self.rel.index(b) + 1 for b in self.names]
        out = out.transpose([0] + axes + [len(self.names) + 1])
        for b in self.gathered:
            k = self.names.index(b) + 1
            out = jnp.where(b.mine() == 1, jnp.flip(out, k), out)
        return out.reshape(count, width)


def tile(index):
    start = index * 128
    return pl.ds(start if isinstance(start, int) else pl.multiple_of(start, 128), 128)


def row_specs(count, rows, width, steps):
    return [pl.BlockSpec((rows // steps, width), lambda i: (i, 0))] * count


def inverse_of(x):
    return lax.rsqrt(jnp.mean(x * x, -1, keepdims=True) + norm_eps)


def norm_kernel(order, mine_ref, x_ref, gain_ref, out_ref):
    mine = [mine_ref[i] for i in range(5)]
    inverse = inverse_of(x_ref[...].astype(F32))

    def write(q, value):
        out_ref[:, tile(q)] = value.astype(BF)

    def read(i):
        return x_ref[:, tile(i)].astype(F32) * inverse * gain_ref[:, tile(i)]

    order.to_tiles(read, write, mine)


def norm_to(order, x, gain):
    if not order.fast:
        x = x.astype(F32)
        return order.to_rel((x * inverse_of(x) * gain).astype(BF))
    rows, width = x.shape
    specs = row_specs(2, rows, width, 2)
    return run(
        functools.partial(norm_kernel, order),
        [order.mine, x, gain],
        [shape_of((rows, width), BF)],
        [SMEM, specs[0], pl.BlockSpec((1, width), lambda i: (0, 0))],
        [specs[1]],
        (2,),
    )[0]


def order_kernel(order, mine_ref, x_ref, out_ref):
    mine = [mine_ref[i] for i in range(5)]

    def write(q, value):
        out_ref[:, tile(q)] = value.astype(out_ref.dtype)

    order.to_tiles(lambda i: x_ref[:, tile(i)].astype(F32), write, mine)


def order_to(order, x):
    if not order.fast:
        return order.to_rel(x)
    rows, width = x.shape
    specs = row_specs(2, rows, width, 2)
    return run(
        functools.partial(order_kernel, order),
        [order.mine, x],
        [shape_of((rows, width), x.dtype)],
        [SMEM, specs[0]],
        [specs[1]],
        (2,),
    )[0]


def middle_kernel(order, mine_ref, x_ref, a_ref, b_ref, mid_ref, out_ref):
    mine = [mine_ref[i] for i in range(5)]
    mid = x_ref[...].astype(F32) + a_ref[...].astype(F32) + b_ref[...].astype(F32)
    mid_ref[...] = mid
    inverse = inverse_of(mid)

    def write(q, value):
        out_ref[:, tile(q)] = value.astype(BF)

    order.to_tiles(lambda i: mid_ref[:, tile(i)] * inverse, write, mine)


def middle_to(order, x, a, b):
    rows, width = x.shape
    if not order.fast:
        mid = x.astype(F32) + a.astype(F32) + b.astype(F32)
        return mid, order.to_rel((mid * inverse_of(mid)).astype(BF))
    specs = row_specs(5, rows, width, 2)
    return run(
        functools.partial(middle_kernel, order),
        [order.mine, x, a, b],
        [shape_of((rows, width), F32), shape_of((rows, width), BF)],
        [SMEM] + specs[:3],
        specs[:2],
        (2,),
    )


def back_kernel(order, scaled, mine_ref, x_ref, g_ref, a_ref, b_ref, *outs):
    mine = [mine_ref[i] for i in range(5)]
    scratch = outs[-1]
    if scaled:
        gain_ref, outs = outs[0], outs[1:]
    inverse = inverse_of(x_ref[...].astype(F32))

    def write(t, value):
        scratch[:, tile(t)] = value * gain_ref[:, tile(t)] if scaled else value

    def read(i):
        return a_ref[:, tile(i)].astype(F32) + b_ref[:, tile(i)].astype(F32)

    order.from_tiles(read, write, mine)
    normed = x_ref[...].astype(F32) * inverse
    scaled = scratch[...]
    shared = jnp.mean(scaled * normed, -1, keepdims=True)
    total = g_ref[...].astype(F32) + inverse * (scaled - normed * shared)
    outs[0][...] = total
    if len(outs) == 3:
        outs[1][...] = total.astype(BF)


def norm_back(order, x, g, a, b, gain=None, low=False):
    rows, width = x.shape
    scaled = gain is not None
    if not order.fast:
        x = x.astype(F32)
        inverse = inverse_of(x)
        normed = x * inverse
        grad = a.astype(F32) + b.astype(F32)
        grad = order.from_rel(grad)
        grad = grad * gain if scaled else grad
        shared = jnp.mean(grad * normed, -1, keepdims=True)
        total = g.astype(F32) + inverse * (grad - normed * shared)
        return (total, total.astype(BF)) if low else (total,)
    specs = row_specs(6, rows, width, 2)
    outs = [shape_of((rows, width), F32)] + ([shape_of((rows, width), BF)] if low else [])
    return run(
        functools.partial(back_kernel, order, scaled),
        [order.mine, x, g, a, b] + ([gain] if scaled else []),
        outs,
        [SMEM] + specs[:4] + [pl.BlockSpec((1, width), lambda i: (0, 0))] * scaled,
        specs[: len(outs)],
        (2,),
        scratch=[pltpu.VMEM((rows // 2, width), F32)],
    )


def result_kernel(order, mine_ref, mid_ref, a_ref, b_ref, out_ref):
    mine = [mine_ref[i] for i in range(5)]

    def write(t, value):
        out_ref[:, tile(t)] = (mid_ref[:, tile(t)] + value).astype(BF)

    order.from_tiles(
        lambda i: a_ref[:, tile(i)].astype(F32) + b_ref[:, tile(i)].astype(F32), write, mine
    )


def result_of(order, mid, a, b):
    rows, width = mid.shape
    if not order.fast:
        return (mid + order.from_rel(a.astype(F32) + b.astype(F32))).astype(BF)
    specs = row_specs(4, rows, width, 2)
    return run(
        functools.partial(result_kernel, order),
        [order.mine, mid, a, b],
        [shape_of((rows, width), BF)],
        [SMEM] + specs[:3],
        specs[:1],
        (2,),
    )[0]


def pack_kernel(count, kinds, *refs):
    out_ref = refs[-1]
    cols = out_ref.shape[-1]
    depth = refs[0].shape[0]
    for m in range(kinds):
        value = refs[m][...].astype(F32)
        if len(refs) > kinds + 1:
            value = value * refs[kinds][...]
        for t in range(count):
            out_ref[t, m * depth : (m + 1) * depth] = value[:, t * cols : (t + 1) * cols].astype(BF)


def pack(weights, gain, count):
    depth, width = weights[0].shape
    return run(
        functools.partial(pack_kernel, count, len(weights)),
        weights + ([] if gain is None else [gain]),
        [shape_of((count, len(weights) * depth, width // count), BF)],
    )[0]


def unpack_kernel(count, kinds, scaled, *refs):
    p_ref = refs[0]
    cols = p_ref.shape[-1]
    depth = p_ref.shape[1] // kinds
    outs = refs[-kinds - 1 : -1] if scaled else refs[-kinds:]
    total = jnp.zeros((depth, 1), F32)
    for m in range(kinds):
        for t in range(count):
            part = p_ref[t, m * depth : (m + 1) * depth].astype(F32)
            lanes = slice(t * cols, (t + 1) * cols)
            if scaled:
                total = total + jnp.sum(part * refs[1 + m][:, lanes].astype(F32), -1, keepdims=True)
                part = part * refs[1 + kinds][...]
            outs[m][:, lanes] = part
    if scaled:
        refs[-1][...] = total


def unpack(parts, weights, gain):
    count, depth, cols = parts.shape
    if gain is None:
        outs = [shape_of((depth, count * cols), F32)]
        return run(functools.partial(unpack_kernel, count, 1, False), [parts], outs)
    kinds = len(weights)
    outs = [shape_of((depth // kinds, count * cols), F32)] * kinds + [shape_of((depth // kinds, 1), F32)]
    return run(functools.partial(unpack_kernel, count, kinds, True), [parts] + weights + [gain], outs)


def pack_qkv_kernel(count, q_ref, k_ref, v_ref, out_ref):
    for t in range(count):
        out_ref[t, :, :HEAD_COLS] = q_ref[:, t * HEAD_COLS : (t + 1) * HEAD_COLS]
        lanes = slice(t * HEAD_DIM, (t + 1) * HEAD_DIM)
        both = jnp.concatenate([k_ref[:, lanes].astype(F32), v_ref[:, lanes].astype(F32)], -1)
        out_ref[t, :, HEAD_COLS:] = both.astype(BF)


def unpack_qkv_kernel(count, q_ref, k_ref, v_ref, g_ref, p_ref, qo_ref, ko_ref, vo_ref, sum_ref):
    gain = g_ref[...]
    total = jnp.zeros_like(gain)
    for t in range(count):
        part = p_ref[t].astype(F32)
        lanes = slice(t * HEAD_COLS, (t + 1) * HEAD_COLS)
        thin = slice(t * HEAD_DIM, (t + 1) * HEAD_DIM)
        gq = part[:, :HEAD_COLS]
        gk = part[:, HEAD_COLS : HEAD_COLS + HEAD_DIM]
        gv = part[:, HEAD_COLS + HEAD_DIM :]
        total = total + jnp.sum(gq * q_ref[:, lanes].astype(F32), -1, keepdims=True)
        total = total + jnp.sum(gk * k_ref[:, thin].astype(F32), -1, keepdims=True)
        total = total + jnp.sum(gv * v_ref[:, thin].astype(F32), -1, keepdims=True)
        qo_ref[:, lanes] = gq
        ko_ref[:, thin] = gk
        vo_ref[:, thin] = gv
    sum_ref[...] = total / gain


def swap_halves(values):
    width = values.shape[-1]
    lanes = lax.broadcasted_iota(jnp.int32, (1, width), 1)
    return jnp.where(
        lanes % HEAD_DIM < HEAD_DIM // 2,
        pltpu.roll(values, width - HEAD_DIM // 2, 1),
        pltpu.roll(values, HEAD_DIM // 2, 1),
    )


def project_kernel(repeat, count, *refs):
    a_ref, cos_ref, sin_ref = refs[:3]
    w_refs, q_ref, kv_ref = refs[3 : 3 + count], refs[-2], refs[-1]
    piece = w_refs[0].shape[0]
    raw = None
    for k in range(count):
        term = dot(a_ref[:, k * piece : (k + 1) * piece], w_refs[k][...])
        raw = term if raw is None else raw + term
    cosine = jnp.concatenate([cos_ref[...]] * repeat, 0)
    sine = jnp.concatenate([sin_ref[...]] * repeat, 0)
    out = (raw * cosine + swap_halves(raw) * sine).astype(BF)
    q_ref[...] = out[:, :HEAD_COLS]
    kv_ref[...] = out[:, HEAD_COLS:]


def project(a1, cosine, sine, parts):
    rows, width = a1.shape
    seq_dev, cols = cosine.shape
    block = min(2 * seq_dev, rows)
    fixed = lambda i: (0, 0)
    moving = lambda i: (i, 0)
    return run(
        functools.partial(project_kernel, block // seq_dev, len(parts)),
        [a1, cosine, sine] + parts,
        [shape_of((rows, HEAD_COLS), BF), shape_of((rows, 2 * HEAD_DIM), BF)],
        [pl.BlockSpec((block, width), moving)]
        + [pl.BlockSpec((seq_dev, cols), fixed)] * 2
        + [pl.BlockSpec(p.shape, fixed) for p in parts],
        [pl.BlockSpec((block, HEAD_COLS), moving), pl.BlockSpec((block, 2 * HEAD_DIM), moving)],
        (rows // block,),
        flops=2 * rows * width * cols,
    )


def stack_heads(values):
    return jnp.concatenate(
        [values[:, j * HEAD_DIM : (j + 1) * HEAD_DIM] for j in range(GROUPS)], 0
    )


def soft_weights(queries, keys, key_ref, seq_dev):
    scores = dot_nt(queries, keys) * FACTOR
    place = lax.broadcasted_iota(jnp.int32, (queries.shape[0], 1), 0) % seq_dev
    return jnp.where(place >= key_ref[...], jnp.exp(scores), 0.0)


def attend_kernel(q_ref, kv_ref, key_ref, o_ref):
    seq_dev = q_ref.shape[0]
    both = kv_ref[...].reshape(-1, 2 * HEAD_DIM)
    keys, values = both[:, :HEAD_DIM], both[:, HEAD_DIM:]
    weights = soft_weights(stack_heads(q_ref[...]), keys, key_ref, seq_dev)
    totals = jnp.sum(weights, -1, keepdims=True)
    attended = dot(weights.astype(BF), values) / totals
    for j in range(GROUPS):
        rows = attended[j * seq_dev : (j + 1) * seq_dev]
        o_ref[:, j * HEAD_DIM : (j + 1) * HEAD_DIM] = rows.astype(BF)


def attend(queries, kv, key_places, seq_dev):
    rows = queries.shape[0]
    count, seqs = kv.shape[:2]
    return run(
        attend_kernel,
        [queries, kv, key_places],
        [shape_of((rows, HEAD_COLS), BF)],
        [
            pl.BlockSpec((seq_dev, HEAD_COLS), lambda s: (s, 0)),
            pl.BlockSpec((count, 1, seq_dev, 2 * HEAD_DIM), lambda s: (0, s, 0, 0)),
            pl.BlockSpec((1, count * seq_dev), lambda s: (0, 0)),
        ],
        [pl.BlockSpec((seq_dev, HEAD_COLS), lambda s: (s, 0))],
        (seqs,),
        flops=4 * rows * GROUPS * HEAD_DIM * count * seq_dev,
    )[0]


def attend_back_kernel(q_ref, kv_ref, key_ref, do_ref, cos_ref, sin_ref, dq_ref, dkv_ref, mid_ref):
    seq_dev = q_ref.shape[0]
    both = kv_ref[...].reshape(-1, 2 * HEAD_DIM)
    keys, values = both[:, :HEAD_DIM], both[:, HEAD_DIM:]
    queries = stack_heads(q_ref[...])
    weights = soft_weights(queries, keys, key_ref, seq_dev)
    totals = jnp.sum(weights, -1, keepdims=True)
    low = weights.astype(BF)
    attended = dot(low, values) / totals
    grads = stack_heads(do_ref[...])
    deltas = jnp.sum(grads * attended, -1, keepdims=True) / totals
    mixed = (grads / totals).astype(BF)
    scores = (weights * (dot_nt(mixed, values) - deltas)).astype(BF)
    turned = dot(scores, keys) * FACTOR
    for j in range(GROUPS):
        mid_ref[:, j * HEAD_DIM : (j + 1) * HEAD_DIM] = turned[j * seq_dev : (j + 1) * seq_dev]
    whole = mid_ref[...]
    dq_ref[...] = (whole * cos_ref[...] - swap_halves(whole) * sin_ref[...]).astype(BF)
    grad_keys = dot_tn(scores, queries) * FACTOR
    grad_values = dot_tn(low, mixed)
    joined = jnp.concatenate([grad_keys, grad_values], -1)
    dkv_ref[...] = joined.astype(BF).reshape(dkv_ref.shape)


def attend_back(queries, kv, key_places, grads, cosine, sine, seq_dev):
    rows = queries.shape[0]
    count, seqs = kv.shape[:2]
    own = pl.BlockSpec((seq_dev, HEAD_COLS), lambda s: (s, 0))
    table = pl.BlockSpec((seq_dev, HEAD_COLS), lambda s: (0, 0))
    blocks = pl.BlockSpec((count, 1, seq_dev, 2 * HEAD_DIM), lambda s: (0, s, 0, 0))
    return run(
        attend_back_kernel,
        [queries, kv, key_places, grads, cosine, sine],
        [shape_of((rows, HEAD_COLS), BF), shape_of(kv.shape, BF)],
        [own, blocks, pl.BlockSpec((1, count * seq_dev), lambda s: (0, 0)), own, table, table],
        [own, blocks],
        (seqs,),
        scratch=[pltpu.VMEM((seq_dev, HEAD_COLS), F32)],
        flops=14 * rows * GROUPS * HEAD_DIM * count * seq_dev,
    )


def turn_back_kernel(repeat, a_ref, b_ref, cos_ref, sin_ref, out_ref):
    total = a_ref[...].astype(F32) + b_ref[...].astype(F32)
    cosine = jnp.concatenate([cos_ref[...]] * repeat, 0)
    sine = jnp.concatenate([sin_ref[...]] * repeat, 0)
    out_ref[...] = (total * cosine - swap_halves(total) * sine).astype(BF)


def wide_kernel(product, left_ref, *refs):
    rights, out_ref = refs[:-1], refs[-1]
    cols = out_ref.shape[1] // len(rights)
    for k, right in enumerate(rights):
        out_ref[:, k * cols : (k + 1) * cols] = product(left_ref[...], right[...]).astype(BF)


def wide(product, left, rights, width, block):
    rows, depth = left.shape
    return run(
        functools.partial(wide_kernel, product),
        [left] + rights,
        [shape_of((rows, width), BF)],
        [pl.BlockSpec((block, depth), lambda i: (i, 0))]
        + [pl.BlockSpec(r.shape, lambda i: (0, 0)) for r in rights],
        [pl.BlockSpec((block, width), lambda i: (i, 0))],
        (rows // block,),
        vmem=48,
        flops=2 * rows * depth * width,
    )[0]


def gate_kernel(pieces, a_ref, *refs):
    both = refs[:pieces]
    hid_ref, one_ref, two_ref = refs[pieces:]
    units, cols = hid_ref.shape[1], both[0].shape[1]
    gate = up = None
    for k in range(pieces):
        part = a_ref[:, k * cols : (k + 1) * cols]
        g, u = dot_nt(part, both[k][:units]), dot_nt(part, both[k][units:])
        gate = g if gate is None else gate + g
        up = u if up is None else up + u
    sigmoid = jax.nn.sigmoid(gate)
    active = gate * sigmoid
    hid_ref[...] = (active * up).astype(BF)
    one_ref[...] = up * sigmoid * (1.0 + gate * (1.0 - sigmoid))
    two_ref[...] = active


def gate_up(a2, both, block):
    rows, width = a2.shape
    cols = both[0].shape[0] // 2
    moving = lambda i: (i, 0)
    out = pl.BlockSpec((block, cols), moving)
    return run(
        functools.partial(gate_kernel, len(both)),
        [a2] + both,
        [shape_of((rows, cols), BF), shape_of((rows, cols), F32), shape_of((rows, cols), F32)],
        [pl.BlockSpec((block, width), moving)]
        + [pl.BlockSpec(w.shape, lambda i: (0, 0)) for w in both],
        [out, out, out],
        (rows // block,),
        vmem=48,
        flops=4 * rows * width * cols,
    )


def hidden_kernel(pieces, g_ref, one_ref, two_ref, *refs):
    downs, both = refs[:pieces], refs[pieces : 2 * pieces]
    dboth_ref, out_ref = refs[2 * pieces :]
    units, cols = downs[0].shape
    total = None
    for k in range(pieces):
        term = dot_nt(g_ref[:, k * cols : (k + 1) * cols], downs[k][...])
        total = term if total is None else total + term
    dgate = (total * one_ref[...]).astype(BF)
    dup = (total * two_ref[...]).astype(BF)
    dboth_ref[:, :units] = dgate
    dboth_ref[:, units:] = dup
    for k in range(pieces):
        part = dot(dgate, both[k][:units]) + dot(dup, both[k][units:])
        out_ref[:, k * cols : (k + 1) * cols] = part.astype(BF)


def hidden_back(gb, one, two, downs, both, block):
    rows, width = gb.shape
    cols = downs[0].shape[0]
    moving = lambda i: (i, 0)
    thin = pl.BlockSpec((block, cols), moving)
    full = pl.BlockSpec((block, width), moving)
    return run(
        functools.partial(hidden_kernel, len(downs)),
        [gb, one, two] + downs + both,
        [shape_of((rows, 2 * cols), BF), shape_of((rows, width), BF)],
        [full, thin, thin] + [pl.BlockSpec(w.shape, lambda i: (0, 0)) for w in downs + both],
        [pl.BlockSpec((block, 2 * cols), moving), full],
        (rows // block,),
        vmem=56,
        flops=6 * rows * width * cols,
    )


def gather_rows(value, bits, what):
    acc = value
    for bit in bits:
        acc = jnp.concatenate([acc, bit.swap(acc, what)], 0)
    return acc


def reduce_rows(acc, bits, what):
    for bit in list(reversed(bits))[:-1]:
        half = acc.shape[0] // 2
        got = bit.swap(acc[half:], what)
        acc = (acc[:half].astype(F32) + got.astype(F32)).astype(BF)
    half = acc.shape[0] // 2
    return acc[:half], bits[0].swap(acc[half:], what)


def gather_team(value, bit_x, near, bit_core, what):
    half = value.shape[0] // 2
    by_x, by_near = bit_x.swap(value, what), near.swap(value, what)
    diagonal = [bit_x.swap(by_near[:half], what), near.swap(by_x[half:], what)]
    four = jnp.concatenate([value, by_x, by_near] + diagonal, 0)
    return jnp.concatenate([four, bit_core.swap(four, what)], 0)


def add_low(a, b):
    return (a.astype(F32) + b.astype(F32)).astype(BF)


def reduce_team(acc, bit_x, near, bit_core, what):
    half = acc.shape[0] // 2
    return reduce_four(acc[:half], bit_core.swap(acc[half:], what), bit_x, near, what)


def reduce_four(acc, got, bit_x, near, what):
    half = acc.shape[0]
    acc = add_low(acc, got)
    rows = half // 4
    own, by_x, by_near = acc[:rows], acc[rows : 2 * rows], acc[2 * rows : 3 * rows]
    first, second = acc[3 * rows : 3 * rows + rows // 2], acc[3 * rows + rows // 2 :]
    got_near = bit_x.swap(first, what)
    got_x = near.swap(second, what)
    by_near = jnp.concatenate([add_low(by_near[: rows // 2], got_near), by_near[rows // 2 :]], 0)
    by_x = jnp.concatenate([by_x[: rows // 2], add_low(by_x[rows // 2 :], got_x)], 0)
    return add_low(own, bit_x.swap(by_x, what)), near.swap(by_near, what)


def absolute(blocks, index, bits):
    def one(j):
        other = index ^ j
        slot = sum(((other >> b.bit) & 1) << i for i, b in enumerate(bits))
        return lax.dynamic_index_in_dim(blocks, slot, 0, False)

    return jnp.stack([one(j) for j in range(blocks.shape[0])])


def relative(blocks, index, bits):
    def one(r):
        code = sum(((r >> i) & 1) << b.bit for i, b in enumerate(bits))
        return lax.dynamic_index_in_dim(blocks, index ^ code, 0, False)

    return jnp.stack([one(r) for r in range(blocks.shape[0])])


def shards(
    dp,
    ctx,
    tokens,
    cotangent,
    attn_gain,
    query_weight,
    key_weight,
    value_weight,
    output_weight,
    mlp_gain,
    gate_weight,
    up_weight,
    down_weight,
):
    seqs, seq_dev, width = tokens.shape
    rows = seqs * seq_dev
    depth = query_weight.shape[0]
    c_index = lax.axis_index("ctx")

    bit_x, bit_core = Bit("dp", 1, dp), Bit("dp", 0, dp)
    ctx_bits = [Bit("ctx", b, ctx) for b in reversed(range(ctx.bit_length() - 1))]
    near = ctx_bits[-2]
    far = [b for b in ctx_bits if b is not near]
    dp_bits = [bit_x, bit_core]
    names = dp_bits + ctx_bits
    attn_order = Order(names, list(reversed(ctx_bits)), dp_bits, depth)
    mlp_order = Order(names, far, dp_bits + [near], depth)
    x = tokens.reshape(rows, width)
    cot = cotangent.reshape(rows, width)
    gain_one = attn_gain.astype(F32)[:, None]
    gain_two = mlp_gain.astype(F32)[:, None]

    team_groups = []
    for c in range(ctx):
        if not (c >> near.bit) & 1:
            team_groups.append([d * ctx + (c | (n << near.bit)) for d in range(dp) for n in range(2)])
    team = 2 * dp

    def mlp_trade(parts):
        return lax.all_to_all(
            parts, ("dp", "ctx"), 0, 0, axis_index_groups=team_groups, tiled=True
        )

    def mlp_slices(weights, gain):
        kinds = len(weights)
        parts = mlp_trade(pack(weights, gain, team)).reshape(team, kinds, depth, -1)
        return parts.transpose(1, 3, 0, 2).reshape(-1, team * depth)

    def mlp_rows(sums, kinds):
        parts = sums.reshape(kinds, -1, team, depth).transpose(2, 0, 3, 1)
        return mlp_trade(parts.reshape(team, kinds * depth, -1))

    digits = [sum(((k >> i) & 1) << (len(far) - 1 - i) for i in range(len(far))) for k in range(1 << len(far))]

    qkv_cols = HEAD_COLS + 2 * HEAD_DIM
    own = run(
        functools.partial(pack_qkv_kernel, dp),
        [query_weight, key_weight, value_weight],
        [shape_of((dp, depth, qkv_cols), BF)],
    )[0]
    own = lax.all_to_all(own, "dp", 0, 0, tiled=True).reshape(dp * depth, qkv_cols)
    both_own = mlp_slices([after(gate_weight, own), up_weight], gain_two)
    gain_all = jnp.broadcast_to(after(attn_gain, both_own)[None], (dp * ctx, depth))
    gain_all = lax.all_to_all(gain_all, ("dp", "ctx"), 0, 0, tiled=True)
    gain_all = gain_all.reshape(1, width).astype(F32)
    down_own = mlp_slices([after(down_weight.T, gain_all)], None)
    half = own
    for bit in ctx_bits[:-1]:
        half = jnp.concatenate([half, bit.swap(half, "qkv")], 0)
    qkv = [half, ctx_bits[-1].swap(half, "qkv")]
    out_bits = ctx_bits[:-2] + [ctx_bits[-1], near]
    out_rel = output_weight
    for i, bit in enumerate(out_bits):
        if bit is near:
            out_rel = after(out_rel, down_own)
        out_rel = jnp.concatenate([out_rel, bit.swap(out_rel, "out")], 0)
    out_full = absolute(out_rel.reshape(ctx, depth, width), c_index, out_bits)
    out_full = out_full.reshape(ctx * depth, width)

    def mlp_parts(own, marks, what):
        parts = [own]
        for i, bit in enumerate(far):
            sent = []
            for k, p in enumerate(parts):
                mark = marks.get((min(i, 1), min(k, 1)))
                sent.append(p if mark is None else after(p, mark))
            parts = parts + [bit.swap(p, what) for p in sent]
        return parts

    both = mlp_parts(both_own, {}, "both")
    downs = mlp_parts(down_own, {(0, 0): both[1]}, "down")
    pieces = len(both)
    piece = width // pieces

    def by_digit(parts):
        return [parts[digits.index(k)] for k in range(pieces)]

    places = jnp.arange(seq_dev, dtype=jnp.int32)
    half_dim = HEAD_DIM // 2
    freqs = rope_base ** (-(jnp.arange(half_dim, dtype=F32) * 2.0) / HEAD_DIM)
    angles = (c_index * seq_dev + places).astype(F32)[:, None] * freqs[None, :]
    cosine, sine = jnp.cos(angles), jnp.sin(angles)
    cosine = jnp.concatenate([cosine, cosine] * (GROUPS + 1) + [jnp.ones((seq_dev, HEAD_DIM), F32)], -1)
    sine = jnp.concatenate([-sine, sine] * (GROUPS + 1) + [jnp.zeros((seq_dev, HEAD_DIM), F32)], -1)
    rel = jnp.arange(ctx, dtype=jnp.int32)
    others = sum(((rel >> i) & 1) << b.bit for i, b in enumerate(ctx_bits)) ^ c_index
    key_places = (((others - c_index) * seq_dev)[:, None] + places[None, :]).reshape(1, -1)

    a1 = gather_rows(norm_to(attn_order, x, gain_all), dp_bits, "a1")
    queries, kv_own = project(after(a1, down_own), cosine, sine, qkv)
    all_seqs = dp * seqs
    kv = kv_own
    for bit in ctx_bits:
        kv = jnp.concatenate([kv, bit.swap(kv, "kv")], 0)
    gb = order_to(mlp_order, after(cot, kv))
    gb = gather_team(gb, bit_x, near, bit_core, "gb")
    kv = kv.reshape(ctx, all_seqs, seq_dev, 2 * HEAD_DIM)
    heads = attend(queries, kv, key_places, seq_dev)
    branch = dot(after(heads, both[1]), out_full).astype(BF)
    branch = reduce_rows(branch, dp_bits, "branch")
    middle, a2 = middle_to(mlp_order, after(x, both[2]), *branch)

    a2 = gather_team(a2, bit_x, near, bit_core, "a2")
    block = min(256, a2.shape[0])
    both, downs = by_digit(both), by_digit(downs)
    hidden, one, two = gate_up(a2, both, block)
    dboth, da2 = hidden_back(gb, one, two, downs, both, block)
    half = da2.shape[0] // 2
    da2_got = bit_core.swap(da2[half:], "da2")
    da2_two = reduce_four(da2[:half], da2_got, bit_x, near, "da2")
    grad_middle, db = norm_back(mlp_order, middle, cot, *da2_two, low=True)
    grad_branch = gather_rows(db, dp_bits, "db")
    down_out = wide(dot, after(hidden, grad_branch), downs, width, block)
    result = reduce_team(down_out, bit_x, near, bit_core, "result")
    result = result_of(mlp_order, middle, *result)

    grad_heads = dot_nt(grad_branch, out_full)
    dq, dkv = attend_back(
        queries, kv, key_places, grad_heads, cosine[:, :HEAD_COLS], sine[:, :HEAD_COLS], seq_dev
    )

    def mlp_return(left, right, kinds, what):
        terms = []
        for k in range(pieces):
            one = left if k == pieces - 1 else after(left, da2_got)
            terms.append(dot_tn(right, one[:, k * piece : (k + 1) * piece]).astype(BF))
        terms = [terms[digits[k]] for k in range(pieces)]
        for bit in reversed(far):
            half = len(terms) // 2
            got = [bit.swap(s, what) for s in terms[half:]]
            terms = [add_low(after(t, dq) if k == 0 else t, got[k]) for k, t in enumerate(terms[:half])]
        return mlp_rows(terms[0], kinds)

    both_back = mlp_return(a2, dboth, 2, "dboth")
    down_back = mlp_return(gb, hidden, 1, "ddown")
    dkv_two = reduce_rows(dkv.reshape(-1, 2 * HEAD_DIM), ctx_bits, "dkv")
    dkv_low = run(
        functools.partial(turn_back_kernel, all_seqs),
        list(dkv_two) + [cosine[:, HEAD_COLS:], sine[:, HEAD_COLS:]],
        [shape_of((dp * rows, 2 * HEAD_DIM), BF)],
    )[0]
    draw = jnp.concatenate([dq, dkv_low], -1)
    da1 = wide(dot_nt, draw, qkv, width, min(256, dp * rows))
    (grad_tokens,) = norm_back(attn_order, x, grad_middle, *reduce_rows(da1, dp_bits, "da1"), gain_all)
    q_total = add_low(*reduce_rows(dot_tn(a1, dq).astype(BF), ctx_bits, "dq_w"))
    kv_total = add_low(*reduce_rows(dot_tn(a1, dkv_low).astype(BF), ctx_bits, "dkv_w"))
    qkv_total = jnp.concatenate([q_total, kv_total], -1).reshape(dp, depth, qkv_cols)
    qkv_back = lax.all_to_all(qkv_total, "dp", 0, 0, tiled=True)
    out_total = dot_tn(heads, grad_branch).astype(BF).reshape(ctx, depth, width)
    out_total = relative(out_total, c_index, out_bits).reshape(ctx * depth, width)
    out_two = reduce_rows(out_total, out_bits, "dout_w")
    output_grad = out_two[0].astype(F32) + out_two[1].astype(F32)

    gate_grad, up_grad, mlp_sum = unpack(both_back, [gate_weight, up_weight], gain_two)
    down_grad = unpack(down_back, None, None)[0].T
    query_grad, key_grad, value_grad, attn_sum = run(
        functools.partial(unpack_qkv_kernel, dp),
        [query_weight, key_weight, value_weight, gain_one, qkv_back],
        [shape_of(w.shape, F32) for w in (query_weight, key_weight, value_weight, gain_one)],
    )
    return (
        result.reshape(seqs, seq_dev, width),
        grad_tokens.reshape(seqs, seq_dev, width),
        attn_sum[:, 0],
        query_grad,
        key_grad,
        value_grad,
        output_grad,
        mlp_sum[:, 0],
        gate_grad,
        up_grad,
        down_grad,
    )


def solution(mesh):
    dp, ctx = mesh.shape["dp"], mesh.shape["ctx"]

    def local(*args):
        return shards(dp, ctx, *args)

    weight = P(("dp", "ctx"), None)
    flat = P(("dp", "ctx"))
    acts = P("dp", "ctx", None)
    down = P(None, ("dp", "ctx"))
    return jax.shard_map(
        local,
        mesh=mesh,
        in_specs=(acts, acts, flat, weight, weight, weight, weight, flat, weight, weight, down),
        out_specs=(acts, acts, flat, weight, weight, weight, weight, flat, weight, weight, down),
        check_vma=False,
    )
```

time: 1010 us -> 642 us (0.64)
  other arithmetic: 181 us -> 43 us
  waiting for transfers between devices: 449 us -> 318 us
  local copies, waits for them, and re-layouts: 181 us -> 89.5 us
  Pallas kernels: 0 us -> 74.3 us
  matrix products: 99.8 us -> 30.6 us
  between operations: 17.1 us -> 2.4 us
    unnamed x2 -> x0, waiting for transfers between devices: 114 us -> none
    pallas_call x0 -> x20, Pallas kernels: none -> 74.3 us  [run(): pl.pallas_call(kernel, name=name, out_shape=list(outs), in_specs=specs or...]
    select_n x39 -> x0, other arithmetic: 63.1 us -> none  [the longest x20 27.4 us: trade(): high = jnp.where(mine == 0, got, keep)]
    ppermute x83 -> x61, waiting for transfers between devices: 334 us -> 277 us  [swap(): return lax.ppermute(value, self.axis, self.pairs)]
    all_to_all x0 -> x7, waiting for transfers between devices: none -> 41.3 us  [the longest x4 22.7 us: mlp_trade(): lax.all_to_all(parts, ('dp', 'ctx'), 0, 0, axis_index_groups=team_groups,...]
    rev x4 -> x0, local copies, waits for them, and re-layouts: 40 us -> none  [the longest x2 22.1 us: from_pieces(): out = jnp.where(bit.mine() == 1, jnp.flip(out, k + 1), out)]
    concatenate x48 -> x17, other arithmetic: 47.8 us -> 16.1 us  [the longest x3 5.76 us: shards(): out_rel = jnp.concatenate([out_rel, bit.swap(out_rel, 'out')], 0)]
    all_to_all x0 -> x7, starting transfers between devices: none -> 29.1 us  [the longest x4 16.4 us: mlp_trade(): lax.all_to_all(parts, ('dp', 'ctx'), 0, 0, axis_index_groups=team_groups,...]
  transfers between devices with their start and end apart: 84 -> 68, of which waited for: 38 -> 38; matrix products, arithmetic and copies ran while one was open for 39% -> 22% of each run, Pallas kernels for 0% -> 9%
where the time goes in v2:
time: 642 us; the launch traced here: 634 us
  waiting for transfers between devices  318 us (50%)
  local copies, waits for them, and re-layouts  89.5 us (14%)
  starting transfers between devices  76.6 us (12%)
  Pallas kernels  74.3 us (12%)
  other arithmetic  43 us (7%)
  matrix products  30.6 us (5%)
    ppermute x61, waiting for transfers between devices, swap(): return lax.ppermute(value, self.axis, self.pairs)  277 us
    pallas_call x20, Pallas kernels, run(): pl.pallas_call(kernel, name=name, out_shape=list(outs), in_specs=specs or...  74.3 us
    ppermute x61, starting transfers between devices, swap(): return lax.ppermute(value, self.axis, self.pairs)  47.5 us
    unnamed x198, local copies, waits for them, and re-layouts  29.8 us
    dot_general x11, matrix products, dot_tn(): lax.dot_general(left, right, (((0,), (0,)), ((), ())), preferred_element_...  28.1 us
    all_to_all x4, waiting for transfers between devices, mlp_trade(): lax.all_to_all(parts, ('dp', 'ctx'), 0, 0, axis_index_groups=team_groups,...  22.7 us
    all_to_all x4, starting transfers between devices, mlp_trade(): lax.all_to_all(parts, ('dp', 'ctx'), 0, 0, axis_index_groups=team_groups,...  16.4 us
    convert_element_type x12, other arithmetic, add_low(): return (a.astype(F32) + b.astype(F32)).astype(BF)  13.6 us
  transfers between devices with their start and end apart: 68, of which 38 were waited for; matrix products, arithmetic and copies ran while one was open for 22% of the time, Pallas kernels for 9%

profile of v2, /device:TPU:0, one launch (start us, length us, event | category | flops | bytes accessed | tf_op | source)
XLA Modules:
  0.0 634.5 jit_solution(14959793283743336545)
XLA Ops:
  8.9 6.5 %all-to-all-done = bf16[4,64,640]{2,1,0:T(8,128)(2,1)} async-done(((bf16[4,64,640]{2,1,0:T(8,128)(2,1)}), bf16[4,64,640]{2,1,0:T(8,128)(2,1)}, u32[]{:S(2)}, u32[]{:S(2)}) %all-to-all-start) | async-done | bytes 327712 | tf_op jit(solution)/shard_map/all_to_all | solution.py:747
  26.8 22.7 %all-to-all-done.1 = bf16[8,128,704]{1,2,0:T(8,128)(2,1)S(1)} async-done(((bf16[8,128,704]{1,2,0:T(8,128)(2,1)}), bf16[8,128,704]{1,2,0:T(8,128)(2,1)S(1)}, u32[]{:S(2)}, u32[]{:S(2)}) %all-to-all-start.1) | async-done | bytes 1441824 | tf_op jit(solution)/shard_map/all_to_all | solution.py:726
  53.0 4.7 reshape.165
  58.3 5.0 all-to-all-start.2
  63.4 6.9 %all-to-all-done.2 = bf16[32,1,64]{2,1,0:T(2,128)(2,1)S(1)} async-done(((bf16[32,1,64]{2,1,0:T(2,128)(2,1)}), bf16[32,1,64]{2,1,0:T(2,128)(2,1)S(1)}, u32[]{:S(2)}, u32[]{:S(2)}) %all-to-all-start.2) | async-done | bytes 4128 | tf_op jit(solution)/shard_map/all_to_all | solution.py:750
  74.3 11.3 %collective-permute-done.1 = bf16[128,2048]{1,0:T(8,128)(2,1)S(1)} collective-permute-done((bf16[128,2048]{1,0:T(8,128)(2,1)S(1)}, bf16[128,2048]{1,0:T(8,128)(2,1)S(1)}, u32[]{:S(2)}, u32[]{:S(2)}) %collective-permute-start.1) | collective-permute-done | bytes 524320 | tf_op jit(solution)/shard_map/a1_dp1/ppermute | solution.py:73
  92.9 4.4 all-to-all-start.3
  97.9 14.4 %collective-permute-done.10 = bf16[64,2048]{1,0:T(8,128)(2,1)} collective-permute-done((bf16[64,2048]{1,0:T(8,128)(2,1)S(1)}, bf16[64,2048]{1,0:T(8,128)(2,1)}, u32[]{:S(2)}, u32[]{:S(2)}) %collective-permute-start.10) | collective-permute-done | bytes 262176 | tf_op jit(solution)/shard_map/out_ctx2/ppermute | solution.py:73
  144.4 43.8 %collective-permute-done.7 = bf16[1024,128]{1,0:T(8,128)(2,1)} collective-permute-done((bf16[1024,128]{1,0:T(8,128)(2,1)}, bf16[1024,128]{1,0:T(8,128)(2,1)}, u32[]{:S(2)}, u32[]{:S(2)}) %collective-permute-start.7) | collective-permute-done | bytes 262176 | tf_op jit(solution)/shard_map/kv_ctx1/ppermute | solution.py:73
  192.3 10.0 %collective-permute-done.8 = bf16[2048,128]{1,0:T(8,128)(2,1)S(1)} collective-permute-done((bf16[2048,128]{1,0:T(8,128)(2,1)S(1)}, bf16[2048,128]{1,0:T(8,128)(2,1)S(1)}, u32[]{:S(2)}, u32[]{:S(2)}) %collective-permute-start.8) | collective-permute-done | bytes 524320 | tf_op jit(solution)/shard_map/kv_ctx0/ppermute | solution.py:73
  202.4 5.2 attend_kernel.1
  214.6 11.0 %collective-permute-done.22 = bf16[128,2048]{1,0:T(8,128)(2,1)S(1)} collective-permute-done((bf16[128,2048]{1,0:T(8,128)(2,1)S(1)}, bf16[128,2048]{1,0:T(8,128)(2,1)S(1)}, u32[]{:S(2)}, u32[]{:S(2)}) %collective-permute-start.22) | collective-permute-done | bytes 524320 | tf_op jit(solution)/shard_map/gb_ctx1/ppermute | solution.py:73
  228.6 8.6 %collective-permute-done.14.b_ref = bf16[128,2048]{1,0:T(8,128)(2,1)S(1)} collective-permute-done((bf16[128,2048]{1,0:T(8,128)(2,1)S(1)}, bf16[128,2048]{1,0:T(8,128)(2,1)S(1)}, u32[]{:S(2)}, u32[]{:S(2)}) %collective-permute-start.14) | collective-permute-done | bytes 524320 | tf_op jit(solution)/shard_map/branch_dp1/ppermute | solution.py:73
  245.4 5.5 collective-permute-done.16
  267.1 31.2 %collective-permute-done.27.refs_2_ = bf16[704,512]{1,0:T(8,128)(2,1)} collective-permute-done((bf16[704,512]{1,0:T(8,128)(2,1)}, bf16[704,512]{1,0:T(8,128)(2,1)}, u32[]{:S(2)}, u32[]{:S(2)}) %collective-permute-start.27) | collective-permute-done | bytes 720928 | tf_op jit(solution)/shard_map/down_ctx2/ppermute | solution.py:73
  306.5 11.1 %gate_kernel.1 = (bf16[1024,704]{1,0:T(8,128)(2,1)}, f32[1024,704]{1,0:T(8,128)}, f32[1024,704]{1,0:T(8,128)}) custom-call(bf16[1024,2048]{1,0:T(8,128)(2,1)} %constant_dynamic-update-slice_fusion.9.a_ref, bf16[1408,512]{1,0:T(8,128)(2,1)S(1)} %copy.67.refs_0_.refs_4_, bf16[1408,512]{1,0:T(8,128)(2,1)S(1)} %copy-done.7, ...), custom_call_target="tpu_custom_call" | custom-call | tf_op jit(solution)/shard_map/gate_kernel/pallas_call | solution.py:47
  317.6 8.9 %collective-permute-done.28.refs_3_ = bf16[704,512]{1,0:T(8,128)(2,1)S(1)} collective-permute-done((bf16[704,512]{1,0:T(8,128)(2,1)}, bf16[704,512]{1,0:T(8,128)(2,1)S(1)}, u32[]{:S(2)}, u32[]{:S(2)}) %collective-permute-start.28) | collective-permute-done | bytes 720928 | tf_op jit(solution)/shard_map/down_ctx0/ppermute | solution.py:73
  327.3 16.6 %hidden_kernel.1 = (bf16[1024,1408]{1,0:T(8,128)(2,1)}, bf16[1024,2048]{1,0:T(8,128)(2,1)}) custom-call(bf16[1024,2048]{1,0:T(8,128)(2,1)} %constant_dynamic-update-slice_fusion.20.g_ref, f32[1024,704]{1,0:T(8,128)} %get-tuple-element.60.one_ref, f32[1024,704]{1,0:T(8,128)} %get-tuple-element.61.two_ref, bf16[704,512]{1,0:T(8,128)(2,1)} %copy-done.4, ...), custom_call_target="tpu_custom_call" | custom-call | tf_op jit(solution)/shard_map/hidden_kernel/pallas_call | solution.py:47
  361.9 5.5 collective-permute-done.30
  371.8 8.8 %collective-permute-done.31 = bf16[128,2048]{1,0:T(8,128)(2,1)S(1)} collective-permute-done((bf16[128,2048]{1,0:T(8,128)(2,1)S(1)}, bf16[128,2048]{1,0:T(8,128)(2,1)S(1)}, u32[]{:S(2)}, u32[]{:S(2)}) %collective-permute-start.31) | collective-permute-done | bytes 524320 | tf_op jit(solution)/shard_map/da2_dp1/ppermute | solution.py:73
  380.8 9.0 %collective-permute-done.33.b_ref = bf16[128,2048]{1,0:T(8,128)(2,1)S(1)} collective-permute-done((bf16[128,2048]{1,0:T(8,128)(2,1)S(1)}, bf16[128,2048]{1,0:T(8,128)(2,1)S(1)}, u32[]{:S(2)}, u32[]{:S(2)}) %collective-permute-start.33) | collective-permute-done | bytes 524320 | tf_op jit(solution)/shard_map/da2_ctx1/ppermute | solution.py:73
  397.7 6.0 collective-permute-done.34
  416.9 11.5 %attend_back_kernel.1 = (bf16[512,512]{1,0:T(8,128)(2,1)S(1)}, bf16[8,8,64,128]{3,2,1,0:T(8,128)(2,1)S(1)}) custom-call(bf16[512,512]{1,0:T(8,128)(2,1)S(1)} %copy-done.30, bf16[8,8,64,128]{3,2,1,0:T(8,128)(2,1)S(1)} %bitcast.65, s32[1,512]{1,0:T(1,128)S(1)} %add.232.key_ref, f32[512,512]{1,0:T(8,128)S(1)} %fusion.33.do_ref, ...), custom_call_target="tpu_custom_call" | custom-call | tf_op jit(solution)/shard_map/attend_back_kernel/pallas_call | solution.py:47
  436.8 10.4 %collective-permute-done.55 = bf16[1408,512]{1,0:T(8,128)(2,1)} collective-permute-done((bf16[1408,512]{1,0:T(8,128)(2,1)}, bf16[1408,512]{1,0:T(8,128)(2,1)}, u32[]{:S(2)}, u32[]{:S(2)}) %collective-permute-start.55) | collective-permute-done | bytes 1441824 | tf_op jit(solution)/shard_map/dboth_ctx0/ppermute | solution.py:73
  453.4 20.8 %collective-permute-done.57 = bf16[1408,512]{1,0:T(8,128)(2,1)} collective-permute-done((bf16[1408,512]{1,0:T(8,128)(2,1)}, bf16[1408,512]{1,0:T(8,128)(2,1)}, u32[]{:S(2)}, u32[]{:S(2)}) %collective-permute-start.57) | collective-permute-done | bytes 1441824 | tf_op jit(solution)/shard_map/dboth_ctx2/ppermute | solution.py:73
  485.2 5.0 reshape.176
  499.0 6.1 wide_kernel.2
  512.3 6.8 %collective-permute-done.43.b_ref = bf16[512,128]{1,0:T(8,128)(2,1)S(1)} collective-permute-done((bf16[512,128]{1,0:T(8,128)(2,1)S(1)}, bf16[512,128]{1,0:T(8,128)(2,1)S(1)}, u32[]{:S(2)}, u32[]{:S(2)}) %collective-permute-start.43) | collective-permute-done | bytes 131104 | tf_op jit(solution)/shard_map/dkv_ctx2/ppermute | solution.py:73
  525.9 4.5 collective-permute-done.49
  552.9 15.4 %collective-permute-done.48 = bf16[256,512]{0,1:T(8,128)(2,1)S(1)} collective-permute-done((bf16[256,512]{0,1:T(8,128)(2,1)S(1)}, bf16[256,512]{0,1:T(8,128)(2,1)S(1)}, u32[]{:S(2)}, u32[]{:S(2)}) %collective-permute-start.48) | collective-permute-done | bytes 262176 | tf_op jit(solution)/shard_map/dq_w_ctx2/ppermute | solution.py:73
  574.5 5.1 all-to-all-done.4.p_ref
  591.9 16.1 %collective-permute-done.37 = bf16[64,2048]{1,0:T(8,128)(2,1)S(1)} collective-permute-done((bf16[64,2048]{1,0:T(8,128)(2,1)S(1)}, bf16[64,2048]{1,0:T(8,128)(2,1)S(1)}, u32[]{:S(2)}, u32[]{:S(2)}) %collective-permute-start.37) | collective-permute-done | bytes 262176 | tf_op jit(solution)/shard_map/result_ctx1/ppermute | solution.py:73
  (445 shorter events, 273.1 us)
Async XLA Ops:
  19.7 29.8 %all-to-all-start.1 = ((bf16[8,128,704]{1,2,0:T(8,128)(2,1)}), bf16[8,128,704]{1,2,0:T(8,128)(2,1)S(1)}, u32[]{:S(2)}, u32[]{:S(2)}) async-start(bf16[8,128,704]{1,2,0:T(8,128)(2,1)} %copy.64), calls=%async_computation.1 | async-start | bytes 2883584 | tf_op jit(solution)/shard_map/all_to_all | solution.py:726
  23.4 49.2 %collective-permute-start.3 = (bf16[256,640]{1,0:T(8,128)(2,1)}, bf16[256,640]{1,0:T(8,128)(2,1)}, u32[]{:S(2)}, u32[]{:S(2)}) collective-permute-start(bf16[256,640]{1,0:T(8,128)(2,1)} %bitcast.3), channel_id=1, source_target_pairs={{0,4},{1,5},{2,6},{3,7},{4,0},{5,1},{6,2},{7,3},{8,12},{9,13},{10,... | collective-permute-start | bytes 983048 | tf_op jit(solution)/shard_map/qkv_ctx2/ppermute | solution.py:73
  86.8 30.7 %collective-permute-start.2 = (bf16[256,2048]{1,0:T(8,128)(2,1)}, bf16[256,2048]{1,0:T(8,128)(2,1)}, u32[]{:S(2)}, u32[]{:S(2)}) collective-permute-start(bf16[256,2048]{1,0:T(8,128)(2,1)} %pad_maximum_fusion.3), channel_id=1, source_target_pairs={{0,8},{8,0},{16,24},{24,16},{1,9},{9,1},{17,25},{25,17},{2,10},{10... | collective-permute-start | bytes 3145736 | tf_op jit(solution)/shard_map/a1_dp0/ppermute | solution.py:73
  91.2 31.8 %collective-permute-start.5 = (bf16[1024,640]{1,0:T(8,128)(2,1)S(1)}, bf16[1024,640]{1,0:T(8,128)(2,1)S(1)}, u32[]{:S(2)}, u32[]{:S(2)}) collective-permute-start(bf16[1024,640]{1,0:T(8,128)(2,1)S(1)} %pad_maximum_fusion.2.refs_3_.refs_0_), channel_id=1, source_target_pairs={{0,1},{1,0},{2,3},{3,2},{4,5},{5,4},{6,7},{7,6},{8,9},{9,8},{10,11... | collective-permute-start | bytes 3932168 | tf_op jit(solution)/shard_map/qkv_ctx0/ppermute | solution.py:73
  92.9 27.8 %all-to-all-start.3 = ((bf16[8,64,704]{2,1,0:T(8,128)(2,1)}), bf16[8,64,704]{2,1,0:T(8,128)(2,1)}, u32[]{:S(2)}, u32[]{:S(2)}) async-start(bf16[8,64,704]{2,1,0:T(8,128)(2,1)} %copy-done.19), calls=%async_computation.3 | async-start | bytes 1572864 | tf_op jit(solution)/shard_map/all_to_all | solution.py:726
  134.0 56.2 %collective-permute-start.12 = (bf16[256,2048]{1,0:T(8,128)(2,1)}, bf16[256,2048]{1,0:T(8,128)(2,1)}, u32[]{:S(2)}, u32[]{:S(2)}) collective-permute-start(bf16[256,2048]{1,0:T(8,128)(2,1)} %pad_maximum_fusion.4), channel_id=1, source_target_pairs={{0,2},{1,3},{2,0},{3,1},{4,6},{5,7},{6,4},{7,5},{8,10},{9,11},{10,... | collective-permute-start | bytes 3145736 | tf_op jit(solution)/shard_map/out_ctx1/ppermute | solution.py:73
  138.9 49.2 %collective-permute-start.7 = (bf16[1024,128]{1,0:T(8,128)(2,1)}, bf16[1024,128]{1,0:T(8,128)(2,1)}, u32[]{:S(2)}, u32[]{:S(2)}) collective-permute-start(bf16[1024,128]{1,0:T(8,128)(2,1)} %pad_maximum_fusion.17), channel_id=1, source_target_pairs={{0,2},{1,3},{2,0},{3,1},{4,6},{5,7},{6,4},{7,5},{8,10},{9,11},{10,... | collective-permute-start | bytes 786440 | tf_op jit(solution)/shard_map/kv_ctx1/ppermute | solution.py:73
  140.7 66.9 %collective-permute-start.9 = (bf16[1408,512]{1,0:T(8,128)(2,1)S(1)}, bf16[1408,512]{1,0:T(8,128)(2,1)}, u32[]{:S(2)}, u32[]{:S(2)}) collective-permute-start(bf16[1408,512]{1,0:T(8,128)(2,1)S(1)} %copy.67.refs_0_.refs_4_), channel_id=1, source_target_pairs={{0,4},{1,5},{2,6},{3,7},{4,0},{5,1},{6,2},{7,3},{8,12},{9,13},{10,... | collective-permute-start | bytes 4325384 | tf_op jit(solution)/shard_map/both_ctx2/ppermute | solution.py:73
  143.3 65.9 %collective-permute-start = (bf16[1408,512]{1,0:T(8,128)(2,1)S(1)}, bf16[1408,512]{1,0:T(8,128)(2,1)S(1)}, u32[]{:S(2)}, u32[]{:S(2)}) collective-permute-start(bf16[1408,512]{1,0:T(8,128)(2,1)S(1)} %copy.67.refs_0_.refs_4_), channel_id=1, source_target_pairs={{0,1},{1,0},{2,3},{3,2},{4,5},{5,4},{6,7},{7,6},{8,9},{9,8},{10,11... | collective-permute-start | bytes 4325384 | tf_op jit(solution)/shard_map/both_ctx0/ppermute | solution.py:73
  212.9 24.3 %collective-permute-start.14 = (bf16[128,2048]{1,0:T(8,128)(2,1)S(1)}, bf16[128,2048]{1,0:T(8,128)(2,1)S(1)}, u32[]{:S(2)}, u32[]{:S(2)}) collective-permute-start(bf16[128,2048]{1,0:T(8,128)(2,1)S(1)} %get-tuple-element.107), channel_id=1, source_target_pairs={{0,16},{8,24},{16,0},{24,8},{1,17},{9,25},{17,1},{25,9},{2,18},{10... | collective-permute-start | bytes 1572872 | tf_op jit(solution)/shard_map/branch_dp1/ppermute | solution.py:73
  244.3 55.8 %collective-permute-start.25 = (bf16[512,2048]{1,0:T(8,128)(2,1)}, bf16[512,2048]{1,0:T(8,128)(2,1)}, u32[]{:S(2)}, u32[]{:S(2)}) collective-permute-start(bf16[512,2048]{1,0:T(8,128)(2,1)} %get-tuple-element.123), channel_id=1, source_target_pairs={{0,8},{8,0},{16,24},{24,16},{1,9},{9,1},{17,25},{25,17},{2,10},{10... | collective-permute-start | bytes 6291464 | tf_op jit(solution)/shard_map/gb_dp0/ppermute | solution.py:73
  261.4 41.9 %collective-permute-start.19 = (bf16[512,2048]{1,0:T(8,128)(2,1)}, bf16[512,2048]{1,0:T(8,128)(2,1)}, u32[]{:S(2)}, u32[]{:S(2)}) collective-permute-start(bf16[512,2048]{1,0:T(8,128)(2,1)} %get-tuple-element.127), channel_id=1, source_target_pairs={{0,8},{8,0},{16,24},{24,16},{1,9},{9,1},{17,25},{25,17},{2,10},{10... | collective-permute-start | bytes 6291464 | tf_op jit(solution)/shard_map/a2_dp0/ppermute | solution.py:73
  261.4 45.1 %collective-permute-start.20 = (bf16[1408,512]{1,0:T(8,128)(2,1)}, bf16[1408,512]{1,0:T(8,128)(2,1)}, u32[]{:S(2)}, u32[]{:S(2)}) collective-permute-start(bf16[1408,512]{1,0:T(8,128)(2,1)} %collective-permute-done.9.refs_2_.refs_6_), channel_id=1, source_target_pairs={{0,1},{1,0},{2,3},{3,2},{4,5},{5,4},{6,7},{7,6},{8,9},{9,8},{10,11... | collective-permute-start | bytes 4325384 | tf_op jit(solution)/shard_map/both_ctx0/ppermute | solution.py:73
  263.9 34.4 %collective-permute-start.27 = (bf16[704,512]{1,0:T(8,128)(2,1)}, bf16[704,512]{1,0:T(8,128)(2,1)}, u32[]{:S(2)}, u32[]{:S(2)}) collective-permute-start(bf16[704,512]{1,0:T(8,128)(2,1)} %copy.71), channel_id=1, source_target_pairs={{0,4},{1,5},{2,6},{3,7},{4,0},{5,1},{6,2},{7,3},{8,12},{9,13},{10,... | collective-permute-start | bytes 2162696 | tf_op jit(solution)/shard_map/down_ctx2/ppermute | solution.py:73
  265.3 52.3 %collective-permute-start.26 = (bf16[704,512]{1,0:T(8,128)(2,1)S(1)}, bf16[704,512]{1,0:T(8,128)(2,1)S(1)}, u32[]{:S(2)}, u32[]{:S(2)}) collective-permute-start(bf16[704,512]{1,0:T(8,128)(2,1)S(1)} %copy.72.refs_0_), channel_id=1, source_target_pairs={{0,1},{1,0},{2,3},{3,2},{4,5},{5,4},{6,7},{7,6},{8,9},{9,8},{10,11... | collective-permute-start | bytes 2162696 | tf_op jit(solution)/shard_map/down_ctx0/ppermute | solution.py:73
  298.3 28.2 %collective-permute-start.28 = (bf16[704,512]{1,0:T(8,128)(2,1)}, bf16[704,512]{1,0:T(8,128)(2,1)S(1)}, u32[]{:S(2)}, u32[]{:S(2)}) collective-permute-start(bf16[704,512]{1,0:T(8,128)(2,1)} %collective-permute-done.27.refs_2_), channel_id=1, source_target_pairs={{0,1},{1,0},{2,3},{3,2},{4,5},{5,4},{6,7},{7,6},{8,9},{9,8},{10,11... | collective-permute-start | bytes 2162696 | tf_op jit(solution)/shard_map/down_ctx0/ppermute | solution.py:73
  354.7 49.2 %collective-permute-start.56 = (bf16[1408,512]{1,0:T(8,128)(2,1)S(1)}, bf16[1408,512]{1,0:T(8,128)(2,1)S(1)}, u32[]{:S(2)}, u32[]{:S(2)}) collective-permute-start(bf16[1408,512]{1,0:T(8,128)(2,1)S(1)} %convolution_convert_fusion), channel_id=1, source_target_pairs={{0,1},{1,0},{2,3},{3,2},{4,5},{5,4},{6,7},{7,6},{8,9},{9,8},{10,11... | collective-permute-start | bytes 4325384 | tf_op jit(solution)/shard_map/dboth_ctx0/ppermute | solution.py:73
  361.6 67.6 %collective-permute-start.58 = (bf16[704,512]{1,0:T(8,128)(2,1)S(1)}, bf16[704,512]{1,0:T(8,128)(2,1)S(1)}, u32[]{:S(2)}, u32[]{:S(2)}) collective-permute-start(bf16[704,512]{1,0:T(8,128)(2,1)S(1)} %convolution_convert_fusion.10), channel_id=1, source_target_pairs={{0,1},{1,0},{2,3},{3,2},{4,5},{5,4},{6,7},{7,6},{8,9},{9,8},{10,11... | collective-permute-start | bytes 2162696 | tf_op jit(solution)/shard_map/ddown_ctx0/ppermute | solution.py:73
  371.8 57.7 %collective-permute-start.60 = (bf16[704,512]{1,0:T(8,128)(2,1)S(1)}, bf16[704,512]{1,0:T(8,128)(2,1)S(1)}, u32[]{:S(2)}, u32[]{:S(2)}) collective-permute-start(bf16[704,512]{1,0:T(8,128)(2,1)S(1)} %add_convert_fusion.8), channel_id=1, source_target_pairs={{0,4},{1,5},{2,6},{3,7},{4,0},{5,1},{6,2},{7,3},{8,12},{9,13},{10,... | collective-permute-start | bytes 2162696 | tf_op jit(solution)/shard_map/ddown_ctx2/ppermute | solution.py:73
  396.4 50.9 %collective-permute-start.55 = (bf16[1408,512]{1,0:T(8,128)(2,1)}, bf16[1408,512]{1,0:T(8,128)(2,1)}, u32[]{:S(2)}, u32[]{:S(2)}) collective-permute-start(bf16[1408,512]{1,0:T(8,128)(2,1)} %convolution_convert_fusion.2), channel_id=1, source_target_pairs={{0,1},{1,0},{2,3},{3,2},{4,5},{5,4},{6,7},{7,6},{8,9},{9,8},{10,11... | collective-permute-start | bytes 4325384 | tf_op jit(solution)/shard_map/dboth_ctx0/ppermute | solution.py:73
  408.0 66.2 %collective-permute-start.57 = (bf16[1408,512]{1,0:T(8,128)(2,1)}, bf16[1408,512]{1,0:T(8,128)(2,1)}, u32[]{:S(2)}, u32[]{:S(2)}) collective-permute-start(bf16[1408,512]{1,0:T(8,128)(2,1)} %fusion.2), channel_id=1, source_target_pairs={{0,4},{1,5},{2,6},{3,7},{4,0},{5,1},{6,2},{7,3},{8,12},{9,13},{10,... | collective-permute-start | bytes 4325384 | tf_op jit(solution)/shard_map/dboth_ctx2/ppermute | solution.py:73
  432.8 110.2 %all-to-all-start.6 = ((bf16[8,64,704]{2,1,0:T(8,128)(2,1)}), bf16[8,64,704]{2,1,0:T(8,128)(2,1)S(1)}, u32[]{:S(2)}, u32[]{:S(2)}) async-start(bf16[8,64,704]{2,1,0:T(8,128)(2,1)} %bitcast.83), calls=%async_computation.6 | async-start | bytes 1572864 | tf_op jit(solution)/shard_map/all_to_all | solution.py:726
  452.9 69.8 %collective-permute-start.52 = (bf16[256,2048]{1,0:T(8,128)(2,1)}, bf16[256,2048]{1,0:T(8,128)(2,1)}, u32[]{:S(2)}, u32[]{:S(2)}) collective-permute-start(bf16[256,2048]{1,0:T(8,128)(2,1)} %bitcast.26), channel_id=1, source_target_pairs={{0,2},{1,3},{2,0},{3,1},{4,6},{5,7},{6,4},{7,5},{8,10},{9,11},{10,... | collective-permute-start | bytes 3145736 | tf_op jit(solution)/shard_map/dout_w_ctx1/ppermute | solution.py:73
  453.1 24.0 %collective-permute-start.41 = (bf16[2048,128]{1,0:T(8,128)(2,1)S(1)}, bf16[2048,128]{1,0:T(8,128)(2,1)S(1)}, u32[]{:S(2)}, u32[]{:S(2)}) collective-permute-start(bf16[2048,128]{1,0:T(8,128)(2,1)S(1)} %bitcast.88), channel_id=1, source_target_pairs={{0,1},{1,0},{2,3},{3,2},{4,5},{5,4},{6,7},{7,6},{8,9},{9,8},{10,11... | collective-permute-start | bytes 1572872 | tf_op jit(solution)/shard_map/dkv_ctx0/ppermute | solution.py:73
  478.7 29.7 %collective-permute-start.42 = (bf16[1024,128]{1,0:T(8,128)(2,1)}, bf16[1024,128]{1,0:T(8,128)(2,1)}, u32[]{:S(2)}, u32[]{:S(2)}) collective-permute-start(bf16[1024,128]{1,0:T(8,128)(2,1)} %slice.291), channel_id=1, source_target_pairs={{0,2},{1,3},{2,0},{3,1},{4,6},{5,7},{6,4},{7,5},{8,10},{9,11},{10,... | collective-permute-start | bytes 786440 | tf_op jit(solution)/shard_map/dkv_ctx1/ppermute | solution.py:73
  497.1 33.5 %collective-permute-start.46 = (bf16[1024,512]{0,1:T(8,128)(2,1)S(1)}, bf16[1024,512]{0,1:T(8,128)(2,1)S(1)}, u32[]{:S(2)}, u32[]{:S(2)}) collective-permute-start(bf16[1024,512]{0,1:T(8,128)(2,1)S(1)} %slice.299), channel_id=1, source_target_pairs={{0,1},{1,0},{2,3},{3,2},{4,5},{5,4},{6,7},{7,6},{8,9},{9,8},{10,11... | collective-permute-start | bytes 3145736 | tf_op jit(solution)/shard_map/dq_w_ctx0/ppermute | solution.py:73
  508.4 75.4 %collective-permute-start.36 = (bf16[512,2048]{1,0:T(8,128)(2,1)}, bf16[512,2048]{1,0:T(8,128)(2,1)}, u32[]{:S(2)}, u32[]{:S(2)}) collective-permute-start(bf16[512,2048]{1,0:T(8,128)(2,1)} %slice.282), channel_id=1, source_target_pairs={{0,8},{8,0},{16,24},{24,16},{1,9},{9,1},{17,25},{25,17},{2,10},{10... | collective-permute-start | bytes 6291464 | tf_op jit(solution)/shard_map/result_dp0/ppermute | solution.py:73
  525.3 24.8 %collective-permute-start.53 = (bf16[128,2048]{1,0:T(8,128)(2,1)}, bf16[128,2048]{1,0:T(8,128)(2,1)}, u32[]{:S(2)}, u32[]{:S(2)}) collective-permute-start(bf16[128,2048]{1,0:T(8,128)(2,1)} %slice.311), channel_id=1, source_target_pairs={{0,1},{1,0},{2,3},{3,2},{4,5},{5,4},{6,7},{7,6},{8,9},{9,8},{10,11... | collective-permute-start | bytes 1572872 | tf_op jit(solution)/shard_map/dout_w_ctx0/ppermute | solution.py:73
  543.0 29.8 %collective-permute-start.44 = (bf16[256,2048]{1,0:T(8,128)(2,1)}, bf16[256,2048]{1,0:T(8,128)(2,1)}, u32[]{:S(2)}, u32[]{:S(2)}) collective-permute-start(bf16[256,2048]{1,0:T(8,128)(2,1)} %slice.295), channel_id=1, source_target_pairs={{0,8},{8,0},{16,24},{24,16},{1,9},{9,1},{17,25},{25,17},{2,10},{10... | collective-permute-start | bytes 3145736 | tf_op jit(solution)/shard_map/da1_dp0/ppermute | solution.py:73
  552.2 59.9 %collective-permute-start.54 = (bf16[64,2048]{1,0:T(8,128)(2,1)}, bf16[64,2048]{1,0:T(8,128)(2,1)}, u32[]{:S(2)}, u32[]{:S(2)}) collective-permute-start(bf16[64,2048]{1,0:T(8,128)(2,1)} %slice.313), channel_id=1, source_target_pairs={{0,4},{1,5},{2,6},{3,7},{4,0},{5,1},{6,2},{7,3},{8,12},{9,13},{10,... | collective-permute-start | bytes 786440 | tf_op jit(solution)/shard_map/dout_w_ctx2/ppermute | solution.py:73
  579.5 42.5 %all-to-all-start.5 = ((bf16[8,128,704]{1,2,0:T(8,128)(2,1)}), bf16[8,128,704]{1,2,0:T(8,128)(2,1)}, u32[]{:S(2)}, u32[]{:S(2)}) async-start(bf16[8,128,704]{1,2,0:T(8,128)(2,1)} %copy.79), calls=%async_computation.5 | async-start | bytes 2883584 | tf_op jit(solution)/shard_map/all_to_all | solution.py:726
  591.3 28.4 %collective-permute-start.45 = (bf16[128,2048]{1,0:T(8,128)(2,1)}, bf16[128,2048]{1,0:T(8,128)(2,1)S(1)}, u32[]{:S(2)}, u32[]{:S(2)}) collective-permute-start(bf16[128,2048]{1,0:T(8,128)(2,1)} %get-tuple-element.103), channel_id=1, source_target_pairs={{0,16},{8,24},{16,0},{24,8},{1,17},{9,25},{17,1},{25,9},{2,18},{10... | collective-permute-start | bytes 1572872 | tf_op jit(solution)/shard_map/da1_dp1/ppermute | solution.py:73
  (125 other events, 1287.6 us)

commit v3 on v2

--- a/solution.py
+++ b/solution.py
@@ -68,20 +68,27 @@
     def mine(self):
         return (lax.axis_index(self.axis) >> self.bit) & 1
 
-    def swap(self, value, what="rows"):
+    def swap(self, value, what):
         with jax.named_scope(f"{what}_{self.axis}{self.bit}"):
             return lax.ppermute(value, self.axis, self.pairs)
 
 
+def swap_difference(value, axis, size, difference, what):
+    with jax.named_scope(f"{what}_{axis}"):
+        return lax.ppermute(value, axis, [(i, i ^ difference) for i in range(size)])
+
+
 def after(value, *others):
     return lax.optimization_barrier((value,) + others)[0]
 
 
 class Order:
-    def __init__(self, names, gathered, rest, depth):
-        self.names, self.gathered, self.rest, self.depth = names, gathered, rest, depth
-        self.rel = gathered + rest
-        self.fast = depth == 64 and len(names) == 5 and names[-1] in gathered and rest[-1] is not names[-1]
+    def __init__(self, names, rel, gathered, depth):
+        self.names, self.rel, self.gathered, self.depth = names, rel, gathered, depth
+        self.whole_tiles = rel[-1] is names[-1] and not gathered
+        self.fast = depth == 64 and len(names) == 5 and (
+            self.whole_tiles or (rel[-1] is not names[-1] and rel[-1] not in gathered)
+        )
         self.mine = jnp.stack(
             [b.mine() if b in gathered else jnp.zeros((), jnp.int32) for b in names]
         ).astype(jnp.int32)
@@ -92,6 +99,9 @@
         last = self.rel[-1]
         for q in range(16):
             value = {b: (q >> (3 - i)) & 1 for i, b in enumerate(head)}
+            if self.whole_tiles:
+                write(q, read(sum(value[b] << (3 - i) for i, b in enumerate(self.names[:-1]))))
+                continue
 
             def source(low):
                 index = 0
@@ -103,15 +113,21 @@
                 return read(index)
 
             a, b = source(0), source(1)
-            side = value[self.names[-1]] ^ mine[4]
-            first = jnp.where(lanes < 64, a, pltpu.roll(b, 64, 1))
-            second = jnp.where(lanes < 64, pltpu.roll(a, 64, 1), b)
-            write(q, jnp.where(side == 0, first, second))
+            side = value[self.names[-1]]
+            low = lambda: jnp.where(lanes < 64, a, pltpu.roll(b, 64, 1))
+            high = lambda: jnp.where(lanes < 64, pltpu.roll(a, 64, 1), b)
+            if self.names[-1] in self.gathered:
+                write(q, jnp.where((side ^ mine[4]) == 0, low(), high()))
+            else:
+                write(q, low() if side == 0 else high())
 
     def from_tiles(self, read, write, mine):
         lanes = lax.broadcasted_iota(jnp.int32, (1, 128), 1)
         for t in range(16):
             value = {b: (t >> (3 - i)) & 1 for i, b in enumerate(self.names[:-1])}
+            if self.whole_tiles:
+                write(t, read(sum(value[b] << (3 - i) for i, b in enumerate(self.rel[:-1]))))
+                continue
 
             def source(y):
                 index = 0
@@ -366,12 +382,42 @@
     return run(functools.partial(unpack_kernel, count, kinds, True), [parts] + weights + [gain], outs)
 
 
-def pack_qkv_kernel(count, q_ref, k_ref, v_ref, out_ref):
+def pack_qkv_kernel(count, me_ref, q_ref, k_ref, v_ref, out_ref):
     for t in range(count):
-        out_ref[t, :, :HEAD_COLS] = q_ref[:, t * HEAD_COLS : (t + 1) * HEAD_COLS]
+        slot = me_ref[0] ^ t
+        out_ref[slot, :, :HEAD_COLS] = q_ref[:, t * HEAD_COLS : (t + 1) * HEAD_COLS]
         lanes = slice(t * HEAD_DIM, (t + 1) * HEAD_DIM)
         both = jnp.concatenate([k_ref[:, lanes].astype(F32), v_ref[:, lanes].astype(F32)], -1)
-        out_ref[t, :, HEAD_COLS:] = both.astype(BF)
+        out_ref[slot, :, HEAD_COLS:] = both.astype(BF)
+
+
+def place_kernel(count, me_ref, *refs):
+    for r in range(count):
+        refs[-1][me_ref[0] ^ r] = refs[r][...]
+
+
+def columns_kernel(kinds, in_ref, *outs):
+    count, depth, units = in_ref.shape
+    depth = depth // kinds
+    step = max(1, 128 // depth)
+    for m in range(kinds):
+        for t in range(0, count, step):
+            rows = [in_ref[t + i, m * depth : (m + 1) * depth] for i in range(step)]
+            both = jnp.concatenate(rows, 0).astype(F32)
+            outs[m][:, t * depth : (t + step) * depth] = both.T.astype(BF)
+
+
+def rows_kernel(kinds, depth, *refs):
+    out_ref = refs[-1]
+    count = out_ref.shape[0]
+    units = out_ref.shape[2]
+    step = max(1, 128 // depth)
+    for m in range(kinds):
+        for t in range(0, count, step):
+            lanes = slice(t * depth, (t + step) * depth)
+            both = sum(r[m * units : (m + 1) * units, lanes].astype(F32) for r in refs[:-1]).T
+            for i in range(step):
+                out_ref[t + i, m * depth : (m + 1) * depth] = both[i * depth : (i + 1) * depth].astype(BF)
 
 
 def unpack_qkv_kernel(count, q_ref, k_ref, v_ref, g_ref, p_ref, qo_ref, ko_ref, vo_ref, sum_ref):
@@ -550,14 +596,13 @@
     )[0]
 
 
-def gate_kernel(pieces, a_ref, *refs):
-    both = refs[:pieces]
-    hid_ref, one_ref, two_ref = refs[pieces:]
-    units, cols = hid_ref.shape[1], both[0].shape[1]
+def gate_kernel(a_ref, gate_ref, up_ref, hid_ref, one_ref, two_ref):
+    units, cols = hid_ref.shape[1], gate_ref.shape[1]
     gate = up = None
-    for k in range(pieces):
+    for k in range(a_ref.shape[1] // cols):
         part = a_ref[:, k * cols : (k + 1) * cols]
-        g, u = dot_nt(part, both[k][:units]), dot_nt(part, both[k][units:])
+        g = dot_nt(part, gate_ref[k * units : (k + 1) * units])
+        u = dot_nt(part, up_ref[k * units : (k + 1) * units])
         gate = g if gate is None else gate + g
         up = u if up is None else up + u
     sigmoid = jax.nn.sigmoid(gate)
@@ -567,57 +612,92 @@
     two_ref[...] = active
 
 
-def gate_up(a2, both, block):
+def gate_up(a2, gate, up, units, block):
     rows, width = a2.shape
-    cols = both[0].shape[0] // 2
     moving = lambda i: (i, 0)
-    out = pl.BlockSpec((block, cols), moving)
-    return run(
-        functools.partial(gate_kernel, len(both)),
-        [a2] + both,
-        [shape_of((rows, cols), BF), shape_of((rows, cols), F32), shape_of((rows, cols), F32)],
-        [pl.BlockSpec((block, width), moving)]
-        + [pl.BlockSpec(w.shape, lambda i: (0, 0)) for w in both],
+    out = pl.BlockSpec((block, units), moving)
+    return run(
+        gate_kernel,
+        [a2, gate, up],
+        [shape_of((rows, units), BF), shape_of((rows, units), F32), shape_of((rows, units), F32)],
+        [pl.BlockSpec((block, width), moving)] + [pl.BlockSpec(gate.shape, lambda i: (0, 0))] * 2,
         [out, out, out],
         (rows // block,),
         vmem=48,
-        flops=4 * rows * width * cols,
-    )
-
-
-def hidden_kernel(pieces, g_ref, one_ref, two_ref, *refs):
-    downs, both = refs[:pieces], refs[pieces : 2 * pieces]
-    dboth_ref, out_ref = refs[2 * pieces :]
-    units, cols = downs[0].shape
+    )
+
+
+def hidden_kernel(g_ref, one_ref, two_ref, down_ref, gate_ref, up_ref, dboth_ref, out_ref):
+    units, cols = one_ref.shape[1], down_ref.shape[1]
+    pieces = g_ref.shape[1] // cols
     total = None
     for k in range(pieces):
-        term = dot_nt(g_ref[:, k * cols : (k + 1) * cols], downs[k][...])
+        term = dot_nt(g_ref[:, k * cols : (k + 1) * cols], down_ref[k * units : (k + 1) * units])
         total = term if total is None else total + term
     dgate = (total * one_ref[...]).astype(BF)
     dup = (total * two_ref[...]).astype(BF)
     dboth_ref[:, :units] = dgate
     dboth_ref[:, units:] = dup
     for k in range(pieces):
-        part = dot(dgate, both[k][:units]) + dot(dup, both[k][units:])
+        part = dot(dgate, gate_ref[k * units : (k + 1) * units])
+        part = part + dot(dup, up_ref[k * units : (k + 1) * units])
         out_ref[:, k * cols : (k + 1) * cols] = part.astype(BF)
 
 
-def hidden_back(gb, one, two, downs, both, block):
+def hidden_back(gb, one, two, down, gate, up, block):
     rows, width = gb.shape
-    cols = downs[0].shape[0]
+    units = one.shape[1]
     moving = lambda i: (i, 0)
-    thin = pl.BlockSpec((block, cols), moving)
+    fixed = lambda i: (0, 0)
+    thin = pl.BlockSpec((block, units), moving)
     full = pl.BlockSpec((block, width), moving)
     return run(
-        functools.partial(hidden_kernel, len(downs)),
-        [gb, one, two] + downs + both,
-        [shape_of((rows, 2 * cols), BF), shape_of((rows, width), BF)],
-        [full, thin, thin] + [pl.BlockSpec(w.shape, lambda i: (0, 0)) for w in downs + both],
-        [pl.BlockSpec((block, 2 * cols), moving), full],
+        hidden_kernel,
+        [gb, one, two, down, gate, up],
+        [shape_of((rows, 2 * units), BF), shape_of((rows, width), BF)],
+        [full, thin, thin] + [pl.BlockSpec(down.shape, fixed)] * 3,
+        [pl.BlockSpec((block, 2 * units), moving), full],
         (rows // block,),
         vmem=56,
-        flops=6 * rows * width * cols,
-    )
+    )
+
+
+def result_rows_kernel(h_ref, down_ref, out_ref):
+    units, cols = h_ref.shape[1], down_ref.shape[1]
+    for k in range(out_ref.shape[1] // cols):
+        part = dot(h_ref[...], down_ref[k * units : (k + 1) * units])
+        out_ref[:, k * cols : (k + 1) * cols] = part.astype(BF)
+
+
+def result_rows(hidden, down, width, block):
+    rows, units = hidden.shape
+    moving = lambda i: (i, 0)
+    return run(
+        result_rows_kernel,
+        [hidden, down],
+        [shape_of((rows, width), BF)],
+        [pl.BlockSpec((block, units), moving), pl.BlockSpec(down.shape, lambda i: (0, 0))],
+        [pl.BlockSpec((block, width), moving)],
+        (rows // block,),
+    )[0]
+
+
+def weight_grad_kernel(left_ref, right_ref, out_ref):
+    out_ref[...] = dot_tn(left_ref[...], right_ref[...]).astype(BF)
+
+
+def weight_grad(left, right, pieces):
+    rows, units = left.shape
+    cols = right.shape[1] // pieces
+    return run(
+        weight_grad_kernel,
+        [left, right],
+        [shape_of((pieces * units, cols), BF)],
+        [pl.BlockSpec((rows, units), lambda i: (0, 0)), pl.BlockSpec((rows, cols), lambda i: (0, i))],
+        [pl.BlockSpec((units, cols), lambda i: (i, 0))],
+        (pieces,),
+        vmem=48,
+    )[0]
 
 
 def gather_rows(value, bits, what):
@@ -627,20 +707,21 @@
     return acc
 
 
-def reduce_rows(acc, bits, what):
+def reduce_rows(acc, bits, what, last_after=()):
     for bit in list(reversed(bits))[:-1]:
         half = acc.shape[0] // 2
         got = bit.swap(acc[half:], what)
         acc = (acc[:half].astype(F32) + got.astype(F32)).astype(BF)
     half = acc.shape[0] // 2
-    return acc[:half], bits[0].swap(acc[half:], what)
-
-
-def gather_team(value, bit_x, near, bit_core, what):
+    last = after(acc[half:], *last_after) if last_after else acc[half:]
+    return acc[:half], bits[0].swap(last, what)
+
+
+def gather_team(value, bit_x, near, bit_core, what, marks):
     half = value.shape[0] // 2
     by_x, by_near = bit_x.swap(value, what), near.swap(value, what)
     diagonal = [bit_x.swap(by_near[:half], what), near.swap(by_x[half:], what)]
-    four = jnp.concatenate([value, by_x, by_near] + diagonal, 0)
+    four = after(jnp.concatenate([value, by_x, by_near] + diagonal, 0), *marks)
     return jnp.concatenate([four, bit_core.swap(four, what)], 0)
 
 
@@ -663,7 +744,7 @@
     got_x = near.swap(second, what)
     by_near = jnp.concatenate([add_low(by_near[: rows // 2], got_near), by_near[rows // 2 :]], 0)
     by_x = jnp.concatenate([by_x[: rows // 2], add_low(by_x[rows // 2 :], got_x)], 0)
-    return add_low(own, bit_x.swap(by_x, what)), near.swap(by_near, what)
+    return (add_low(own, bit_x.swap(by_x, what)), near.swap(by_near, what)), by_x
 
 
 def absolute(blocks, index, bits):
@@ -705,12 +786,12 @@
 
     bit_x, bit_core = Bit("dp", 1, dp), Bit("dp", 0, dp)
     ctx_bits = [Bit("ctx", b, ctx) for b in reversed(range(ctx.bit_length() - 1))]
-    near = ctx_bits[-2]
+    near = ctx_bits[-1]
     far = [b for b in ctx_bits if b is not near]
     dp_bits = [bit_x, bit_core]
     names = dp_bits + ctx_bits
-    attn_order = Order(names, list(reversed(ctx_bits)), dp_bits, depth)
-    mlp_order = Order(names, far, dp_bits + [near], depth)
+    attn_order = Order(names, list(reversed(ctx_bits)) + dp_bits, ctx_bits, depth)
+    mlp_order = Order(names, far + dp_bits + [near], [], depth)
     x = tokens.reshape(rows, width)
     cot = cotangent.reshape(rows, width)
     gain_one = attn_gain.astype(F32)[:, None]
@@ -727,59 +808,66 @@
             parts, ("dp", "ctx"), 0, 0, axis_index_groups=team_groups, tiled=True
         )
 
-    def mlp_slices(weights, gain):
+    def mlp_slices(weights, gain, *marks):
         kinds = len(weights)
-        parts = mlp_trade(pack(weights, gain, team)).reshape(team, kinds, depth, -1)
-        return parts.transpose(1, 3, 0, 2).reshape(-1, team * depth)
+        parts = after(mlp_trade(pack(weights, gain, team)), *marks)
+        shape = (parts.shape[2], team * depth)
+        return run(functools.partial(columns_kernel, kinds), [parts], [shape_of(shape, BF)] * kinds)
 
     def mlp_rows(sums, kinds):
-        parts = sums.reshape(kinds, -1, team, depth).transpose(2, 0, 3, 1)
-        return mlp_trade(parts.reshape(team, kinds * depth, -1))
-
-    digits = [sum(((k >> i) & 1) << (len(far) - 1 - i) for i in range(len(far))) for k in range(1 << len(far))]
+        shape = (team, kinds * depth, sums[0].shape[0] // kinds)
+        return mlp_trade(run(functools.partial(rows_kernel, kinds, depth), sums, [shape_of(shape, BF)])[0])
+
+    far_groups = []
+    for n in range(2):
+        far_groups.append([c for c in range(ctx) if (c >> near.bit) & 1 == n])
+    pieces = ctx // 2
+
+    def far_gather(own):
+        return lax.all_gather(own, "ctx", axis=0, tiled=True, axis_index_groups=far_groups)
+
+    def far_reduce(terms):
+        return lax.psum_scatter(
+            terms, "ctx", scatter_dimension=0, tiled=True, axis_index_groups=far_groups
+        )
 
     qkv_cols = HEAD_COLS + 2 * HEAD_DIM
+    me = lax.axis_index("dp").astype(jnp.int32).reshape(1)
+    slices = run(
+        functools.partial(pack_qkv_kernel, dp),
+        [me, query_weight, key_weight, value_weight],
+        [shape_of((dp, depth, qkv_cols), BF)],
+        [SMEM] + [pl.BlockSpec(memory_space=pltpu.VMEM)] * 3,
+    )[0]
+    out_acc = [output_weight]
+    for bit in ctx_bits[:-1]:
+        out_acc.append(jnp.concatenate([out_acc[-1], bit.swap(out_acc[-1], "out")], 0))
+    slices = [slices[0]] + [swap_difference(slices[r], "dp", dp, r, "slice") for r in range(1, dp)]
     own = run(
-        functools.partial(pack_qkv_kernel, dp),
-        [query_weight, key_weight, value_weight],
+        functools.partial(place_kernel, dp),
+        [me, after(slices[0], out_acc[1])] + slices[1:],
         [shape_of((dp, depth, qkv_cols), BF)],
-    )[0]
-    own = lax.all_to_all(own, "dp", 0, 0, tiled=True).reshape(dp * depth, qkv_cols)
-    both_own = mlp_slices([after(gate_weight, own), up_weight], gain_two)
-    gain_all = jnp.broadcast_to(after(attn_gain, both_own)[None], (dp * ctx, depth))
+        [SMEM] + [pl.BlockSpec(memory_space=pltpu.VMEM)] * dp,
+    )[0].reshape(dp * depth, qkv_cols)
+    halves = [own]
+    for i, bit in enumerate(ctx_bits[:-1]):
+        sent = halves[-1] if i == 0 else after(halves[-1], out_acc[i + 1])
+        halves.append(jnp.concatenate([sent, bit.swap(sent, "qkv")], 0))
+    qkv = [halves[-1], ctx_bits[-1].swap(halves[-1], "qkv")]
+    out_rel = after(out_acc[-1], qkv[1])
+    out_rel = jnp.concatenate([out_rel, ctx_bits[-1].swap(out_rel, "out")], 0)
+    out_full = absolute(out_rel.reshape(ctx, depth, width), c_index, ctx_bits)
+    out_full = out_full.reshape(ctx * depth, width)
+
+    gain_all = jnp.broadcast_to(after(attn_gain, own)[None], (dp * ctx, depth))
     gain_all = lax.all_to_all(gain_all, ("dp", "ctx"), 0, 0, tiled=True)
     gain_all = gain_all.reshape(1, width).astype(F32)
-    down_own = mlp_slices([after(down_weight.T, gain_all)], None)
-    half = own
-    for bit in ctx_bits[:-1]:
-        half = jnp.concatenate([half, bit.swap(half, "qkv")], 0)
-    qkv = [half, ctx_bits[-1].swap(half, "qkv")]
-    out_bits = ctx_bits[:-2] + [ctx_bits[-1], near]
-    out_rel = output_weight
-    for i, bit in enumerate(out_bits):
-        if bit is near:
-            out_rel = after(out_rel, down_own)
-        out_rel = jnp.concatenate([out_rel, bit.swap(out_rel, "out")], 0)
-    out_full = absolute(out_rel.reshape(ctx, depth, width), c_index, out_bits)
-    out_full = out_full.reshape(ctx * depth, width)
-
-    def mlp_parts(own, marks, what):
-        parts = [own]
-        for i, bit in enumerate(far):
-            sent = []
-            for k, p in enumerate(parts):
-                mark = marks.get((min(i, 1), min(k, 1)))
-                sent.append(p if mark is None else after(p, mark))
-            parts = parts + [bit.swap(p, what) for p in sent]
-        return parts
-
-    both = mlp_parts(both_own, {}, "both")
-    downs = mlp_parts(down_own, {(0, 0): both[1]}, "down")
-    pieces = len(both)
-    piece = width // pieces
-
-    def by_digit(parts):
-        return [parts[digits.index(k)] for k in range(pieces)]
+    a1_half = gather_rows(norm_to(attn_order, x, gain_all), dp_bits[:1], "a1")
+    a1 = gather_rows(a1_half, dp_bits[1:], "a1")
+    gate_own, up_own = mlp_slices([after(gate_weight, halves[1]), up_weight], gain_two, halves[-1], a1_half)
+    gate = far_gather(gate_own)
+    (down_own,) = mlp_slices([after(down_weight.T, gate_own)], None)
+    units = down_own.shape[0]
 
     places = jnp.arange(seq_dev, dtype=jnp.int32)
     half_dim = HEAD_DIM // 2
@@ -792,54 +880,54 @@
     others = sum(((rel >> i) & 1) << b.bit for i, b in enumerate(ctx_bits)) ^ c_index
     key_places = (((others - c_index) * seq_dev)[:, None] + places[None, :]).reshape(1, -1)
 
-    a1 = gather_rows(norm_to(attn_order, x, gain_all), dp_bits, "a1")
-    queries, kv_own = project(after(a1, down_own), cosine, sine, qkv)
+    queries, kv_own = project(a1, cosine, sine, qkv)
     all_seqs = dp * seqs
     kv = kv_own
-    for bit in ctx_bits:
+    for i, bit in enumerate(ctx_bits):
+        if i == 1:
+            kv = after(kv, down_own)
+        if i == len(ctx_bits) - 1:
+            up = far_gather(after(up_own, kv))
+            down = far_gather(after(down_own, kv))
         kv = jnp.concatenate([kv, bit.swap(kv, "kv")], 0)
-    gb = order_to(mlp_order, after(cot, kv))
-    gb = gather_team(gb, bit_x, near, bit_core, "gb")
+    gb = gather_team(order_to(mlp_order, after(cot, qkv[1])), bit_x, near, bit_core, "gb", [])
     kv = kv.reshape(ctx, all_seqs, seq_dev, 2 * HEAD_DIM)
-    heads = attend(queries, kv, key_places, seq_dev)
-    branch = dot(after(heads, both[1]), out_full).astype(BF)
+    heads = attend(queries, after(kv, gb), key_places, seq_dev)
+    branch = dot(heads, out_full).astype(BF)
     branch = reduce_rows(branch, dp_bits, "branch")
-    middle, a2 = middle_to(mlp_order, after(x, both[2]), *branch)
-
-    a2 = gather_team(a2, bit_x, near, bit_core, "a2")
+    middle, a2 = middle_to(mlp_order, x, *branch)
+
+    a2 = gather_team(a2, bit_x, near, bit_core, "a2", [])
     block = min(256, a2.shape[0])
-    both, downs = by_digit(both), by_digit(downs)
-    hidden, one, two = gate_up(a2, both, block)
-    dboth, da2 = hidden_back(gb, one, two, downs, both, block)
+    hidden, one, two = gate_up(a2, gate, up, units, block)
+    down_back = far_reduce(weight_grad(hidden, gb, pieces))
+    dboth, da2 = hidden_back(gb, one, two, down, gate, up, block)
     half = da2.shape[0] // 2
     da2_got = bit_core.swap(da2[half:], "da2")
-    da2_two = reduce_four(da2[:half], da2_got, bit_x, near, "da2")
+    da2_two, da2_mark = reduce_four(da2[:half], da2_got, bit_x, near, "da2")
+    both_back = far_reduce(weight_grad(dboth, after(a2, da2_mark), pieces))
     grad_middle, db = norm_back(mlp_order, middle, cot, *da2_two, low=True)
     grad_branch = gather_rows(db, dp_bits, "db")
-    down_out = wide(dot, after(hidden, grad_branch), downs, width, block)
-    result = reduce_team(down_out, bit_x, near, bit_core, "result")
-    result = result_of(mlp_order, middle, *result)
 
     grad_heads = dot_nt(grad_branch, out_full)
     dq, dkv = attend_back(
         queries, kv, key_places, grad_heads, cosine[:, :HEAD_COLS], sine[:, :HEAD_COLS], seq_dev
     )
 
-    def mlp_return(left, right, kinds, what):
-        terms = []
-        for k in range(pieces):
-            one = left if k == pieces - 1 else after(left, da2_got)
-            terms.append(dot_tn(right, one[:, k * piece : (k + 1) * piece]).astype(BF))
-        terms = [terms[digits[k]] for k in range(pieces)]
-        for bit in reversed(far):
-            half = len(terms) // 2
-            got = [bit.swap(s, what) for s in terms[half:]]
-            terms = [add_low(after(t, dq) if k == 0 else t, got[k]) for k, t in enumerate(terms[:half])]
-        return mlp_rows(terms[0], kinds)
-
-    both_back = mlp_return(a2, dboth, 2, "dboth")
-    down_back = mlp_return(gb, hidden, 1, "ddown")
-    dkv_two = reduce_rows(dkv.reshape(-1, 2 * HEAD_DIM), ctx_bits, "dkv")
+    dkv_steps = []
+    acc = dkv.reshape(-1, 2 * HEAD_DIM)
+    for bit in reversed(ctx_bits):
+        half = acc.shape[0] // 2
+        dkv_steps.append((acc[:half], bit.swap(acc[half:], "dkv")))
+        acc = add_low(*dkv_steps[-1])
+    dkv_two = dkv_steps[-1]
+    dkv_first, dkv_last = dkv_steps[0][1], dkv_steps[-1][1]
+
+    down_back = mlp_rows([after(down_back, dq)], 1)
+    down_out = result_rows(after(hidden, dq), down, width, block)
+    result_two = reduce_team(down_out, bit_x, near, bit_core, "result")[0]
+    result = result_of(mlp_order, middle, *result_two)
+    both_back = mlp_rows([after(both_back, dkv_last, *result_two)], 2)
     dkv_low = run(
         functools.partial(turn_back_kernel, all_seqs),
         list(dkv_two) + [cosine[:, HEAD_COLS:], sine[:, HEAD_COLS:]],
@@ -847,14 +935,17 @@
     )[0]
     draw = jnp.concatenate([dq, dkv_low], -1)
     da1 = wide(dot_nt, draw, qkv, width, min(256, dp * rows))
-    (grad_tokens,) = norm_back(attn_order, x, grad_middle, *reduce_rows(da1, dp_bits, "da1"), gain_all)
-    q_total = add_low(*reduce_rows(dot_tn(a1, dq).astype(BF), ctx_bits, "dq_w"))
-    kv_total = add_low(*reduce_rows(dot_tn(a1, dkv_low).astype(BF), ctx_bits, "dkv_w"))
+    da1_two = reduce_rows(da1, dp_bits, "da1")
+    (grad_tokens,) = norm_back(attn_order, x, grad_middle, *da1_two, gain_all)
+    q_total = add_low(*reduce_rows(dot_tn(a1, dq).astype(BF), ctx_bits, "dq_w", [down_back]))
+    kv_total = add_low(*reduce_rows(
+        dot_tn(a1, dkv_low).astype(BF), ctx_bits, "dkv_w", [*da1_two]
+    ))
+    out_total = dot_tn(heads, grad_branch).astype(BF).reshape(ctx, depth, width)
+    out_total = relative(after(out_total, dkv_steps[1][1]), c_index, ctx_bits).reshape(ctx * depth, width)
+    out_two = reduce_rows(out_total, ctx_bits, "dout_w")
     qkv_total = jnp.concatenate([q_total, kv_total], -1).reshape(dp, depth, qkv_cols)
     qkv_back = lax.all_to_all(qkv_total, "dp", 0, 0, tiled=True)
-    out_total = dot_tn(heads, grad_branch).astype(BF).reshape(ctx, depth, width)
-    out_total = relative(out_total, c_index, out_bits).reshape(ctx * depth, width)
-    out_two = reduce_rows(out_total, out_bits, "dout_w")
     output_grad = out_two[0].astype(F32) + out_two[1].astype(F32)
 
     gate_grad, up_grad, mlp_sum = unpack(both_back, [gate_weight, up_weight], gain_two)

time: 642 us -> 564 us (0.88)
  waiting for transfers between devices: 318 us -> 267 us
  local copies, waits for them, and re-layouts: 89.5 us -> 58.5 us
  matrix products: 30.6 us -> 8.04 us
  Pallas kernels: 74.3 us -> 90.1 us
  between operations: 2.4 us -> 15.9 us
    ppermute x61 -> x49, waiting for transfers between devices: 277 us -> 251 us  [swap(): return lax.ppermute(value, self.axis, self.pairs)]
    all_to_all x4, waiting for transfers between devices: 22.7 us -> 0.01 us  [mlp_trade(): lax.all_to_all(parts, ('dp', 'ctx'), 0, 0, axis_index_groups=team_groups,...]
    dot_general x11 -> x3, matrix products: 28.1 us -> 5.51 us  [dot_tn(): lax.dot_general(left, right, (((0,), (0,)), ((), ())), preferred_element_...]
    pallas_call x20 -> x27, Pallas kernels: 74.3 us -> 90.1 us  [run(): pl.pallas_call(kernel, name=name, out_shape=list(outs), in_specs=specs or...]
    reshape x5 -> x0, local copies, waits for them, and re-layouts: 15.4 us -> none  [the longest x3 7.78 us: mlp_slices(): return parts.transpose(1, 3, 0, 2).reshape(-1, team * depth)]
    all_gather x0 -> x3, waiting for transfers between devices: none -> 10.7 us  [far_gather(): lax.all_gather(own, 'ctx', axis=0, tiled=True, axis_index_groups=far_groups)]
    all_to_all x1 -> x0, waiting for transfers between devices: 6.55 us -> none  [shards(): lax.all_to_all(own, 'dp', 0, 0, tiled=True).reshape(dp * depth, qkv_cols)]
    convert_element_type x12 -> x10, other arithmetic: 13.6 us -> 7.98 us  [add_low(): return (a.astype(F32) + b.astype(F32)).astype(BF)]
  transfers between devices with their start and end apart: 68 -> 63, of which waited for: 38 -> 32; matrix products, arithmetic and copies ran while one was open for 22% -> 14% of each run, Pallas kernels for 9% -> 15%
where the time goes in v3:
time: 564 us; the launch traced here: 554 us
  waiting for transfers between devices  267 us (47%)
  Pallas kernels  90.1 us (16%)
  starting transfers between devices  75.5 us (13%)
  local copies, waits for them, and re-layouts  58.5 us (10%)
  other arithmetic  39.4 us (7%)
  between operations  15.9 us (3%)
  matrix products  8.04 us (1%)
    ppermute x49, waiting for transfers between devices, swap(): return lax.ppermute(value, self.axis, self.pairs)  251 us
    pallas_call x27, Pallas kernels, run(): pl.pallas_call(kernel, name=name, out_shape=list(outs), in_specs=specs or...  90.1 us
    ppermute x49, starting transfers between devices, swap(): return lax.ppermute(value, self.axis, self.pairs)  49.6 us
    unnamed x201, local copies, waits for them, and re-layouts  30.7 us
    all_to_all x4, starting transfers between devices, mlp_trade(): lax.all_to_all(parts, ('dp', 'ctx'), 0, 0, axis_index_groups=team_groups,...  16.7 us
  transfers between devices with their start and end apart: 63, of which 32 were waited for; matrix products, arithmetic and copies ran while one was open for 14% of the time, Pallas kernels for 15%

profile of v3, /device:TPU:0, one launch (start us, length us, event | category | flops | bytes accessed | tf_op | source)
XLA Modules:
  0.0 554.2 jit_solution(11200129098144550891)
XLA Ops:
  17.7 5.8 %collective-permute-done = bf16[64,2048]{1,0:T(8,128)(2,1)S(1)} collective-permute-done((bf16[64,2048]{1,0:T(8,128)(2,1)}, bf16[64,2048]{1,0:T(8,128)(2,1)S(1)}, u32[]{:S(2)}, u32[]{:S(2)}) %collective-permute-start) | collective-permute-done | bytes 262176 | tf_op jit(solution)/shard_map/out_ctx2/ppermute | solution.py:73
  32.0 9.3 %collective-permute-done.6 = bf16[256,640]{1,0:T(8,128)(2,1)S(1)} collective-permute-done((bf16[256,640]{1,0:T(8,128)(2,1)S(1)}, bf16[256,640]{1,0:T(8,128)(2,1)S(1)}, u32[]{:S(2)}, u32[]{:S(2)}) %collective-permute-start.6) | collective-permute-done | bytes 327712 | tf_op jit(solution)/shard_map/qkv_ctx2/ppermute | solution.py:73
  44.3 4.8 all-to-all-done
  49.1 4.3 all-to-all-start.1
  59.5 23.8 %collective-permute-done.4 = bf16[128,2048]{1,0:T(8,128)(2,1)S(1)} collective-permute-done((bf16[128,2048]{1,0:T(8,128)(2,1)S(1)}, bf16[128,2048]{1,0:T(8,128)(2,1)S(1)}, u32[]{:S(2)}, u32[]{:S(2)}) %collective-permute-start.4) | collective-permute-done | bytes 524320 | tf_op jit(solution)/shard_map/a1_dp1/ppermute | solution.py:73
  92.8 4.2 all-to-all-start.2
  101.5 23.5 %collective-permute-done.9.refs_4_.refs_1_ = bf16[1024,640]{1,0:T(8,128)(2,1)S(1)} collective-permute-done((bf16[1024,640]{1,0:T(8,128)(2,1)S(1)}, bf16[1024,640]{1,0:T(8,128)(2,1)S(1)}, u32[]{:S(2)}, u32[]{:S(2)}) %collective-permute-start.9) | collective-permute-done | bytes 1310752 | tf_op jit(solution)/shard_map/qkv_ctx0/ppermute | solution.py:73
  136.5 9.4 %collective-permute-done.10 = bf16[512,128]{1,0:T(8,128)(2,1)S(1)} collective-permute-done((bf16[512,128]{1,0:T(8,128)(2,1)}, bf16[512,128]{1,0:T(8,128)(2,1)S(1)}, u32[]{:S(2)}, u32[]{:S(2)}) %collective-permute-start.10) | collective-permute-done | bytes 131104 | tf_op jit(solution)/shard_map/kv_ctx2/ppermute | solution.py:73
  147.8 10.0 %collective-permute-done.11 = bf16[1024,128]{1,0:T(8,128)(2,1)S(1)} collective-permute-done((bf16[1024,128]{1,0:T(8,128)(2,1)S(1)}, bf16[1024,128]{1,0:T(8,128)(2,1)S(1)}, u32[]{:S(2)}, u32[]{:S(2)}) %collective-permute-start.11) | collective-permute-done | bytes 262176 | tf_op jit(solution)/shard_map/kv_ctx1/ppermute | solution.py:73
  169.9 16.5 %collective-permute-done.16 = bf16[64,2048]{1,0:T(8,128)(2,1)S(1)} collective-permute-done((bf16[64,2048]{1,0:T(8,128)(2,1)S(1)}, bf16[64,2048]{1,0:T(8,128)(2,1)S(1)}, u32[]{:S(2)}, u32[]{:S(2)}) %collective-permute-start.16) | collective-permute-done | bytes 262176 | tf_op jit(solution)/shard_map/gb_ctx0/ppermute | solution.py:73
  193.3 5.2 attend_kernel.1
  205.1 12.1 %collective-permute-done.20.b_ref = bf16[128,2048]{1,0:T(8,128)(2,1)S(1)} collective-permute-done((bf16[128,2048]{1,0:T(8,128)(2,1)S(1)}, bf16[128,2048]{1,0:T(8,128)(2,1)S(1)}, u32[]{:S(2)}, u32[]{:S(2)}) %collective-permute-start.20) | collective-permute-done | bytes 524320 | tf_op jit(solution)/shard_map/branch_dp1/ppermute | solution.py:73
  221.5 10.1 %collective-permute-done.22 = bf16[128,2048]{1,0:T(8,128)(2,1)S(1)} collective-permute-done((bf16[128,2048]{1,0:T(8,128)(2,1)S(1)}, bf16[128,2048]{1,0:T(8,128)(2,1)S(1)}, u32[]{:S(2)}, u32[]{:S(2)}) %collective-permute-start.22) | collective-permute-done | bytes 524320 | tf_op jit(solution)/shard_map/a2_ctx0/ppermute | solution.py:73
  240.0 4.1 collective-permute-done.25
  248.6 10.7 %gate_kernel.1 = (bf16[1024,704]{1,0:T(8,128)(2,1)S(1)}, f32[1024,704]{1,0:T(8,128)}, f32[1024,704]{1,0:T(8,128)}) custom-call(bf16[1024,2048]{1,0:T(8,128)(2,1)} %pad_maximum_fusion.1.a_ref.right_ref, bf16[2816,512]{1,0:T(8,128)(2,1)S(1)} %copy-done.2, bf16[2816,512]{1,0:T(8,128)(2,1)} %all-gather.6.cloned.1.call-done.up_ref), custom_call_target="tpu_custom_call" | custom-call | tf_op jit(solution)/shard_map/gate_kernel/pallas_call | solution.py:47
  259.3 6.5 %weight_grad_kernel.2 = bf16[2816,512]{1,0:T(8,128)(2,1)} custom-call(bf16[1024,704]{1,0:T(8,128)(2,1)S(1)} %get-tuple-element.76.h_ref.left_ref, bf16[1024,2048]{1,0:T(8,128)(2,1)} %pad_maximum_fusion.g_ref.right_ref), custom_call_target="tpu_custom_call" | custom-call | tf_op jit(solution)/shard_map/weight_grad_kernel/pallas_call | solution.py:47
  267.1 10.7 %all-gather.8.cloned.1.call-done.down_ref = bf16[2816,512]{1,0:T(8,128)(2,1)} async-done(((bf16[704,512]{1,0:T(8,128)(2,1)}), bf16[2816,512]{1,0:T(8,128)(2,1)}) %all-gather.8.cloned.1.call-update) | async-done | bytes 2883600 | tf_op jit(solution)/shard_map/all_gather | solution.py:827
  277.8 16.4 %hidden_kernel.1 = (bf16[1024,1408]{1,0:T(8,128)(2,1)}, bf16[1024,2048]{1,0:T(8,128)(2,1)}) custom-call(bf16[1024,2048]{1,0:T(8,128)(2,1)} %pad_maximum_fusion.g_ref.right_ref, f32[1024,704]{1,0:T(8,128)} %get-tuple-element.70.one_ref, f32[1024,704]{1,0:T(8,128)} %get-tuple-element.71.two_ref, bf16[2816,512]{1,0:T(8,128)(2,1)} %all-gather.8.cloned.1.call-done.down_ref, ...), custom_call_target="tpu_custom_call" | custom-call | tf_op jit(solution)/shard_map/hidden_kernel/pallas_call | solution.py:47
  296.1 4.1 collective-permute-done.26
  304.3 5.4 collective-permute-done.29
  314.8 9.3 %weight_grad_kernel.3 = bf16[5632,512]{1,0:T(8,128)(2,1)} custom-call(bf16[1024,1408]{1,0:T(8,128)(2,1)S(1)} %copy-done.18, bf16[1024,2048]{1,0:T(8,128)(2,1)} %pad_maximum_fusion.1.a_ref.right_ref), custom_call_target="tpu_custom_call" | custom-call | tf_op jit(solution)/shard_map/weight_grad_kernel/pallas_call | solution.py:47
  329.9 10.8 %collective-permute-done.31 = bf16[128,2048]{1,0:T(8,128)(2,1)S(1)} collective-permute-done((bf16[128,2048]{1,0:T(8,128)(2,1)S(1)}, bf16[128,2048]{1,0:T(8,128)(2,1)S(1)}, u32[]{:S(2)}, u32[]{:S(2)}) %collective-permute-start.31) | collective-permute-done | bytes 524320 | tf_op jit(solution)/shard_map/db_dp1/ppermute | solution.py:73
  347.5 11.5 %attend_back_kernel.1 = (bf16[512,512]{1,0:T(8,128)(2,1)S(1)}, bf16[8,8,64,128]{3,2,1,0:T(8,128)(2,1)S(1)}) custom-call(bf16[512,512]{1,0:T(8,128)(2,1)S(1)} %copy-done.25, bf16[8,8,64,128]{3,2,1,0:T(8,128)(2,1)S(1)} %bitcast.47, s32[1,512]{1,0:T(1,128)S(1)} %add.218.key_ref, f32[512,512]{1,0:T(8,128)S(1)} %fusion.20.do_ref, ...), custom_call_target="tpu_custom_call" | custom-call | tf_op jit(solution)/shard_map/attend_back_kernel/pallas_call | solution.py:47
  363.9 4.1 result_rows_kernel.1
  377.0 20.1 %collective-permute-done.39 = bf16[1024,128]{1,0:T(8,128)(2,1)S(1)} collective-permute-done((bf16[1024,128]{1,0:T(8,128)(2,1)S(1)}, bf16[1024,128]{1,0:T(8,128)(2,1)S(1)}, u32[]{:S(2)}, u32[]{:S(2)}) %collective-permute-start.39) | collective-permute-done | bytes 262176 | tf_op jit(solution)/shard_map/dkv_ctx1/ppermute | solution.py:73
  400.0 15.3 %collective-permute-done.40.b_ref = bf16[512,128]{1,0:T(8,128)(2,1)S(1)} collective-permute-done((bf16[512,128]{1,0:T(8,128)(2,1)S(1)}, bf16[512,128]{1,0:T(8,128)(2,1)S(1)}, u32[]{:S(2)}, u32[]{:S(2)}) %collective-permute-start.40) | collective-permute-done | bytes 131104 | tf_op jit(solution)/shard_map/dkv_ctx2/ppermute | solution.py:73
  424.3 5.4 collective-permute-done.46
  437.6 22.5 %collective-permute-done.47 = bf16[512,128]{0,1:T(8,128)(2,1)} collective-permute-done((bf16[512,128]{0,1:T(8,128)(2,1)S(1)}, bf16[512,128]{0,1:T(8,128)(2,1)}, u32[]{:S(2)}, u32[]{:S(2)}) %collective-permute-start.47) | collective-permute-done | bytes 131104 | tf_op jit(solution)/shard_map/dkv_w_ctx1/ppermute | solution.py:73
  476.0 8.4 %collective-permute-done.45 = bf16[256,512]{0,1:T(8,128)(2,1)S(1)} collective-permute-done((bf16[256,512]{0,1:T(8,128)(2,1)}, bf16[256,512]{0,1:T(8,128)(2,1)S(1)}, u32[]{:S(2)}, u32[]{:S(2)}) %collective-permute-start.45) | collective-permute-done | bytes 262176 | tf_op jit(solution)/shard_map/dq_w_ctx2/ppermute | solution.py:73
  486.2 5.8 %collective-permute-done.42.b_ref = bf16[128,2048]{1,0:T(8,128)(2,1)S(1)} collective-permute-done((bf16[128,2048]{1,0:T(8,128)(2,1)S(1)}, bf16[128,2048]{1,0:T(8,128)(2,1)S(1)}, u32[]{:S(2)}, u32[]{:S(2)}) %collective-permute-start.42) | collective-permute-done | bytes 524320 | tf_op jit(solution)/shard_map/da1_dp1/ppermute | solution.py:73
  512.4 4.7 all-to-all-start.5
  525.0 9.8 %collective-permute-done.51 = bf16[64,2048]{1,0:T(8,128)(2,1)} collective-permute-done((bf16[64,2048]{1,0:T(8,128)(2,1)}, bf16[64,2048]{1,0:T(8,128)(2,1)}, u32[]{:S(2)}, u32[]{:S(2)}) %collective-permute-start.51) | collective-permute-done | bytes 262176 | tf_op jit(solution)/shard_map/dout_w_ctx2/ppermute | solution.py:73
  (430 shorter events, 213.7 us)
Async XLA Ops:
  24.3 17.1 %collective-permute-start.6 = (bf16[256,640]{1,0:T(8,128)(2,1)S(1)}, bf16[256,640]{1,0:T(8,128)(2,1)S(1)}, u32[]{:S(2)}, u32[]{:S(2)}) collective-permute-start(bf16[256,640]{1,0:T(8,128)(2,1)S(1)} %bitcast.53), channel_id=1, source_target_pairs={{0,4},{1,5},{2,6},{3,7},{4,0},{5,1},{6,2},{7,3},{8,12},{9,13},{10,... | collective-permute-start | bytes 983048 | tf_op jit(solution)/shard_map/qkv_ctx2/ppermute | solution.py:73
  24.4 32.6 %collective-permute-start.7 = (bf16[128,2048]{1,0:T(8,128)(2,1)}, bf16[128,2048]{1,0:T(8,128)(2,1)}, u32[]{:S(2)}, u32[]{:S(2)}) collective-permute-start(bf16[128,2048]{1,0:T(8,128)(2,1)} %get-tuple-element.126), channel_id=1, source_target_pairs={{0,2},{1,3},{2,0},{3,1},{4,6},{5,7},{6,4},{7,5},{8,10},{9,11},{10,... | collective-permute-start | bytes 1572872 | tf_op jit(solution)/shard_map/out_ctx1/ppermute | solution.py:73
  29.2 19.9 %all-to-all-start = ((bf16[32,1,64]{2,1,0:T(2,128)(2,1)}), bf16[32,1,64]{2,1,0:T(2,128)(2,1)S(1)}, u32[]{:S(2)}, u32[]{:S(2)}) async-start(bf16[32,1,64]{2,1,0:T(2,128)(2,1)} %broadcast_in_dim.26), calls=%async_computation | async-start | bytes 32768 | tf_op jit(solution)/shard_map/all_to_all | solution.py:863
  49.1 35.4 %all-to-all-start.1 = ((bf16[8,128,704]{1,2,0:T(8,128)(2,1)}), bf16[8,128,704]{1,2,0:T(8,128)(2,1)}, u32[]{:S(2)}, u32[]{:S(2)}) async-start(bf16[8,128,704]{1,2,0:T(8,128)(2,1)} %copy.31), calls=%async_computation.1 | async-start | bytes 2883584 | tf_op jit(solution)/shard_map/all_to_all | solution.py:807
  53.4 193.3 %all-gather.4.cloned.1.call-start = ((), (), s32[]{:S(2)}) async-start(), calls=%async_computation.8 | async-start | bytes 3604480 | tf_op jit(solution)/shard_map/all_gather | solution.py:827
  55.1 28.2 %collective-permute-start.4 = (bf16[128,2048]{1,0:T(8,128)(2,1)S(1)}, bf16[128,2048]{1,0:T(8,128)(2,1)S(1)}, u32[]{:S(2)}, u32[]{:S(2)}) collective-permute-start(bf16[128,2048]{1,0:T(8,128)(2,1)S(1)} %norm_kernel.1), channel_id=1, source_target_pairs={{0,16},{8,24},{16,0},{24,8},{1,17},{9,25},{17,1},{25,9},{2,18},{10... | collective-permute-start | bytes 1572872 | tf_op jit(solution)/shard_map/a1_dp1/ppermute | solution.py:73
  58.9 25.5 %collective-permute-start.8 = (bf16[512,640]{1,0:T(8,128)(2,1)S(1)}, bf16[512,640]{1,0:T(8,128)(2,1)S(1)}, u32[]{:S(2)}, u32[]{:S(2)}) collective-permute-start(bf16[512,640]{1,0:T(8,128)(2,1)S(1)} %copy-done.69), channel_id=1, source_target_pairs={{0,2},{1,3},{2,0},{3,1},{4,6},{5,7},{6,4},{7,5},{8,10},{9,11},{10,... | collective-permute-start | bytes 1966088 | tf_op jit(solution)/shard_map/qkv_ctx1/ppermute | solution.py:73
  89.1 35.9 %collective-permute-start.9 = (bf16[1024,640]{1,0:T(8,128)(2,1)S(1)}, bf16[1024,640]{1,0:T(8,128)(2,1)S(1)}, u32[]{:S(2)}, u32[]{:S(2)}) collective-permute-start(bf16[1024,640]{1,0:T(8,128)(2,1)S(1)} %constant_dynamic-update-slice_fusion.5.refs_3_.refs_0_), channel_id=1, source_target_pairs={{0,1},{1,0},{2,3},{3,2},{4,5},{5,4},{6,7},{7,6},{8,9},{9,8},{10,11... | collective-permute-start | bytes 3932168 | tf_op jit(solution)/shard_map/qkv_ctx0/ppermute | solution.py:73
  92.8 37.3 %all-to-all-start.2 = ((bf16[8,64,704]{2,1,0:T(8,128)(2,1)}), bf16[8,64,704]{2,1,0:T(8,128)(2,1)}, u32[]{:S(2)}, u32[]{:S(2)}) async-start(bf16[8,64,704]{2,1,0:T(8,128)(2,1)} %copy-done.16), calls=%async_computation.2 | async-start | bytes 1572864 | tf_op jit(solution)/shard_map/all_to_all | solution.py:807
  97.1 149.7 %all-gather.6.cloned.1.call-start = ((), (), s32[]{:S(2)}) async-start(), calls=%async_computation.9 | async-start | bytes 3604480 | tf_op jit(solution)/shard_map/all_gather | solution.py:827
  129.3 16.6 %collective-permute-start.10 = (bf16[512,128]{1,0:T(8,128)(2,1)}, bf16[512,128]{1,0:T(8,128)(2,1)S(1)}, u32[]{:S(2)}, u32[]{:S(2)}) collective-permute-start(bf16[512,128]{1,0:T(8,128)(2,1)} %get-tuple-element.56), channel_id=1, source_target_pairs={{0,4},{1,5},{2,6},{3,7},{4,0},{5,1},{6,2},{7,3},{8,12},{9,13},{10,... | collective-permute-start | bytes 393224 | tf_op jit(solution)/shard_map/kv_ctx2/ppermute | solution.py:73
  134.1 29.2 %collective-permute-start.13 = (bf16[128,2048]{1,0:T(8,128)(2,1)S(1)}, bf16[128,2048]{1,0:T(8,128)(2,1)}, u32[]{:S(2)}, u32[]{:S(2)}) collective-permute-start(bf16[128,2048]{1,0:T(8,128)(2,1)S(1)} %order_kernel.1), channel_id=1, source_target_pairs={{0,16},{8,24},{16,0},{24,8},{1,17},{9,25},{17,1},{25,9},{2,18},{10... | collective-permute-start | bytes 1572872 | tf_op jit(solution)/shard_map/gb_dp1/ppermute | solution.py:73
  134.5 26.3 %collective-permute-start.14 = (bf16[128,2048]{1,0:T(8,128)(2,1)S(1)}, bf16[128,2048]{1,0:T(8,128)(2,1)}, u32[]{:S(2)}, u32[]{:S(2)}) collective-permute-start(bf16[128,2048]{1,0:T(8,128)(2,1)S(1)} %order_kernel.1), channel_id=1, source_target_pairs={{0,1},{1,0},{2,3},{3,2},{4,5},{5,4},{6,7},{7,6},{8,9},{9,8},{10,11... | collective-permute-start | bytes 1572872 | tf_op jit(solution)/shard_map/gb_ctx0/ppermute | solution.py:73
  136.2 51.5 %collective-permute-start.18 = (bf16[256,2048]{1,0:T(8,128)(2,1)}, bf16[256,2048]{1,0:T(8,128)(2,1)}, u32[]{:S(2)}, u32[]{:S(2)}) collective-permute-start(bf16[256,2048]{1,0:T(8,128)(2,1)} %constant_dynamic-update-slice_fusion.2), channel_id=1, source_target_pairs={{0,1},{1,0},{2,3},{3,2},{4,5},{5,4},{6,7},{7,6},{8,9},{9,8},{10,11... | collective-permute-start | bytes 3145736 | tf_op jit(solution)/shard_map/out_ctx0/ppermute | solution.py:73
  159.2 27.3 %collective-permute-start.12 = (bf16[2048,128]{1,0:T(8,128)(2,1)}, bf16[2048,128]{1,0:T(8,128)(2,1)}, u32[]{:S(2)}, u32[]{:S(2)}) collective-permute-start(bf16[2048,128]{1,0:T(8,128)(2,1)} %constant_dynamic-update-slice_fusion.7), channel_id=1, source_target_pairs={{0,1},{1,0},{2,3},{3,2},{4,5},{5,4},{6,7},{7,6},{8,9},{9,8},{10,11... | collective-permute-start | bytes 1572872 | tf_op jit(solution)/shard_map/kv_ctx0/ppermute | solution.py:73
  160.7 117.1 %all-gather.8.cloned.1.call-start = ((), (), s32[]{:S(2)}) async-start(), calls=%async_computation.10 | async-start | bytes 3604480 | tf_op jit(solution)/shard_map/all_gather | solution.py:827
  164.3 22.1 %collective-permute-start.16 = (bf16[64,2048]{1,0:T(8,128)(2,1)S(1)}, bf16[64,2048]{1,0:T(8,128)(2,1)S(1)}, u32[]{:S(2)}, u32[]{:S(2)}) collective-permute-start(bf16[64,2048]{1,0:T(8,128)(2,1)S(1)} %slice.255), channel_id=1, source_target_pairs={{0,1},{1,0},{2,3},{3,2},{4,5},{5,4},{6,7},{7,6},{8,9},{9,8},{10,11... | collective-permute-start | bytes 786440 | tf_op jit(solution)/shard_map/gb_ctx0/ppermute | solution.py:73
  204.9 226.8 %reduce-scatter.3.cloned.1.call-start = ((), (), s32[]{:S(2)}) async-start(), calls=%async_computation.11 | async-start | bytes 3604480 | tf_op jit(solution)/shard_map/reduce_scatter | solution.py:830
  267.0 241.9 %reduce-scatter.5.cloned.1.call-start = ((), (), s32[]{:S(2)}) async-start(), calls=%async_computation.12 | async-start | bytes 7208960 | tf_op jit(solution)/shard_map/reduce_scatter | solution.py:830
  370.7 97.7 %collective-permute-start.33 = (bf16[512,2048]{1,0:T(8,128)(2,1)}, bf16[512,2048]{1,0:T(8,128)(2,1)}, u32[]{:S(2)}, u32[]{:S(2)}) collective-permute-start(bf16[512,2048]{1,0:T(8,128)(2,1)} %slice.270), channel_id=1, source_target_pairs={{0,8},{8,0},{16,24},{24,16},{1,9},{9,1},{17,25},{25,17},{2,10},{10... | collective-permute-start | bytes 6291464 | tf_op jit(solution)/shard_map/result_dp0/ppermute | solution.py:73
  373.3 48.8 %collective-permute-start.43 = (bf16[1024,512]{0,1:T(8,128)(2,1)S(1)}, bf16[1024,512]{0,1:T(8,128)(2,1)S(1)}, u32[]{:S(2)}, u32[]{:S(2)}) collective-permute-start(bf16[1024,512]{0,1:T(8,128)(2,1)S(1)} %slice.287), channel_id=1, source_target_pairs={{0,1},{1,0},{2,3},{3,2},{4,5},{5,4},{6,7},{7,6},{8,9},{9,8},{10,11... | collective-permute-start | bytes 3145736 | tf_op jit(solution)/shard_map/dq_w_ctx0/ppermute | solution.py:73
  375.6 21.5 %collective-permute-start.39 = (bf16[1024,128]{1,0:T(8,128)(2,1)S(1)}, bf16[1024,128]{1,0:T(8,128)(2,1)S(1)}, u32[]{:S(2)}, u32[]{:S(2)}) collective-permute-start(bf16[1024,128]{1,0:T(8,128)(2,1)S(1)} %slice.279), channel_id=1, source_target_pairs={{0,2},{1,3},{2,0},{3,1},{4,6},{5,7},{6,4},{7,5},{8,10},{9,11},{10,... | collective-permute-start | bytes 786440 | tf_op jit(solution)/shard_map/dkv_ctx1/ppermute | solution.py:73
  397.2 18.2 %collective-permute-start.40 = (bf16[512,128]{1,0:T(8,128)(2,1)S(1)}, bf16[512,128]{1,0:T(8,128)(2,1)S(1)}, u32[]{:S(2)}, u32[]{:S(2)}) collective-permute-start(bf16[512,128]{1,0:T(8,128)(2,1)S(1)} %get-tuple-element.123), channel_id=1, source_target_pairs={{0,4},{1,5},{2,6},{3,7},{4,0},{5,1},{6,2},{7,3},{8,12},{9,13},{10,... | collective-permute-start | bytes 393224 | tf_op jit(solution)/shard_map/dkv_ctx2/ppermute | solution.py:73
  398.6 65.4 %collective-permute-start.49 = (bf16[256,2048]{1,0:T(8,128)(2,1)}, bf16[256,2048]{1,0:T(8,128)(2,1)}, u32[]{:S(2)}, u32[]{:S(2)}) collective-permute-start(bf16[256,2048]{1,0:T(8,128)(2,1)} %bitcast.24), channel_id=1, source_target_pairs={{0,1},{1,0},{2,3},{3,2},{4,5},{5,4},{6,7},{7,6},{8,9},{9,8},{10,11... | collective-permute-start | bytes 3145736 | tf_op jit(solution)/shard_map/dout_w_ctx0/ppermute | solution.py:73
  418.7 48.0 %collective-permute-start.41 = (bf16[256,2048]{1,0:T(8,128)(2,1)}, bf16[256,2048]{1,0:T(8,128)(2,1)}, u32[]{:S(2)}, u32[]{:S(2)}) collective-permute-start(bf16[256,2048]{1,0:T(8,128)(2,1)} %slice.283), channel_id=1, source_target_pairs={{0,8},{8,0},{16,24},{24,16},{1,9},{9,1},{17,25},{25,17},{2,10},{10... | collective-permute-start | bytes 3145736 | tf_op jit(solution)/shard_map/da1_dp0/ppermute | solution.py:73
  424.3 37.4 %collective-permute-start.44 = (bf16[512,512]{0,1:T(8,128)(2,1)}, bf16[512,512]{0,1:T(8,128)(2,1)}, u32[]{:S(2)}, u32[]{:S(2)}) collective-permute-start(bf16[512,512]{0,1:T(8,128)(2,1)} %slice.289), channel_id=1, source_target_pairs={{0,2},{1,3},{2,0},{3,1},{4,6},{5,7},{6,4},{7,5},{8,10},{9,11},{10,... | collective-permute-start | bytes 1572872 | tf_op jit(solution)/shard_map/dq_w_ctx1/ppermute | solution.py:73
  430.6 29.6 %collective-permute-start.47 = (bf16[512,128]{0,1:T(8,128)(2,1)S(1)}, bf16[512,128]{0,1:T(8,128)(2,1)}, u32[]{:S(2)}, u32[]{:S(2)}) collective-permute-start(bf16[512,128]{0,1:T(8,128)(2,1)S(1)} %slice.295), channel_id=1, source_target_pairs={{0,2},{1,3},{2,0},{3,1},{4,6},{5,7},{6,4},{7,5},{8,10},{9,11},{10,... | collective-permute-start | bytes 393224 | tf_op jit(solution)/shard_map/dkv_w_ctx1/ppermute | solution.py:73
  434.0 32.7 %all-to-all-start.3 = ((bf16[8,64,704]{2,1,0:T(8,128)(2,1)}), bf16[8,64,704]{2,1,0:T(8,128)(2,1)S(1)}, u32[]{:S(2)}, u32[]{:S(2)}) async-start(bf16[8,64,704]{2,1,0:T(8,128)(2,1)} %copy-done.17), calls=%async_computation.4 | async-start | bytes 1572864 | tf_op jit(solution)/shard_map/all_to_all | solution.py:807
  466.8 50.3 %collective-permute-start.50 = (bf16[128,2048]{1,0:T(8,128)(2,1)}, bf16[128,2048]{1,0:T(8,128)(2,1)}, u32[]{:S(2)}, u32[]{:S(2)}) collective-permute-start(bf16[128,2048]{1,0:T(8,128)(2,1)} %slice.299), channel_id=1, source_target_pairs={{0,2},{1,3},{2,0},{3,1},{4,6},{5,7},{6,4},{7,5},{8,10},{9,11},{10,... | collective-permute-start | bytes 1572872 | tf_op jit(solution)/shard_map/dout_w_ctx1/ppermute | solution.py:73
  466.8 17.7 %collective-permute-start.45 = (bf16[256,512]{0,1:T(8,128)(2,1)}, bf16[256,512]{0,1:T(8,128)(2,1)S(1)}, u32[]{:S(2)}, u32[]{:S(2)}) collective-permute-start(bf16[256,512]{0,1:T(8,128)(2,1)} %slice.291), channel_id=1, source_target_pairs={{0,4},{1,5},{2,6},{3,7},{4,0},{5,1},{6,2},{7,3},{8,12},{9,13},{10,... | collective-permute-start | bytes 786440 | tf_op jit(solution)/shard_map/dq_w_ctx2/ppermute | solution.py:73
  484.7 18.4 %collective-permute-start.35 = (bf16[128,2048]{1,0:T(8,128)(2,1)S(1)}, bf16[128,2048]{1,0:T(8,128)(2,1)S(1)}, u32[]{:S(2)}, u32[]{:S(2)}) collective-permute-start(bf16[128,2048]{1,0:T(8,128)(2,1)S(1)} %pad_maximum_fusion.13), channel_id=1, source_target_pairs={{0,16},{8,24},{16,0},{24,8},{1,17},{9,25},{17,1},{25,9},{2,18},{10... | collective-permute-start | bytes 1572872 | tf_op jit(solution)/shard_map/result_dp1/ppermute | solution.py:73
  512.4 28.7 %all-to-all-start.5 = ((bf16[8,128,704]{1,2,0:T(8,128)(2,1)}), bf16[8,128,704]{1,2,0:T(8,128)(2,1)}, u32[]{:S(2)}, u32[]{:S(2)}) async-start(bf16[8,128,704]{1,2,0:T(8,128)(2,1)} %copy.35), calls=%async_computation.7 | async-start | bytes 2883584 | tf_op jit(solution)/shard_map/all_to_all | solution.py:807
  (121 other events, 1065.8 us)
Sparse Core Ops, SparseCore 0:
  89.1 63.4 all-gather.3
  160.8 56.8 all-gather.5
  219.9 57.8 all-gather.7
  279.9 54.8 reduce-scatter.2
  337.0 123.2 reduce-scatter.4

commit v4 on v3

--- a/solution.py
+++ b/solution.py
@@ -354,32 +354,18 @@
     )[0]
 
 
-def unpack_kernel(count, kinds, scaled, *refs):
-    p_ref = refs[0]
-    cols = p_ref.shape[-1]
-    depth = p_ref.shape[1] // kinds
-    outs = refs[-kinds - 1 : -1] if scaled else refs[-kinds:]
+def unpack_kernel(p_ref, gate_ref, up_ref, gain_ref, gate_out, up_out, down_out, sum_ref):
+    count, depth, cols = p_ref.shape
+    depth = depth // 3
     total = jnp.zeros((depth, 1), F32)
-    for m in range(kinds):
-        for t in range(count):
+    for t in range(count):
+        lanes = slice(t * cols, (t + 1) * cols)
+        for m, (w_ref, out_ref) in enumerate([(gate_ref, gate_out), (up_ref, up_out)]):
             part = p_ref[t, m * depth : (m + 1) * depth].astype(F32)
-            lanes = slice(t * cols, (t + 1) * cols)
-            if scaled:
-                total = total + jnp.sum(part * refs[1 + m][:, lanes].astype(F32), -1, keepdims=True)
-                part = part * refs[1 + kinds][...]
-            outs[m][:, lanes] = part
-    if scaled:
-        refs[-1][...] = total
-
-
-def unpack(parts, weights, gain):
-    count, depth, cols = parts.shape
-    if gain is None:
-        outs = [shape_of((depth, count * cols), F32)]
-        return run(functools.partial(unpack_kernel, count, 1, False), [parts], outs)
-    kinds = len(weights)
-    outs = [shape_of((depth // kinds, count * cols), F32)] * kinds + [shape_of((depth // kinds, 1), F32)]
-    return run(functools.partial(unpack_kernel, count, kinds, True), [parts] + weights + [gain], outs)
+            total = total + jnp.sum(part * w_ref[:, lanes].astype(F32), -1, keepdims=True)
+            out_ref[:, lanes] = part * gain_ref[...]
+        down_out[:, lanes] = p_ref[t, 2 * depth :].astype(F32)
+    sum_ref[...] = total
 
 
 def pack_qkv_kernel(count, me_ref, q_ref, k_ref, v_ref, out_ref):
@@ -407,17 +393,20 @@
             outs[m][:, t * depth : (t + step) * depth] = both.T.astype(BF)
 
 
-def rows_kernel(kinds, depth, *refs):
+def rows_kernel(depth, *refs):
     out_ref = refs[-1]
-    count = out_ref.shape[0]
-    units = out_ref.shape[2]
+    count, _, units = out_ref.shape
     step = max(1, 128 // depth)
-    for m in range(kinds):
-        for t in range(0, count, step):
-            lanes = slice(t * depth, (t + step) * depth)
-            both = sum(r[m * units : (m + 1) * units, lanes].astype(F32) for r in refs[:-1]).T
-            for i in range(step):
-                out_ref[t + i, m * depth : (m + 1) * depth] = both[i * depth : (i + 1) * depth].astype(BF)
+    m = 0
+    for ref in refs[:-1]:
+        for first in range(0, ref.shape[0], units):
+            for t in range(0, count, step):
+                lanes = slice(t * depth, (t + step) * depth)
+                both = ref[first : first + units, lanes].astype(F32).T
+                for i in range(step):
+                    rows = both[i * depth : (i + 1) * depth]
+                    out_ref[t + i, m * depth : (m + 1) * depth] = rows.astype(BF)
+            m += 1
 
 
 def unpack_qkv_kernel(count, q_ref, k_ref, v_ref, g_ref, p_ref, qo_ref, ko_ref, vo_ref, sum_ref):
@@ -542,7 +531,8 @@
     for j in range(GROUPS):
         mid_ref[:, j * HEAD_DIM : (j + 1) * HEAD_DIM] = turned[j * seq_dev : (j + 1) * seq_dev]
     whole = mid_ref[...]
-    dq_ref[...] = (whole * cos_ref[...] - swap_halves(whole) * sin_ref[...]).astype(BF)
+    cosine, sine = cos_ref[:, :HEAD_COLS], sin_ref[:, :HEAD_COLS]
+    dq_ref[...] = (whole * cosine - swap_halves(whole) * sine).astype(BF)
     grad_keys = dot_tn(scores, queries) * FACTOR
     grad_values = dot_tn(low, mixed)
     joined = jnp.concatenate([grad_keys, grad_values], -1)
@@ -553,7 +543,7 @@
     rows = queries.shape[0]
     count, seqs = kv.shape[:2]
     own = pl.BlockSpec((seq_dev, HEAD_COLS), lambda s: (s, 0))
-    table = pl.BlockSpec((seq_dev, HEAD_COLS), lambda s: (0, 0))
+    table = pl.BlockSpec(cosine.shape, lambda s: (0, 0))
     blocks = pl.BlockSpec((count, 1, seq_dev, 2 * HEAD_DIM), lambda s: (0, s, 0, 0))
     return run(
         attend_back_kernel,
@@ -569,8 +559,8 @@
 
 def turn_back_kernel(repeat, a_ref, b_ref, cos_ref, sin_ref, out_ref):
     total = a_ref[...].astype(F32) + b_ref[...].astype(F32)
-    cosine = jnp.concatenate([cos_ref[...]] * repeat, 0)
-    sine = jnp.concatenate([sin_ref[...]] * repeat, 0)
+    cosine = jnp.concatenate([cos_ref[:, HEAD_COLS:]] * repeat, 0)
+    sine = jnp.concatenate([sin_ref[:, HEAD_COLS:]] * repeat, 0)
     out_ref[...] = (total * cosine - swap_halves(total) * sine).astype(BF)
 
 
@@ -707,14 +697,13 @@
     return acc
 
 
-def reduce_rows(acc, bits, what, last_after=()):
-    for bit in list(reversed(bits))[:-1]:
+def reduce_rows(acc, bits, what):
+    steps = []
+    for bit in reversed(bits):
         half = acc.shape[0] // 2
-        got = bit.swap(acc[half:], what)
-        acc = (acc[:half].astype(F32) + got.astype(F32)).astype(BF)
-    half = acc.shape[0] // 2
-    last = after(acc[half:], *last_after) if last_after else acc[half:]
-    return acc[:half], bits[0].swap(last, what)
+        steps.append((acc[:half], bit.swap(acc[half:], what)))
+        acc = add_low(*steps[-1])
+    return steps
 
 
 def gather_team(value, bit_x, near, bit_core, what, marks):
@@ -727,11 +716,6 @@
 
 def add_low(a, b):
     return (a.astype(F32) + b.astype(F32)).astype(BF)
-
-
-def reduce_team(acc, bit_x, near, bit_core, what):
-    half = acc.shape[0] // 2
-    return reduce_four(acc[:half], bit_core.swap(acc[half:], what), bit_x, near, what)
 
 
 def reduce_four(acc, got, bit_x, near, what):
@@ -814,9 +798,10 @@
         shape = (parts.shape[2], team * depth)
         return run(functools.partial(columns_kernel, kinds), [parts], [shape_of(shape, BF)] * kinds)
 
-    def mlp_rows(sums, kinds):
-        shape = (team, kinds * depth, sums[0].shape[0] // kinds)
-        return mlp_trade(run(functools.partial(rows_kernel, kinds, depth), sums, [shape_of(shape, BF)])[0])
+    def mlp_rows(sums):
+        kinds = sum(t.shape[0] for t in sums) // units
+        shape = (team, kinds * depth, units)
+        return mlp_trade(run(functools.partial(rows_kernel, depth), sums, [shape_of(shape, BF)])[0])
 
     far_groups = []
     for n in range(2):
@@ -859,14 +844,14 @@
     out_full = absolute(out_rel.reshape(ctx, depth, width), c_index, ctx_bits)
     out_full = out_full.reshape(ctx * depth, width)
 
-    gain_all = jnp.broadcast_to(after(attn_gain, own)[None], (dp * ctx, depth))
+    gate_own, up_own = mlp_slices([after(gate_weight, own), up_weight], gain_two, halves[-1])
+    gain_all = jnp.broadcast_to(after(attn_gain, gate_own)[None], (dp * ctx, depth))
     gain_all = lax.all_to_all(gain_all, ("dp", "ctx"), 0, 0, tiled=True)
     gain_all = gain_all.reshape(1, width).astype(F32)
     a1_half = gather_rows(norm_to(attn_order, x, gain_all), dp_bits[:1], "a1")
     a1 = gather_rows(a1_half, dp_bits[1:], "a1")
-    gate_own, up_own = mlp_slices([after(gate_weight, halves[1]), up_weight], gain_two, halves[-1], a1_half)
     gate = far_gather(gate_own)
-    (down_own,) = mlp_slices([after(down_weight.T, gate_own)], None)
+    (down_own,) = mlp_slices([after(down_weight.T, gain_all)], None)
     units = down_own.shape[0]
 
     places = jnp.arange(seq_dev, dtype=jnp.int32)
@@ -890,66 +875,93 @@
             up = far_gather(after(up_own, kv))
             down = far_gather(after(down_own, kv))
         kv = jnp.concatenate([kv, bit.swap(kv, "kv")], 0)
-    gb = gather_team(order_to(mlp_order, after(cot, qkv[1])), bit_x, near, bit_core, "gb", [])
     kv = kv.reshape(ctx, all_seqs, seq_dev, 2 * HEAD_DIM)
-    heads = attend(queries, after(kv, gb), key_places, seq_dev)
+    heads = attend(queries, kv, key_places, seq_dev)
     branch = dot(heads, out_full).astype(BF)
-    branch = reduce_rows(branch, dp_bits, "branch")
+    branch = reduce_rows(branch, dp_bits, "branch")[-1]
     middle, a2 = middle_to(mlp_order, x, *branch)
 
+    gb = gather_team(order_to(mlp_order, after(cot, middle)), bit_x, near, bit_core, "gb", [])
     a2 = gather_team(a2, bit_x, near, bit_core, "a2", [])
     block = min(256, a2.shape[0])
     hidden, one, two = gate_up(a2, gate, up, units, block)
-    down_back = far_reduce(weight_grad(hidden, gb, pieces))
-    dboth, da2 = hidden_back(gb, one, two, down, gate, up, block)
+    down_terms = weight_grad(hidden, gb, pieces)
+    down_back = far_reduce(down_terms)
+    dboth, da2 = hidden_back(after(gb, down_terms), one, two, down, gate, up, block)
     half = da2.shape[0] // 2
     da2_got = bit_core.swap(da2[half:], "da2")
     da2_two, da2_mark = reduce_four(da2[:half], da2_got, bit_x, near, "da2")
-    both_back = far_reduce(weight_grad(dboth, after(a2, da2_mark), pieces))
-    grad_middle, db = norm_back(mlp_order, middle, cot, *da2_two, low=True)
+    down_out = result_rows(after(hidden, da2), down, width, block)
+    result_got = bit_core.swap(after(down_out[half:], da2_mark), "result")
+    both_terms = weight_grad(dboth, after(a2, da2_mark), pieces)
+    both_back = far_reduce(both_terms)
+    grad_middle, db = norm_back(mlp_order, middle, after(cot, both_terms, result_got), *da2_two, low=True)
     grad_branch = gather_rows(db, dp_bits, "db")
+    result_two, result_mark = reduce_four(
+        down_out[:half], after(result_got, db), bit_x, near, "result"
+    )
+    result = result_of(mlp_order, middle, *result_two)
 
     grad_heads = dot_nt(grad_branch, out_full)
     dq, dkv = attend_back(
-        queries, kv, key_places, grad_heads, cosine[:, :HEAD_COLS], sine[:, :HEAD_COLS], seq_dev
-    )
-
-    dkv_steps = []
-    acc = dkv.reshape(-1, 2 * HEAD_DIM)
-    for bit in reversed(ctx_bits):
-        half = acc.shape[0] // 2
-        dkv_steps.append((acc[:half], bit.swap(acc[half:], "dkv")))
-        acc = add_low(*dkv_steps[-1])
-    dkv_two = dkv_steps[-1]
-    dkv_first, dkv_last = dkv_steps[0][1], dkv_steps[-1][1]
-
-    down_back = mlp_rows([after(down_back, dq)], 1)
-    down_out = result_rows(after(hidden, dq), down, width, block)
-    result_two = reduce_team(down_out, bit_x, near, bit_core, "result")[0]
-    result = result_of(mlp_order, middle, *result_two)
-    both_back = mlp_rows([after(both_back, dkv_last, *result_two)], 2)
+        queries, kv, after(key_places, *result_two), grad_heads, cosine, sine, seq_dev
+    )
+
+    class Sum:
+        def __init__(self, terms, what):
+            self.terms, self.what, self.bits = terms, what, list(reversed(ctx_bits))
+
+        def step(self, *marks):
+            half = self.terms.shape[0] // 2
+            sent = after(self.terms[half:], *marks) if marks else self.terms[half:]
+            self.pair = self.terms[:half], self.bits.pop(0).swap(sent, self.what)
+            self.terms = add_low(*self.pair)
+            return self.pair[1]
+
+        def finish(self, *marks):
+            while self.bits:
+                self.step(*marks)
+            return self.pair
+
+    dkv_sum = Sum(dkv.reshape(-1, 2 * HEAD_DIM), "dkv")
+    dkv_first = dkv_sum.step()
+    dq_sum = Sum(dot_tn(a1, after(dq, dkv_first)).astype(BF), "dq_w")
+    dq_first = dq_sum.step()
+    dkv_sum.step(down_back)
+    dkv_two = dkv_sum.finish()
     dkv_low = run(
         functools.partial(turn_back_kernel, all_seqs),
-        list(dkv_two) + [cosine[:, HEAD_COLS:], sine[:, HEAD_COLS:]],
+        [after(dkv_two[0], dq_first), dkv_two[1]] + [cosine, sine],
         [shape_of((dp * rows, 2 * HEAD_DIM), BF)],
     )[0]
-    draw = jnp.concatenate([dq, dkv_low], -1)
-    da1 = wide(dot_nt, draw, qkv, width, min(256, dp * rows))
-    da1_two = reduce_rows(da1, dp_bits, "da1")
+    kv_sum = Sum(dot_tn(a1, dkv_low).astype(BF), "dkv_w")
+    kv_first = kv_sum.step()
+    da1 = wide(dot_nt, jnp.concatenate([dq, dkv_low], -1), qkv, width, min(256, dp * rows))
+    da1_steps = reduce_rows(da1, dp_bits, "da1")
+    da1_two = da1_steps[-1]
     (grad_tokens,) = norm_back(attn_order, x, grad_middle, *da1_two, gain_all)
-    q_total = add_low(*reduce_rows(dot_tn(a1, dq).astype(BF), ctx_bits, "dq_w", [down_back]))
-    kv_total = add_low(*reduce_rows(
-        dot_tn(a1, dkv_low).astype(BF), ctx_bits, "dkv_w", [*da1_two]
-    ))
+    dq_second = dq_sum.step()
+    kv_second = kv_sum.step(dq_second, da1_steps[0][1])
     out_total = dot_tn(heads, grad_branch).astype(BF).reshape(ctx, depth, width)
-    out_total = relative(after(out_total, dkv_steps[1][1]), c_index, ctx_bits).reshape(ctx * depth, width)
-    out_two = reduce_rows(out_total, ctx_bits, "dout_w")
-    qkv_total = jnp.concatenate([q_total, kv_total], -1).reshape(dp, depth, qkv_cols)
-    qkv_back = lax.all_to_all(qkv_total, "dp", 0, 0, tiled=True)
+    out_total = relative(after(out_total, kv_first), c_index, ctx_bits).reshape(ctx * depth, width)
+    out_sum = Sum(out_total, "dout_w")
+    out_first = out_sum.step()
+    all_back = mlp_rows([after(both_back, kv_first), down_back])
+    dq_two = dq_sum.finish()
+    kv_two = kv_sum.finish(dq_two[1], *da1_two)
+    out_second = out_sum.step()
+    out_two = out_sum.finish()
     output_grad = out_two[0].astype(F32) + out_two[1].astype(F32)
-
-    gate_grad, up_grad, mlp_sum = unpack(both_back, [gate_weight, up_weight], gain_two)
-    down_grad = unpack(down_back, None, None)[0].T
+    qkv_total = jnp.concatenate([add_low(*dq_two), add_low(*kv_two)], -1).reshape(dp, depth, qkv_cols)
+    qkv_back = lax.all_to_all(after(qkv_total, all_back), "dp", 0, 0, tiled=True)
+
+    wide_shape = shape_of(gate_weight.shape, F32)
+    gate_grad, up_grad, down_grad, mlp_sum = run(
+        unpack_kernel,
+        [all_back, gate_weight, up_weight, gain_two],
+        [wide_shape, wide_shape, wide_shape, shape_of((depth, 1), F32)],
+    )
+    down_grad = down_grad.T
     query_grad, key_grad, value_grad, attn_sum = run(
         functools.partial(unpack_qkv_kernel, dp),
         [query_weight, key_weight, value_weight, gain_one, qkv_back],

time: 564 us -> 533 us (0.945)
  waiting for transfers between devices: 267 us -> 227 us
  Pallas kernels: 90.1 us -> 99.1 us
    ppermute x49, waiting for transfers between devices: 251 us -> 209 us  [swap(): return lax.ppermute(value, self.axis, self.pairs)]
    unnamed x201 -> x179, local copies, waits for them, and re-layouts: 30.7 us -> 40.3 us
    pallas_call x27 -> x25, Pallas kernels: 90.1 us -> 99.1 us  [run(): pl.pallas_call(kernel, name=name, out_shape=list(outs), in_specs=specs or...]
    convert_element_type x8 -> x0, other arithmetic: 7.83 us -> none  [reduce_rows(): acc = (acc[:half].astype(F32) + got.astype(F32)).astype(BF)]
    convert_element_type x10 -> x18, other arithmetic: 7.98 us -> 14 us  [add_low(): return (a.astype(F32) + b.astype(F32)).astype(BF)]
    all_to_all x4 -> x3, starting transfers between devices: 16.7 us -> 11.6 us  [mlp_trade(): lax.all_to_all(parts, ('dp', 'ctx'), 0, 0, axis_index_groups=team_groups,...]
  transfers between devices with their start and end apart: 63 -> 62, of which waited for: 32 -> 32; matrix products, arithmetic and copies ran while one was open for 14% -> 15% of each run, Pallas kernels for 15% -> 18%
where the time goes in v4:
time: 533 us; the launch traced here: 527 us
  waiting for transfers between devices  227 us (43%)
  Pallas kernels  99.1 us (19%)
  starting transfers between devices  75.9 us (14%)
  local copies, waits for them, and re-layouts  62.6 us (12%)
  other arithmetic  38.1 us (7%)
  between operations  15.3 us (3%)
  matrix products  8.22 us (2%)
    ppermute x49, waiting for transfers between devices, swap(): return lax.ppermute(value, self.axis, self.pairs)  209 us
    pallas_call x25, Pallas kernels, run(): pl.pallas_call(kernel, name=name, out_shape=list(outs), in_specs=specs or...  99.1 us
    ppermute x49, starting transfers between devices, swap(): return lax.ppermute(value, self.axis, self.pairs)  54.4 us
    unnamed x179, local copies, waits for them, and re-layouts  40.3 us
    convert_element_type x18, other arithmetic, add_low(): return (a.astype(F32) + b.astype(F32)).astype(BF)  14 us
    all_to_all x3, starting transfers between devices, mlp_trade(): lax.all_to_all(parts, ('dp', 'ctx'), 0, 0, axis_index_groups=team_groups,...  11.6 us
  transfers between devices with their start and end apart: 62, of which 32 were waited for; matrix products, arithmetic and copies ran while one was open for 15% of the time, Pallas kernels for 18%

profile of v4, /device:TPU:0, one launch (start us, length us, event | category | flops | bytes accessed | tf_op | source)
XLA Modules:
  0.0 526.6 jit_solution(1624492589867704363)
XLA Ops:
  17.5 5.9 %collective-permute-done = bf16[64,2048]{1,0:T(8,128)(2,1)S(1)} collective-permute-done((bf16[64,2048]{1,0:T(8,128)(2,1)}, bf16[64,2048]{1,0:T(8,128)(2,1)S(1)}, u32[]{:S(2)}, u32[]{:S(2)}) %collective-permute-start) | collective-permute-done | bytes 262176 | tf_op jit(solution)/shard_map/out_ctx2/ppermute | solution.py:73
  30.6 4.4 all-to-all-start
  35.0 8.6 %collective-permute-done.4 = bf16[256,640]{1,0:T(8,128)(2,1)} collective-permute-done((bf16[256,640]{1,0:T(8,128)(2,1)S(1)}, bf16[256,640]{1,0:T(8,128)(2,1)}, u32[]{:S(2)}, u32[]{:S(2)}) %collective-permute-start.4) | collective-permute-done | bytes 327712 | tf_op jit(solution)/shard_map/qkv_ctx2/ppermute | solution.py:73
  50.0 14.3 %collective-permute-done.6 = bf16[512,640]{1,0:T(8,128)(2,1)S(1)} collective-permute-done((bf16[512,640]{1,0:T(8,128)(2,1)S(1)}, bf16[512,640]{1,0:T(8,128)(2,1)S(1)}, u32[]{:S(2)}, u32[]{:S(2)}) %collective-permute-start.6) | collective-permute-done | bytes 655392 | tf_op jit(solution)/shard_map/qkv_ctx1/ppermute | solution.py:73
  75.5 6.9 %all-to-all-done.1 = bf16[32,1,64]{2,1,0:T(2,128)(2,1)S(1)} async-done(((bf16[32,1,64]{2,1,0:T(2,128)(2,1)}), bf16[32,1,64]{2,1,0:T(2,128)(2,1)S(1)}, u32[]{:S(2)}, u32[]{:S(2)}) %all-to-all-start.1) | async-done | bytes 4128 | tf_op jit(solution)/shard_map/all_to_all | solution.py:849
  85.2 12.5 %collective-permute-done.7 = bf16[128,2048]{1,0:T(8,128)(2,1)S(1)} collective-permute-done((bf16[128,2048]{1,0:T(8,128)(2,1)S(1)}, bf16[128,2048]{1,0:T(8,128)(2,1)S(1)}, u32[]{:S(2)}, u32[]{:S(2)}) %collective-permute-start.7) | collective-permute-done | bytes 524320 | tf_op jit(solution)/shard_map/a1_dp1/ppermute | solution.py:73
  104.2 16.4 %collective-permute-done.9.refs_4_.refs_1_ = bf16[1024,640]{1,0:T(8,128)(2,1)} collective-permute-done((bf16[1024,640]{1,0:T(8,128)(2,1)S(1)}, bf16[1024,640]{1,0:T(8,128)(2,1)}, u32[]{:S(2)}, u32[]{:S(2)}) %collective-permute-start.9) | collective-permute-done | bytes 1310752 | tf_op jit(solution)/shard_map/qkv_ctx0/ppermute | solution.py:73
  124.2 4.9 project_kernel.1
  131.6 5.8 %collective-permute-done.10 = bf16[512,128]{1,0:T(8,128)(2,1)S(1)} collective-permute-done((bf16[512,128]{1,0:T(8,128)(2,1)}, bf16[512,128]{1,0:T(8,128)(2,1)S(1)}, u32[]{:S(2)}, u32[]{:S(2)}) %collective-permute-start.10) | collective-permute-done | bytes 131104 | tf_op jit(solution)/shard_map/kv_ctx2/ppermute | solution.py:73
  138.6 6.2 %collective-permute-done.11 = bf16[1024,128]{1,0:T(8,128)(2,1)S(1)} collective-permute-done((bf16[1024,128]{1,0:T(8,128)(2,1)S(1)}, bf16[1024,128]{1,0:T(8,128)(2,1)S(1)}, u32[]{:S(2)}, u32[]{:S(2)}) %collective-permute-start.11) | collective-permute-done | bytes 262176 | tf_op jit(solution)/shard_map/kv_ctx1/ppermute | solution.py:73
  149.4 7.6 %collective-permute-done.12 = bf16[2048,128]{1,0:T(8,128)(2,1)} collective-permute-done((bf16[2048,128]{1,0:T(8,128)(2,1)S(1)}, bf16[2048,128]{1,0:T(8,128)(2,1)}, u32[]{:S(2)}, u32[]{:S(2)}) %collective-permute-start.12) | collective-permute-done | bytes 524320 | tf_op jit(solution)/shard_map/kv_ctx0/ppermute | solution.py:73
  158.2 5.2 attend_kernel.1
  169.5 12.5 %collective-permute-done.15.b_ref = bf16[128,2048]{1,0:T(8,128)(2,1)S(1)} collective-permute-done((bf16[128,2048]{1,0:T(8,128)(2,1)S(1)}, bf16[128,2048]{1,0:T(8,128)(2,1)S(1)}, u32[]{:S(2)}, u32[]{:S(2)}) %collective-permute-start.15) | collective-permute-done | bytes 524320 | tf_op jit(solution)/shard_map/branch_dp1/ppermute | solution.py:73
  193.5 7.8 %collective-permute-done.22 = bf16[128,2048]{1,0:T(8,128)(2,1)} collective-permute-done((bf16[128,2048]{1,0:T(8,128)(2,1)}, bf16[128,2048]{1,0:T(8,128)(2,1)}, u32[]{:S(2)}, u32[]{:S(2)}) %collective-permute-start.22) | collective-permute-done | bytes 524320 | tf_op jit(solution)/shard_map/gb_ctx0/ppermute | solution.py:73
  205.4 7.1 %collective-permute-done.17 = bf16[128,2048]{1,0:T(8,128)(2,1)} collective-permute-done((bf16[128,2048]{1,0:T(8,128)(2,1)}, bf16[128,2048]{1,0:T(8,128)(2,1)}, u32[]{:S(2)}, u32[]{:S(2)}) %collective-permute-start.17) | collective-permute-done | bytes 524320 | tf_op jit(solution)/shard_map/a2_ctx0/ppermute | solution.py:73
  231.3 10.8 %gate_kernel.1 = (bf16[1024,704]{1,0:T(8,128)(2,1)S(1)}, f32[1024,704]{1,0:T(8,128)}, f32[1024,704]{1,0:T(8,128)}) custom-call(bf16[1024,2048]{1,0:T(8,128)(2,1)} %pad_maximum_fusion.a_ref.right_ref, bf16[2816,512]{1,0:T(8,128)(2,1)S(1)} %copy-done.3, bf16[2816,512]{1,0:T(8,128)(2,1)} %all-gather.6.cloned.1.call-done.up_ref), custom_call_target="tpu_custom_call" | custom-call | tf_op jit(solution)/shard_map/gate_kernel/pallas_call | solution.py:47
  242.1 5.4 %pad_maximum_fusion.1.right_ref.g_ref = bf16[1024,2048]{1,0:T(8,128)(2,1)} fusion(bf16[512,2048]{1,0:T(8,128)(2,1)} %collective-permute-done.25, bf16[512,2048]{1,0:T(8,128)(2,1)} %constant_dynamic-update-slice_fusion.14), kind=kLoop, calls=%fused_computation.1 | loop fusion | flops 8388608 | bytes 8388608 | tf_op jit(solution)/shard_map/concatenate | solution.py:714
  247.5 6.5 %weight_grad_kernel.2 = bf16[2816,512]{1,0:T(8,128)(2,1)} custom-call(bf16[1024,704]{1,0:T(8,128)(2,1)S(1)} %get-tuple-element.82.left_ref.h_ref, bf16[1024,2048]{1,0:T(8,128)(2,1)} %pad_maximum_fusion.1.right_ref.g_ref), custom_call_target="tpu_custom_call" | custom-call | tf_op jit(solution)/shard_map/weight_grad_kernel/pallas_call | solution.py:47
  254.1 9.0 %all-gather.8.cloned.1.call-done.down_ref = bf16[2816,512]{1,0:T(8,128)(2,1)} async-done(((bf16[704,512]{1,0:T(8,128)(2,1)}), bf16[2816,512]{1,0:T(8,128)(2,1)}) %all-gather.8.cloned.1.call-update) | async-done | bytes 2883600 | tf_op jit(solution)/shard_map/all_gather | solution.py:812
  263.1 16.4 %hidden_kernel.1 = (bf16[1024,1408]{1,0:T(8,128)(2,1)}, bf16[1024,2048]{1,0:T(8,128)(2,1)}) custom-call(bf16[1024,2048]{1,0:T(8,128)(2,1)} %pad_maximum_fusion.1.right_ref.g_ref, f32[1024,704]{1,0:T(8,128)} %get-tuple-element.78.one_ref, f32[1024,704]{1,0:T(8,128)} %get-tuple-element.79.two_ref, bf16[2816,512]{1,0:T(8,128)(2,1)} %all-gather.8.cloned.1.call-done.down_ref, ...), custom_call_target="tpu_custom_call" | custom-call | tf_op jit(solution)/shard_map/hidden_kernel/pallas_call | solution.py:47
  298.8 9.2 %weight_grad_kernel.3 = bf16[5632,512]{1,0:T(8,128)(2,1)} custom-call(bf16[1024,1408]{1,0:T(8,128)(2,1)S(1)} %copy-done.14, bf16[1024,2048]{1,0:T(8,128)(2,1)} %pad_maximum_fusion.a_ref.right_ref), custom_call_target="tpu_custom_call" | custom-call | tf_op jit(solution)/shard_map/weight_grad_kernel/pallas_call | solution.py:47
  311.1 11.6 %collective-permute-done.29 = bf16[128,2048]{1,0:T(8,128)(2,1)S(1)} collective-permute-done((bf16[128,2048]{1,0:T(8,128)(2,1)}, bf16[128,2048]{1,0:T(8,128)(2,1)S(1)}, u32[]{:S(2)}, u32[]{:S(2)}) %collective-permute-start.29) | collective-permute-done | bytes 524320 | tf_op jit(solution)/shard_map/da2_dp1/ppermute | solution.py:73
  332.2 4.9 collective-permute-done.32
  340.6 10.1 %collective-permute-done.36 = bf16[128,2048]{1,0:T(8,128)(2,1)S(1)} collective-permute-done((bf16[128,2048]{1,0:T(8,128)(2,1)S(1)}, bf16[128,2048]{1,0:T(8,128)(2,1)S(1)}, u32[]{:S(2)}, u32[]{:S(2)}) %collective-permute-start.36) | collective-permute-done | bytes 524320 | tf_op jit(solution)/shard_map/db_dp1/ppermute | solution.py:73
  353.0 6.9 %collective-permute-done.33 = bf16[128,2048]{1,0:T(8,128)(2,1)S(1)} collective-permute-done((bf16[128,2048]{1,0:T(8,128)(2,1)S(1)}, bf16[128,2048]{1,0:T(8,128)(2,1)S(1)}, u32[]{:S(2)}, u32[]{:S(2)}) %collective-permute-start.33) | collective-permute-done | bytes 524320 | tf_op jit(solution)/shard_map/result_dp1/ppermute | solution.py:73
  360.8 4.7 collective-permute-done.35.b_ref
  368.3 20.1 %attend_back_kernel.1 = (bf16[512,512]{1,0:T(8,128)(2,1)S(1)}, bf16[8,8,64,128]{3,2,1,0:T(8,128)(2,1)S(1)}) custom-call(bf16[512,512]{1,0:T(8,128)(2,1)S(1)} %copy-done.27, bf16[8,8,64,128]{3,2,1,0:T(8,128)(2,1)S(1)} %bitcast.47, s32[1,512]{1,0:T(1,128)S(1)} %add.218.key_ref, f32[512,512]{1,0:T(8,128)S(1)} %fusion.20.do_ref, f32[64,640]{1,0:T(8,128)S(1)} %copy-done.20, ...), custom_call_target="tpu_custom_call" | custom-call | tf_op jit(solution)/shard_map/attend_back_kernel/pallas_call | solution.py:47
  391.1 12.0 %collective-permute-done.38 = bf16[2048,128]{1,0:T(8,128)(2,1)S(1)} collective-permute-done((bf16[2048,128]{1,0:T(8,128)(2,1)S(1)}, bf16[2048,128]{1,0:T(8,128)(2,1)S(1)}, u32[]{:S(2)}, u32[]{:S(2)}) %collective-permute-start.38) | collective-permute-done | bytes 524320 | tf_op jit(solution)/shard_map/dkv_ctx0/ppermute | solution.py:73
  414.5 8.1 %collective-permute-done.39 = bf16[1024,128]{1,0:T(8,128)(2,1)} collective-permute-done((bf16[1024,128]{1,0:T(8,128)(2,1)}, bf16[1024,128]{1,0:T(8,128)(2,1)}, u32[]{:S(2)}, u32[]{:S(2)}) %collective-permute-start.39) | collective-permute-done | bytes 262176 | tf_op jit(solution)/shard_map/dkv_ctx1/ppermute | solution.py:73
  425.9 7.9 %collective-permute-done.40 = bf16[1024,512]{0,1:T(8,128)(2,1)} collective-permute-done((bf16[1024,512]{0,1:T(8,128)(2,1)}, bf16[1024,512]{0,1:T(8,128)(2,1)}, u32[]{:S(2)}, u32[]{:S(2)}) %collective-permute-start.40) | collective-permute-done | bytes 1048608 | tf_op jit(solution)/shard_map/dq_w_ctx0/ppermute | solution.py:73
  449.6 7.5 %collective-permute-done.44 = bf16[512,512]{0,1:T(8,128)(2,1)S(1)} collective-permute-done((bf16[512,512]{0,1:T(8,128)(2,1)S(1)}, bf16[512,512]{0,1:T(8,128)(2,1)S(1)}, u32[]{:S(2)}, u32[]{:S(2)}) %collective-permute-start.44) | collective-permute-done | bytes 524320 | tf_op jit(solution)/shard_map/dq_w_ctx1/ppermute | solution.py:73
  477.3 12.3 %collective-permute-done.47 = bf16[512,128]{0,1:T(8,128)(2,1)S(1)} collective-permute-done((bf16[512,128]{0,1:T(8,128)(2,1)S(1)}, bf16[512,128]{0,1:T(8,128)(2,1)S(1)}, u32[]{:S(2)}, u32[]{:S(2)}) %collective-permute-start.47) | collective-permute-done | bytes 131104 | tf_op jit(solution)/shard_map/dkv_w_ctx1/ppermute | solution.py:73
  (399 shorter events, 221.8 us)
Async XLA Ops:
  7.2 16.2 %collective-permute-start = (bf16[64,2048]{1,0:T(8,128)(2,1)}, bf16[64,2048]{1,0:T(8,128)(2,1)S(1)}, u32[]{:S(2)}, u32[]{:S(2)}) collective-permute-start(bf16[64,2048]{1,0:T(8,128)(2,1)} %param.17), channel_id=1, source_target_pairs={{0,4},{1,5},{2,6},{3,7},{4,0},{5,1},{6,2},{7,3},{8,12},{9,13},{10,... | collective-permute-start | bytes 786440 | tf_op jit(solution)/shard_map/out_ctx2/ppermute | solution.py:73
  24.2 20.5 %collective-permute-start.5 = (bf16[128,2048]{1,0:T(8,128)(2,1)}, bf16[128,2048]{1,0:T(8,128)(2,1)}, u32[]{:S(2)}, u32[]{:S(2)}) collective-permute-start(bf16[128,2048]{1,0:T(8,128)(2,1)} %get-tuple-element.142), channel_id=1, source_target_pairs={{0,2},{1,3},{2,0},{3,1},{4,6},{5,7},{6,4},{7,5},{8,10},{9,11},{10,... | collective-permute-start | bytes 1572872 | tf_op jit(solution)/shard_map/out_ctx1/ppermute | solution.py:73
  25.2 18.4 %collective-permute-start.4 = (bf16[256,640]{1,0:T(8,128)(2,1)S(1)}, bf16[256,640]{1,0:T(8,128)(2,1)}, u32[]{:S(2)}, u32[]{:S(2)}) collective-permute-start(bf16[256,640]{1,0:T(8,128)(2,1)S(1)} %bitcast.53), channel_id=1, source_target_pairs={{0,4},{1,5},{2,6},{3,7},{4,0},{5,1},{6,2},{7,3},{8,12},{9,13},{10,... | collective-permute-start | bytes 983048 | tf_op jit(solution)/shard_map/qkv_ctx2/ppermute | solution.py:73
  30.6 33.9 %all-to-all-start = ((bf16[8,128,704]{1,2,0:T(8,128)(2,1)}), bf16[8,128,704]{1,2,0:T(8,128)(2,1)}, u32[]{:S(2)}, u32[]{:S(2)}) async-start(bf16[8,128,704]{1,2,0:T(8,128)(2,1)} %copy.31), calls=%async_computation | async-start | bytes 2883584 | tf_op jit(solution)/shard_map/all_to_all | solution.py:791
  35.0 194.5 %all-gather.4.cloned.1.call-start = ((), (), s32[]{:S(2)}) async-start(), calls=%async_computation.7 | async-start | bytes 3604480 | tf_op jit(solution)/shard_map/all_gather | solution.py:812
  45.8 18.6 %collective-permute-start.6 = (bf16[512,640]{1,0:T(8,128)(2,1)S(1)}, bf16[512,640]{1,0:T(8,128)(2,1)S(1)}, u32[]{:S(2)}, u32[]{:S(2)}) collective-permute-start(bf16[512,640]{1,0:T(8,128)(2,1)S(1)} %pad_maximum_fusion.9), channel_id=1, source_target_pairs={{0,2},{1,3},{2,0},{3,1},{4,6},{5,7},{6,4},{7,5},{8,10},{9,11},{10,... | collective-permute-start | bytes 1966088 | tf_op jit(solution)/shard_map/qkv_ctx1/ppermute | solution.py:73
  84.6 36.0 %collective-permute-start.9 = (bf16[1024,640]{1,0:T(8,128)(2,1)S(1)}, bf16[1024,640]{1,0:T(8,128)(2,1)}, u32[]{:S(2)}, u32[]{:S(2)}) collective-permute-start(bf16[1024,640]{1,0:T(8,128)(2,1)S(1)} %constant_dynamic-update-slice_fusion.5.refs_3_.refs_0_), channel_id=1, source_target_pairs={{0,1},{1,0},{2,3},{3,2},{4,5},{5,4},{6,7},{7,6},{8,9},{9,8},{10,11... | collective-permute-start | bytes 3932168 | tf_op jit(solution)/shard_map/qkv_ctx0/ppermute | solution.py:73
  99.5 23.0 %collective-permute-start.8 = (bf16[256,2048]{1,0:T(8,128)(2,1)}, bf16[256,2048]{1,0:T(8,128)(2,1)}, u32[]{:S(2)}, u32[]{:S(2)}) collective-permute-start(bf16[256,2048]{1,0:T(8,128)(2,1)} %pad_maximum_fusion.4), channel_id=1, source_target_pairs={{0,8},{8,0},{16,24},{24,16},{1,9},{9,1},{17,25},{25,17},{2,10},{10... | collective-permute-start | bytes 3145736 | tf_op jit(solution)/shard_map/a1_dp0/ppermute | solution.py:73
  100.6 29.8 %all-to-all-start.2 = ((bf16[8,64,704]{2,1,0:T(8,128)(2,1)}), bf16[8,64,704]{2,1,0:T(8,128)(2,1)S(1)}, u32[]{:S(2)}, u32[]{:S(2)}) async-start(bf16[8,64,704]{2,1,0:T(8,128)(2,1)} %copy-done.12), calls=%async_computation.2 | async-start | bytes 1572864 | tf_op jit(solution)/shard_map/all_to_all | solution.py:791
  104.2 125.3 %all-gather.6.cloned.1.call-start = ((), (), s32[]{:S(2)}) async-start(), calls=%async_computation.8 | async-start | bytes 3604480 | tf_op jit(solution)/shard_map/all_gather | solution.py:812
  120.6 26.7 %collective-permute-start.13 = (bf16[256,2048]{1,0:T(8,128)(2,1)}, bf16[256,2048]{1,0:T(8,128)(2,1)}, u32[]{:S(2)}, u32[]{:S(2)}) collective-permute-start(bf16[256,2048]{1,0:T(8,128)(2,1)} %copy-done.66), channel_id=1, source_target_pairs={{0,1},{1,0},{2,3},{3,2},{4,5},{5,4},{6,7},{7,6},{8,9},{9,8},{10,11... | collective-permute-start | bytes 3145736 | tf_op jit(solution)/shard_map/out_ctx0/ppermute | solution.py:73
  146.3 116.7 %all-gather.8.cloned.1.call-start = ((), (), s32[]{:S(2)}) async-start(), calls=%async_computation.9 | async-start | bytes 3604480 | tf_op jit(solution)/shard_map/all_gather | solution.py:812
  186.7 17.1 %collective-permute-start.21 = (bf16[128,2048]{1,0:T(8,128)(2,1)}, bf16[128,2048]{1,0:T(8,128)(2,1)}, u32[]{:S(2)}, u32[]{:S(2)}) collective-permute-start(bf16[128,2048]{1,0:T(8,128)(2,1)} %order_kernel.1), channel_id=1, source_target_pairs={{0,16},{8,24},{16,0},{24,8},{1,17},{9,25},{17,1},{25,9},{2,18},{10... | collective-permute-start | bytes 1572872 | tf_op jit(solution)/shard_map/gb_dp1/ppermute | solution.py:73
  188.2 24.3 %collective-permute-start.17 = (bf16[128,2048]{1,0:T(8,128)(2,1)}, bf16[128,2048]{1,0:T(8,128)(2,1)}, u32[]{:S(2)}, u32[]{:S(2)}) collective-permute-start(bf16[128,2048]{1,0:T(8,128)(2,1)} %get-tuple-element.72), channel_id=1, source_target_pairs={{0,1},{1,0},{2,3},{3,2},{4,5},{5,4},{6,7},{7,6},{8,9},{9,8},{10,11... | collective-permute-start | bytes 1572872 | tf_op jit(solution)/shard_map/a2_ctx0/ppermute | solution.py:73
  189.6 25.4 %collective-permute-start.16 = (bf16[128,2048]{1,0:T(8,128)(2,1)}, bf16[128,2048]{1,0:T(8,128)(2,1)}, u32[]{:S(2)}, u32[]{:S(2)}) collective-permute-start(bf16[128,2048]{1,0:T(8,128)(2,1)} %get-tuple-element.72), channel_id=1, source_target_pairs={{0,16},{8,24},{16,0},{24,8},{1,17},{9,25},{17,1},{25,9},{2,18},{10... | collective-permute-start | bytes 1572872 | tf_op jit(solution)/shard_map/a2_dp1/ppermute | solution.py:73
  190.2 213.9 %reduce-scatter.3.cloned.1.call-start = ((), (), s32[]{:S(2)}) async-start(), calls=%async_computation.10 | async-start | bytes 3604480 | tf_op jit(solution)/shard_map/reduce_scatter | solution.py:815
  202.2 20.6 %collective-permute-start.23 = (bf16[64,2048]{1,0:T(8,128)(2,1)S(1)}, bf16[64,2048]{1,0:T(8,128)(2,1)S(1)}, u32[]{:S(2)}, u32[]{:S(2)}) collective-permute-start(bf16[64,2048]{1,0:T(8,128)(2,1)S(1)} %slice.260), channel_id=1, source_target_pairs={{0,16},{8,24},{16,0},{24,8},{1,17},{9,25},{17,1},{25,9},{2,18},{10... | collective-permute-start | bytes 786440 | tf_op jit(solution)/shard_map/gb_dp1/ppermute | solution.py:73
  204.8 18.8 %collective-permute-start.24 = (bf16[64,2048]{1,0:T(8,128)(2,1)S(1)}, bf16[64,2048]{1,0:T(8,128)(2,1)S(1)}, u32[]{:S(2)}, u32[]{:S(2)}) collective-permute-start(bf16[64,2048]{1,0:T(8,128)(2,1)S(1)} %slice.261), channel_id=1, source_target_pairs={{0,1},{1,0},{2,3},{3,2},{4,5},{5,4},{6,7},{7,6},{8,9},{9,8},{10,11... | collective-permute-start | bytes 786440 | tf_op jit(solution)/shard_map/gb_ctx0/ppermute | solution.py:73
  224.3 17.8 %collective-permute-start.25 = (bf16[512,2048]{1,0:T(8,128)(2,1)}, bf16[512,2048]{1,0:T(8,128)(2,1)}, u32[]{:S(2)}, u32[]{:S(2)}) collective-permute-start(bf16[512,2048]{1,0:T(8,128)(2,1)} %constant_dynamic-update-slice_fusion.14), channel_id=1, source_target_pairs={{0,8},{8,0},{16,24},{24,16},{1,9},{9,1},{17,25},{25,17},{2,10},{10... | collective-permute-start | bytes 6291464 | tf_op jit(solution)/shard_map/gb_dp0/ppermute | solution.py:73
  254.0 209.3 %reduce-scatter.5.cloned.1.call-start = ((), (), s32[]{:S(2)}) async-start(), calls=%async_computation.11 | async-start | bytes 7208960 | tf_op jit(solution)/shard_map/reduce_scatter | solution.py:815
  298.8 25.0 %collective-permute-start.28 = (bf16[512,2048]{1,0:T(8,128)(2,1)}, bf16[512,2048]{1,0:T(8,128)(2,1)}, u32[]{:S(2)}, u32[]{:S(2)}) collective-permute-start(bf16[512,2048]{1,0:T(8,128)(2,1)} %slice.263), channel_id=1, source_target_pairs={{0,8},{8,0},{16,24},{24,16},{1,9},{9,1},{17,25},{25,17},{2,10},{10... | collective-permute-start | bytes 6291464 | tf_op jit(solution)/shard_map/result_dp0/ppermute | solution.py:73
  331.1 19.6 %collective-permute-start.36 = (bf16[128,2048]{1,0:T(8,128)(2,1)S(1)}, bf16[128,2048]{1,0:T(8,128)(2,1)S(1)}, u32[]{:S(2)}, u32[]{:S(2)}) collective-permute-start(bf16[128,2048]{1,0:T(8,128)(2,1)S(1)} %get-tuple-element.87), channel_id=1, source_target_pairs={{0,16},{8,24},{16,0},{24,8},{1,17},{9,25},{17,1},{25,9},{2,18},{10... | collective-permute-start | bytes 1572872 | tf_op jit(solution)/shard_map/db_dp1/ppermute | solution.py:73
  339.6 20.2 %collective-permute-start.33 = (bf16[128,2048]{1,0:T(8,128)(2,1)S(1)}, bf16[128,2048]{1,0:T(8,128)(2,1)S(1)}, u32[]{:S(2)}, u32[]{:S(2)}) collective-permute-start(bf16[128,2048]{1,0:T(8,128)(2,1)S(1)} %pad_maximum_fusion.13), channel_id=1, source_target_pairs={{0,16},{8,24},{16,0},{24,8},{1,17},{9,25},{17,1},{25,9},{2,18},{10... | collective-permute-start | bytes 1572872 | tf_op jit(solution)/shard_map/result_dp1/ppermute | solution.py:73
  404.0 18.6 %collective-permute-start.39 = (bf16[1024,128]{1,0:T(8,128)(2,1)}, bf16[1024,128]{1,0:T(8,128)(2,1)}, u32[]{:S(2)}, u32[]{:S(2)}) collective-permute-start(bf16[1024,128]{1,0:T(8,128)(2,1)} %slice.279), channel_id=1, source_target_pairs={{0,2},{1,3},{2,0},{3,1},{4,6},{5,7},{6,4},{7,5},{8,10},{9,11},{10,... | collective-permute-start | bytes 786440 | tf_op jit(solution)/shard_map/dkv_ctx1/ppermute | solution.py:73
  409.2 24.6 %collective-permute-start.40 = (bf16[1024,512]{0,1:T(8,128)(2,1)}, bf16[1024,512]{0,1:T(8,128)(2,1)}, u32[]{:S(2)}, u32[]{:S(2)}) collective-permute-start(bf16[1024,512]{0,1:T(8,128)(2,1)} %slice.281), channel_id=1, source_target_pairs={{0,1},{1,0},{2,3},{3,2},{4,5},{5,4},{6,7},{7,6},{8,9},{9,8},{10,11... | collective-permute-start | bytes 3145736 | tf_op jit(solution)/shard_map/dq_w_ctx0/ppermute | solution.py:73
  440.9 19.6 %collective-permute-start.42 = (bf16[256,2048]{1,0:T(8,128)(2,1)S(1)}, bf16[256,2048]{1,0:T(8,128)(2,1)S(1)}, u32[]{:S(2)}, u32[]{:S(2)}) collective-permute-start(bf16[256,2048]{1,0:T(8,128)(2,1)S(1)} %slice.284), channel_id=1, source_target_pairs={{0,8},{8,0},{16,24},{24,16},{1,9},{9,1},{17,25},{25,17},{2,10},{10... | collective-permute-start | bytes 3145736 | tf_op jit(solution)/shard_map/da1_dp0/ppermute | solution.py:73
  447.8 24.2 %collective-permute-start.49 = (bf16[256,2048]{1,0:T(8,128)(2,1)}, bf16[256,2048]{1,0:T(8,128)(2,1)}, u32[]{:S(2)}, u32[]{:S(2)}) collective-permute-start(bf16[256,2048]{1,0:T(8,128)(2,1)} %bitcast.24), channel_id=1, source_target_pairs={{0,1},{1,0},{2,3},{3,2},{4,5},{5,4},{6,7},{7,6},{8,9},{9,8},{10,11... | collective-permute-start | bytes 3145736 | tf_op jit(solution)/shard_map/dout_w_ctx0/ppermute | solution.py:73
  458.0 18.2 %collective-permute-start.45 = (bf16[256,512]{0,1:T(8,128)(2,1)}, bf16[256,512]{0,1:T(8,128)(2,1)}, u32[]{:S(2)}, u32[]{:S(2)}) collective-permute-start(bf16[256,512]{0,1:T(8,128)(2,1)} %slice.291), channel_id=1, source_target_pairs={{0,4},{1,5},{2,6},{3,7},{4,0},{5,1},{6,2},{7,3},{8,12},{9,13},{10,... | collective-permute-start | bytes 786440 | tf_op jit(solution)/shard_map/dq_w_ctx2/ppermute | solution.py:73
  461.9 27.8 %collective-permute-start.43 = (bf16[128,2048]{1,0:T(8,128)(2,1)}, bf16[128,2048]{1,0:T(8,128)(2,1)}, u32[]{:S(2)}, u32[]{:S(2)}) collective-permute-start(bf16[128,2048]{1,0:T(8,128)(2,1)} %get-tuple-element.129), channel_id=1, source_target_pairs={{0,16},{8,24},{16,0},{24,8},{1,17},{9,25},{17,1},{25,9},{2,18},{10... | collective-permute-start | bytes 1572872 | tf_op jit(solution)/shard_map/da1_dp1/ppermute | solution.py:73
  466.7 33.5 %all-to-all-start.3 = ((bf16[8,192,704]{2,1,0:T(8,128)(2,1)}), bf16[8,192,704]{2,1,0:T(8,128)(2,1)S(1)}, u32[]{:S(2)}, u32[]{:S(2)}) async-start(bf16[8,192,704]{2,1,0:T(8,128)(2,1)} %copy-done.4), calls=%async_computation.5 | async-start | bytes 4718592 | tf_op jit(solution)/shard_map/all_to_all | solution.py:791
  474.0 20.8 %collective-permute-start.50 = (bf16[128,2048]{1,0:T(8,128)(2,1)S(1)}, bf16[128,2048]{1,0:T(8,128)(2,1)S(1)}, u32[]{:S(2)}, u32[]{:S(2)}) collective-permute-start(bf16[128,2048]{1,0:T(8,128)(2,1)S(1)} %slice.299), channel_id=1, source_target_pairs={{0,2},{1,3},{2,0},{3,1},{4,6},{5,7},{6,4},{7,5},{8,10},{9,11},{10,... | collective-permute-start | bytes 1572872 | tf_op jit(solution)/shard_map/dout_w_ctx1/ppermute | solution.py:73
  500.3 16.6 %all-to-all-start.4 = ((bf16[4,64,640]{2,1,0:T(8,128)(2,1)}), bf16[4,64,640]{2,1,0:T(8,128)(2,1)S(1)}, u32[]{:S(2)}, u32[]{:S(2)}) async-start(bf16[4,64,640]{2,1,0:T(8,128)(2,1)} %bitcast.65), calls=%async_computation.6 | async-start | bytes 655360 | tf_op jit(solution)/shard_map/all_to_all | solution.py:956
  (109 other events, 809.3 us)
Sparse Core Ops, SparseCore 0:
  70.9 58.5 all-gather.3
  146.4 56.5 all-gather.5
  205.2 57.8 all-gather.7
  265.2 54.8 reduce-scatter.2
  322.3 110.1 reduce-scatter.4

commit v5 on v4

--- a/solution.py
+++ b/solution.py
@@ -586,11 +586,24 @@
     )[0]
 
 
-def gate_kernel(a_ref, gate_ref, up_ref, hid_ref, one_ref, two_ref):
+def either(first_ref, second_ref):
+    steps = pl.num_programs(0)
+    return jnp.where(pl.program_id(0) < steps // 2, first_ref[...], second_ref[...])
+
+
+def either_specs(block, width, steps):
+    return [
+        pl.BlockSpec((block, width), lambda i: (jnp.minimum(i, steps // 2 - 1), 0)),
+        pl.BlockSpec((block, width), lambda i: (jnp.maximum(i - steps // 2, 0), 0)),
+    ]
+
+
+def gate_kernel(first_ref, second_ref, gate_ref, up_ref, hid_ref, one_ref, two_ref):
     units, cols = hid_ref.shape[1], gate_ref.shape[1]
+    rows = either(first_ref, second_ref)
     gate = up = None
-    for k in range(a_ref.shape[1] // cols):
-        part = a_ref[:, k * cols : (k + 1) * cols]
+    for k in range(rows.shape[1] // cols):
+        part = rows[:, k * cols : (k + 1) * cols]
         g = dot_nt(part, gate_ref[k * units : (k + 1) * units])
         u = dot_nt(part, up_ref[k * units : (k + 1) * units])
         gate = g if gate is None else gate + g
@@ -603,26 +616,27 @@
 
 
 def gate_up(a2, gate, up, units, block):
-    rows, width = a2.shape
+    rows, width = 2 * a2[0].shape[0], a2[0].shape[1]
     moving = lambda i: (i, 0)
     out = pl.BlockSpec((block, units), moving)
     return run(
         gate_kernel,
-        [a2, gate, up],
+        [*a2, gate, up],
         [shape_of((rows, units), BF), shape_of((rows, units), F32), shape_of((rows, units), F32)],
-        [pl.BlockSpec((block, width), moving)] + [pl.BlockSpec(gate.shape, lambda i: (0, 0))] * 2,
+        either_specs(block, width, rows // block) + [pl.BlockSpec(gate.shape, lambda i: (0, 0))] * 2,
         [out, out, out],
         (rows // block,),
         vmem=48,
     )
 
 
-def hidden_kernel(g_ref, one_ref, two_ref, down_ref, gate_ref, up_ref, dboth_ref, out_ref):
+def hidden_kernel(first_ref, second_ref, one_ref, two_ref, down_ref, gate_ref, up_ref, dboth_ref, out_ref):
     units, cols = one_ref.shape[1], down_ref.shape[1]
-    pieces = g_ref.shape[1] // cols
+    rows = either(first_ref, second_ref)
+    pieces = rows.shape[1] // cols
     total = None
     for k in range(pieces):
-        term = dot_nt(g_ref[:, k * cols : (k + 1) * cols], down_ref[k * units : (k + 1) * units])
+        term = dot_nt(rows[:, k * cols : (k + 1) * cols], down_ref[k * units : (k + 1) * units])
         total = term if total is None else total + term
     dgate = (total * one_ref[...]).astype(BF)
     dup = (total * two_ref[...]).astype(BF)
@@ -635,7 +649,7 @@
 
 
 def hidden_back(gb, one, two, down, gate, up, block):
-    rows, width = gb.shape
+    rows, width = 2 * gb[0].shape[0], gb[0].shape[1]
     units = one.shape[1]
     moving = lambda i: (i, 0)
     fixed = lambda i: (0, 0)
@@ -643,9 +657,9 @@
     full = pl.BlockSpec((block, width), moving)
     return run(
         hidden_kernel,
-        [gb, one, two, down, gate, up],
+        [*gb, one, two, down, gate, up],
         [shape_of((rows, 2 * units), BF), shape_of((rows, width), BF)],
-        [full, thin, thin] + [pl.BlockSpec(down.shape, fixed)] * 3,
+        either_specs(block, width, rows // block) + [thin, thin] + [pl.BlockSpec(down.shape, fixed)] * 3,
         [pl.BlockSpec((block, 2 * units), moving), full],
         (rows // block,),
         vmem=56,
@@ -672,18 +686,20 @@
     )[0]
 
 
-def weight_grad_kernel(left_ref, right_ref, out_ref):
-    out_ref[...] = dot_tn(left_ref[...], right_ref[...]).astype(BF)
+def weight_grad_kernel(left_ref, first_ref, second_ref, out_ref):
+    half = first_ref.shape[0]
+    total = dot_tn(left_ref[:half], first_ref[...]) + dot_tn(left_ref[half:], second_ref[...])
+    out_ref[...] = total.astype(BF)
 
 
 def weight_grad(left, right, pieces):
     rows, units = left.shape
-    cols = right.shape[1] // pieces
+    cols = right[0].shape[1] // pieces
     return run(
         weight_grad_kernel,
-        [left, right],
+        [left, *right],
         [shape_of((pieces * units, cols), BF)],
-        [pl.BlockSpec((rows, units), lambda i: (0, 0)), pl.BlockSpec((rows, cols), lambda i: (0, i))],
+        [pl.BlockSpec((rows, units), lambda i: (0, 0)), *[pl.BlockSpec((rows // 2, cols), lambda i: (0, i))] * 2],
         [pl.BlockSpec((units, cols), lambda i: (i, 0))],
         (pieces,),
         vmem=48,
@@ -711,7 +727,7 @@
     by_x, by_near = bit_x.swap(value, what), near.swap(value, what)
     diagonal = [bit_x.swap(by_near[:half], what), near.swap(by_x[half:], what)]
     four = after(jnp.concatenate([value, by_x, by_near] + diagonal, 0), *marks)
-    return jnp.concatenate([four, bit_core.swap(four, what)], 0)
+    return four, bit_core.swap(four, what)
 
 
 def add_low(a, b):
@@ -871,7 +887,7 @@
     for i, bit in enumerate(ctx_bits):
         if i == 1:
             kv = after(kv, down_own)
-        if i == len(ctx_bits) - 1:
+        if i == len(ctx_bits) - 2:
             up = far_gather(after(up_own, kv))
             down = far_gather(after(down_own, kv))
         kv = jnp.concatenate([kv, bit.swap(kv, "kv")], 0)
@@ -883,17 +899,17 @@
 
     gb = gather_team(order_to(mlp_order, after(cot, middle)), bit_x, near, bit_core, "gb", [])
     a2 = gather_team(a2, bit_x, near, bit_core, "a2", [])
-    block = min(256, a2.shape[0])
+    block = min(256, a2[0].shape[0])
     hidden, one, two = gate_up(a2, gate, up, units, block)
     down_terms = weight_grad(hidden, gb, pieces)
     down_back = far_reduce(down_terms)
-    dboth, da2 = hidden_back(after(gb, down_terms), one, two, down, gate, up, block)
+    dboth, da2 = hidden_back((after(gb[0], down_terms), gb[1]), one, two, down, gate, up, block)
     half = da2.shape[0] // 2
     da2_got = bit_core.swap(da2[half:], "da2")
     da2_two, da2_mark = reduce_four(da2[:half], da2_got, bit_x, near, "da2")
     down_out = result_rows(after(hidden, da2), down, width, block)
     result_got = bit_core.swap(after(down_out[half:], da2_mark), "result")
-    both_terms = weight_grad(dboth, after(a2, da2_mark), pieces)
+    both_terms = weight_grad(dboth, (after(a2[0], da2_mark), a2[1]), pieces)
     both_back = far_reduce(both_terms)
     grad_middle, db = norm_back(mlp_order, middle, after(cot, both_terms, result_got), *da2_two, low=True)
     grad_branch = gather_rows(db, dp_bits, "db")
@@ -949,7 +965,7 @@
     all_back = mlp_rows([after(both_back, kv_first), down_back])
     dq_two = dq_sum.finish()
     kv_two = kv_sum.finish(dq_two[1], *da1_two)
-    out_second = out_sum.step()
+    out_second = out_sum.step(kv_second)
     out_two = out_sum.finish()
     output_grad = out_two[0].astype(F32) + out_two[1].astype(F32)
     qkv_total = jnp.concatenate([add_low(*dq_two), add_low(*kv_two)], -1).reshape(dp, depth, qkv_cols)

time: 533 us -> 520 us (0.976)
  waiting for transfers between devices: 227 us -> 213 us
  starting transfers between devices: 75.9 us -> 89.7 us
  other arithmetic: 38.1 us -> 28.1 us
    ppermute x49, starting transfers between devices: 54.4 us -> 67.6 us  [swap(): return lax.ppermute(value, self.axis, self.pairs)]
    ppermute x49, waiting for transfers between devices: 209 us -> 197 us  [swap(): return lax.ppermute(value, self.axis, self.pairs)]
    concatenate x2 -> x0, other arithmetic: 7.92 us -> none  [gather_team(): return jnp.concatenate([four, bit_core.swap(four, what)], 0)]
    unnamed x179 -> x164, local copies, waits for them, and re-layouts: 40.3 us -> 35.8 us
  transfers between devices with their start and end apart: 62 -> 62, of which waited for: 32 -> 32; matrix products, arithmetic and copies ran while one was open for 15% -> 14% of each run, Pallas kernels for 18% -> 19%
where the time goes in v5:
time: 520 us; the launch traced here: 516 us
  waiting for transfers between devices  213 us (41%)
  Pallas kernels  101 us (19%)
  starting transfers between devices  89.7 us (17%)
  local copies, waits for them, and re-layouts  58.9 us (11%)
  other arithmetic  28.1 us (5%)
  between operations  15.3 us (3%)
  matrix products  10 us (2%)
    ppermute x49, waiting for transfers between devices, swap(): return lax.ppermute(value, self.axis, self.pairs)  197 us
    pallas_call x25, Pallas kernels, run(): pl.pallas_call(kernel, name=name, out_shape=list(outs), in_specs=specs or...  101 us
    ppermute x49, starting transfers between devices, swap(): return lax.ppermute(value, self.axis, self.pairs)  67.6 us
    unnamed x164, local copies, waits for them, and re-layouts  35.8 us
    convert_element_type x18, other arithmetic, add_low(): return (a.astype(F32) + b.astype(F32)).astype(BF)  13.1 us
    all_to_all x3, starting transfers between devices, mlp_trade(): lax.all_to_all(parts, ('dp', 'ctx'), 0, 0, axis_index_groups=team_groups,...  12.2 us
  transfers between devices with their start and end apart: 62, of which 32 were waited for; matrix products, arithmetic and copies ran while one was open for 14% of the time, Pallas kernels for 19%

profile of v5, /device:TPU:0, one launch (start us, length us, event | category | flops | bytes accessed | tf_op | source)
XLA Modules:
  0.0 516.1 jit_solution(7159958032190933128)
XLA Ops:
  17.5 5.9 %collective-permute-done = bf16[64,2048]{1,0:T(8,128)(2,1)S(1)} collective-permute-done((bf16[64,2048]{1,0:T(8,128)(2,1)}, bf16[64,2048]{1,0:T(8,128)(2,1)S(1)}, u32[]{:S(2)}, u32[]{:S(2)}) %collective-permute-start) | collective-permute-done | bytes 262176 | tf_op jit(solution)/shard_map/out_ctx2/ppermute | solution.py:73
  30.6 4.4 all-to-all-start
  35.0 8.6 %collective-permute-done.4 = bf16[256,640]{1,0:T(8,128)(2,1)} collective-permute-done((bf16[256,640]{1,0:T(8,128)(2,1)S(1)}, bf16[256,640]{1,0:T(8,128)(2,1)}, u32[]{:S(2)}, u32[]{:S(2)}) %collective-permute-start.4) | collective-permute-done | bytes 327712 | tf_op jit(solution)/shard_map/qkv_ctx2/ppermute | solution.py:73
  45.8 4.2 collective-permute-start.6
  50.0 14.3 %collective-permute-done.6 = bf16[512,640]{1,0:T(8,128)(2,1)S(1)} collective-permute-done((bf16[512,640]{1,0:T(8,128)(2,1)S(1)}, bf16[512,640]{1,0:T(8,128)(2,1)S(1)}, u32[]{:S(2)}, u32[]{:S(2)}) %collective-permute-start.6) | collective-permute-done | bytes 655392 | tf_op jit(solution)/shard_map/qkv_ctx1/ppermute | solution.py:73
  73.6 6.9 %all-to-all-done.1 = bf16[32,1,64]{2,1,0:T(2,128)(2,1)S(1)} async-done(((bf16[32,1,64]{2,1,0:T(2,128)(2,1)}), bf16[32,1,64]{2,1,0:T(2,128)(2,1)S(1)}, u32[]{:S(2)}, u32[]{:S(2)}) %all-to-all-start.1) | async-done | bytes 4128 | tf_op jit(solution)/shard_map/all_to_all | solution.py:865
  84.0 12.7 %collective-permute-done.7 = bf16[128,2048]{1,0:T(8,128)(2,1)S(1)} collective-permute-done((bf16[128,2048]{1,0:T(8,128)(2,1)}, bf16[128,2048]{1,0:T(8,128)(2,1)S(1)}, u32[]{:S(2)}, u32[]{:S(2)}) %collective-permute-start.7) | collective-permute-done | bytes 524320 | tf_op jit(solution)/shard_map/a1_dp1/ppermute | solution.py:73
  101.8 4.2 all-to-all-start.2
  107.4 12.0 %collective-permute-done.9.refs_4_.refs_1_ = bf16[1024,640]{1,0:T(8,128)(2,1)S(1)} collective-permute-done((bf16[1024,640]{1,0:T(8,128)(2,1)S(1)}, bf16[1024,640]{1,0:T(8,128)(2,1)S(1)}, u32[]{:S(2)}, u32[]{:S(2)}) %collective-permute-start.9) | collective-permute-done | bytes 1310752 | tf_op jit(solution)/shard_map/qkv_ctx0/ppermute | solution.py:73
  128.9 4.6 collective-permute-done.10
  134.9 6.1 %collective-permute-done.11 = bf16[1024,128]{1,0:T(8,128)(2,1)S(1)} collective-permute-done((bf16[1024,128]{1,0:T(8,128)(2,1)S(1)}, bf16[1024,128]{1,0:T(8,128)(2,1)S(1)}, u32[]{:S(2)}, u32[]{:S(2)}) %collective-permute-start.11) | collective-permute-done | bytes 262176 | tf_op jit(solution)/shard_map/kv_ctx1/ppermute | solution.py:73
  147.8 7.9 %collective-permute-done.12 = bf16[2048,128]{1,0:T(8,128)(2,1)S(1)} collective-permute-done((bf16[2048,128]{1,0:T(8,128)(2,1)S(1)}, bf16[2048,128]{1,0:T(8,128)(2,1)S(1)}, u32[]{:S(2)}, u32[]{:S(2)}) %collective-permute-start.12) | collective-permute-done | bytes 524320 | tf_op jit(solution)/shard_map/kv_ctx0/ppermute | solution.py:73
  155.8 5.2 %attend_kernel.1 = bf16[512,512]{1,0:T(8,128)(2,1)S(1)} custom-call(bf16[512,512]{1,0:T(8,128)(2,1)S(1)} %copy-done.25, bf16[8,8,64,128]{3,2,1,0:T(8,128)(2,1)S(1)} %bitcast.46, s32[1,512]{1,0:T(1,128)S(1)} %add.218.key_ref), custom_call_target="tpu_custom_call" | custom-call | tf_op jit(solution)/shard_map/attend_kernel/pallas_call | solution.py:47
  167.2 12.5 %collective-permute-done.15.b_ref = bf16[128,2048]{1,0:T(8,128)(2,1)S(1)} collective-permute-done((bf16[128,2048]{1,0:T(8,128)(2,1)S(1)}, bf16[128,2048]{1,0:T(8,128)(2,1)S(1)}, u32[]{:S(2)}, u32[]{:S(2)}) %collective-permute-start.15) | collective-permute-done | bytes 524320 | tf_op jit(solution)/shard_map/branch_dp1/ppermute | solution.py:73
  191.1 7.8 %collective-permute-done.22 = bf16[128,2048]{1,0:T(8,128)(2,1)} collective-permute-done((bf16[128,2048]{1,0:T(8,128)(2,1)}, bf16[128,2048]{1,0:T(8,128)(2,1)}, u32[]{:S(2)}, u32[]{:S(2)}) %collective-permute-start.22) | collective-permute-done | bytes 524320 | tf_op jit(solution)/shard_map/gb_ctx0/ppermute | solution.py:73
  203.2 7.0 %collective-permute-done.17 = bf16[128,2048]{1,0:T(8,128)(2,1)} collective-permute-done((bf16[128,2048]{1,0:T(8,128)(2,1)}, bf16[128,2048]{1,0:T(8,128)(2,1)}, u32[]{:S(2)}, u32[]{:S(2)}) %collective-permute-start.17) | collective-permute-done | bytes 524320 | tf_op jit(solution)/shard_map/a2_ctx0/ppermute | solution.py:73
  224.8 11.7 %gate_kernel.1 = (bf16[1024,704]{1,0:T(8,128)(2,1)S(1)}, f32[1024,704]{1,0:T(8,128)}, f32[1024,704]{1,0:T(8,128)}) custom-call(bf16[512,2048]{1,0:T(8,128)(2,1)S(1)} %constant_dynamic-update-slice_fusion.7.first_ref, bf16[512,2048]{1,0:T(8,128)(2,1)} %collective-permute-done.20.second_ref, bf16[2816,512]{1,0:T(8,128)(2,1)} %all-gather.4.cloned.1.call-done.gate_ref, ...), custom_call_target="tpu_custom_call" | custom-call | tf_op jit(solution)/shard_map/gate_kernel/pallas_call | solution.py:47
  236.5 6.5 %weight_grad_kernel.2 = bf16[2816,512]{1,0:T(8,128)(2,1)} custom-call(bf16[1024,704]{1,0:T(8,128)(2,1)S(1)} %get-tuple-element.83.left_ref.h_ref, bf16[512,2048]{1,0:T(8,128)(2,1)} %constant_dynamic-update-slice_fusion.12.first_ref, bf16[512,2048]{1,0:T(8,128)(2,1)} %collective-permute-done.25.second_ref), custom_call_target="tpu_custom_call" | custom-call | tf_op jit(solution)/shard_map/weight_grad_kernel/pallas_call | solution.py:47
  244.3 8.8 %all-gather.8.cloned.1.call-done.down_ref = bf16[2816,512]{1,0:T(8,128)(2,1)} async-done(((bf16[704,512]{1,0:T(8,128)(2,1)}), bf16[2816,512]{1,0:T(8,128)(2,1)}) %all-gather.8.cloned.1.call-update) | async-done | bytes 2883600 | tf_op jit(solution)/shard_map/all_gather | solution.py:828
  253.1 16.5 %hidden_kernel.1 = (bf16[1024,1408]{1,0:T(8,128)(2,1)}, bf16[1024,2048]{1,0:T(8,128)(2,1)}) custom-call(bf16[512,2048]{1,0:T(8,128)(2,1)} %constant_dynamic-update-slice_fusion.12.first_ref, bf16[512,2048]{1,0:T(8,128)(2,1)} %collective-permute-done.25.second_ref, f32[1024,704]{1,0:T(8,128)} %get-tuple-element.79.one_ref, ...), custom_call_target="tpu_custom_call" | custom-call | tf_op jit(solution)/shard_map/hidden_kernel/pallas_call | solution.py:47
  287.9 10.1 %weight_grad_kernel.3 = bf16[5632,512]{1,0:T(8,128)(2,1)} custom-call(bf16[1024,1408]{1,0:T(8,128)(2,1)} %get-tuple-element.85.left_ref, bf16[512,2048]{1,0:T(8,128)(2,1)S(1)} %constant_dynamic-update-slice_fusion.7.first_ref, bf16[512,2048]{1,0:T(8,128)(2,1)} %collective-permute-done.20.second_ref), custom_call_target="tpu_custom_call" | custom-call | tf_op jit(solution)/shard_map/weight_grad_kernel/pallas_call | solution.py:47
  301.2 12.2 %collective-permute-done.29 = bf16[128,2048]{1,0:T(8,128)(2,1)S(1)} collective-permute-done((bf16[128,2048]{1,0:T(8,128)(2,1)S(1)}, bf16[128,2048]{1,0:T(8,128)(2,1)S(1)}, u32[]{:S(2)}, u32[]{:S(2)}) %collective-permute-start.29) | collective-permute-done | bytes 524320 | tf_op jit(solution)/shard_map/da2_dp1/ppermute | solution.py:73
  321.5 5.2 %collective-permute-done.32 = bf16[64,2048]{1,0:T(8,128)(2,1)S(1)} collective-permute-done((bf16[64,2048]{1,0:T(8,128)(2,1)S(1)}, bf16[64,2048]{1,0:T(8,128)(2,1)S(1)}, u32[]{:S(2)}, u32[]{:S(2)}) %collective-permute-start.32) | collective-permute-done | bytes 262176 | tf_op jit(solution)/shard_map/result_ctx0/ppermute | solution.py:73
  330.3 9.6 %collective-permute-done.36 = bf16[128,2048]{1,0:T(8,128)(2,1)S(1)} collective-permute-done((bf16[128,2048]{1,0:T(8,128)(2,1)S(1)}, bf16[128,2048]{1,0:T(8,128)(2,1)S(1)}, u32[]{:S(2)}, u32[]{:S(2)}) %collective-permute-start.36) | collective-permute-done | bytes 524320 | tf_op jit(solution)/shard_map/db_dp1/ppermute | solution.py:73
  341.7 7.8 %collective-permute-done.33 = bf16[128,2048]{1,0:T(8,128)(2,1)S(1)} collective-permute-done((bf16[128,2048]{1,0:T(8,128)(2,1)S(1)}, bf16[128,2048]{1,0:T(8,128)(2,1)S(1)}, u32[]{:S(2)}, u32[]{:S(2)}) %collective-permute-start.33) | collective-permute-done | bytes 524320 | tf_op jit(solution)/shard_map/result_dp1/ppermute | solution.py:73
  349.7 4.9 collective-permute-done.35.b_ref
  358.2 20.1 %attend_back_kernel.1 = (bf16[512,512]{1,0:T(8,128)(2,1)S(1)}, bf16[8,8,64,128]{3,2,1,0:T(8,128)(2,1)S(1)}) custom-call(bf16[512,512]{1,0:T(8,128)(2,1)S(1)} %copy-done.26, bf16[8,8,64,128]{3,2,1,0:T(8,128)(2,1)S(1)} %bitcast.47, s32[1,512]{1,0:T(1,128)S(1)} %add.218.key_ref, f32[512,512]{1,0:T(8,128)S(1)} %fusion.20.do_ref, f32[64,640]{1,0:T(8,128)S(1)} %copy-done.21, ...), custom_call_target="tpu_custom_call" | custom-call | tf_op jit(solution)/shard_map/attend_back_kernel/pallas_call | solution.py:47
  380.0 12.2 %collective-permute-done.38 = bf16[2048,128]{1,0:T(8,128)(2,1)S(1)} collective-permute-done((bf16[2048,128]{1,0:T(8,128)(2,1)S(1)}, bf16[2048,128]{1,0:T(8,128)(2,1)S(1)}, u32[]{:S(2)}, u32[]{:S(2)}) %collective-permute-start.38) | collective-permute-done | bytes 524320 | tf_op jit(solution)/shard_map/dkv_ctx0/ppermute | solution.py:73
  399.1 12.2 %collective-permute-done.39 = bf16[1024,128]{1,0:T(8,128)(2,1)S(1)} collective-permute-done((bf16[1024,128]{1,0:T(8,128)(2,1)S(1)}, bf16[1024,128]{1,0:T(8,128)(2,1)S(1)}, u32[]{:S(2)}, u32[]{:S(2)}) %collective-permute-start.39) | collective-permute-done | bytes 262176 | tf_op jit(solution)/shard_map/dkv_ctx1/ppermute | solution.py:73
  416.0 6.1 %collective-permute-done.40 = bf16[1024,512]{0,1:T(8,128)(2,1)} collective-permute-done((bf16[1024,512]{0,1:T(8,128)(2,1)}, bf16[1024,512]{0,1:T(8,128)(2,1)}, u32[]{:S(2)}, u32[]{:S(2)}) %collective-permute-start.40) | collective-permute-done | bytes 1048608 | tf_op jit(solution)/shard_map/dq_w_ctx0/ppermute | solution.py:73
  469.0 11.7 %collective-permute-start.48 = (bf16[256,128]{0,1:T(8,128)(2,1)S(1)}, bf16[256,128]{0,1:T(8,128)(2,1)S(1)}, u32[]{:S(2)}, u32[]{:S(2)}) collective-permute-start(bf16[256,128]{0,1:T(8,128)(2,1)S(1)} %slice.297), channel_id=1, source_target_pairs={{0,4},{1,5},{2,6},{3,7},{4,0},{5,1},{6,2},{7,3},{8,12},{9,13},{10,... | collective-permute-start | bytes 196616 | tf_op jit(solution)/shard_map/dkv_w_ctx2/ppermute | solution.py:73
  492.8 4.6 collective-permute-done.51
  (382 shorter events, 216.2 us)
Async XLA Ops:
  7.2 16.2 %collective-permute-start = (bf16[64,2048]{1,0:T(8,128)(2,1)}, bf16[64,2048]{1,0:T(8,128)(2,1)S(1)}, u32[]{:S(2)}, u32[]{:S(2)}) collective-permute-start(bf16[64,2048]{1,0:T(8,128)(2,1)} %param.17), channel_id=1, source_target_pairs={{0,4},{1,5},{2,6},{3,7},{4,0},{5,1},{6,2},{7,3},{8,12},{9,13},{10,... | collective-permute-start | bytes 786440 | tf_op jit(solution)/shard_map/out_ctx2/ppermute | solution.py:73
  24.2 20.5 %collective-permute-start.5 = (bf16[128,2048]{1,0:T(8,128)(2,1)}, bf16[128,2048]{1,0:T(8,128)(2,1)}, u32[]{:S(2)}, u32[]{:S(2)}) collective-permute-start(bf16[128,2048]{1,0:T(8,128)(2,1)} %get-tuple-element.144), channel_id=1, source_target_pairs={{0,2},{1,3},{2,0},{3,1},{4,6},{5,7},{6,4},{7,5},{8,10},{9,11},{10,... | collective-permute-start | bytes 1572872 | tf_op jit(solution)/shard_map/out_ctx1/ppermute | solution.py:73
  25.2 18.4 %collective-permute-start.4 = (bf16[256,640]{1,0:T(8,128)(2,1)S(1)}, bf16[256,640]{1,0:T(8,128)(2,1)}, u32[]{:S(2)}, u32[]{:S(2)}) collective-permute-start(bf16[256,640]{1,0:T(8,128)(2,1)S(1)} %bitcast.53), channel_id=1, source_target_pairs={{0,4},{1,5},{2,6},{3,7},{4,0},{5,1},{6,2},{7,3},{8,12},{9,13},{10,... | collective-permute-start | bytes 983048 | tf_op jit(solution)/shard_map/qkv_ctx2/ppermute | solution.py:73
  30.6 33.9 %all-to-all-start = ((bf16[8,128,704]{1,2,0:T(8,128)(2,1)}), bf16[8,128,704]{1,2,0:T(8,128)(2,1)}, u32[]{:S(2)}, u32[]{:S(2)}) async-start(bf16[8,128,704]{1,2,0:T(8,128)(2,1)} %copy.31), calls=%async_computation | async-start | bytes 2883584 | tf_op jit(solution)/shard_map/all_to_all | solution.py:807
  35.0 187.5 %all-gather.4.cloned.1.call-start = ((), (), s32[]{:S(2)}) async-start(), calls=%async_computation.7 | async-start | bytes 3604480 | tf_op jit(solution)/shard_map/all_gather | solution.py:828
  45.8 18.6 %collective-permute-start.6 = (bf16[512,640]{1,0:T(8,128)(2,1)S(1)}, bf16[512,640]{1,0:T(8,128)(2,1)S(1)}, u32[]{:S(2)}, u32[]{:S(2)}) collective-permute-start(bf16[512,640]{1,0:T(8,128)(2,1)S(1)} %pad_maximum_fusion.7), channel_id=1, source_target_pairs={{0,2},{1,3},{2,0},{3,1},{4,6},{5,7},{6,4},{7,5},{8,10},{9,11},{10,... | collective-permute-start | bytes 1966088 | tf_op jit(solution)/shard_map/qkv_ctx1/ppermute | solution.py:73
  83.4 35.9 %collective-permute-start.9 = (bf16[1024,640]{1,0:T(8,128)(2,1)S(1)}, bf16[1024,640]{1,0:T(8,128)(2,1)S(1)}, u32[]{:S(2)}, u32[]{:S(2)}) collective-permute-start(bf16[1024,640]{1,0:T(8,128)(2,1)S(1)} %constant_dynamic-update-slice_fusion.5.refs_3_.refs_0_), channel_id=1, source_target_pairs={{0,1},{1,0},{2,3},{3,2},{4,5},{5,4},{6,7},{7,6},{8,9},{9,8},{10,11... | collective-permute-start | bytes 3932168 | tf_op jit(solution)/shard_map/qkv_ctx0/ppermute | solution.py:73
  99.6 20.3 %collective-permute-start.8 = (bf16[256,2048]{1,0:T(8,128)(2,1)}, bf16[256,2048]{1,0:T(8,128)(2,1)}, u32[]{:S(2)}, u32[]{:S(2)}) collective-permute-start(bf16[256,2048]{1,0:T(8,128)(2,1)} %pad_maximum_fusion.2), channel_id=1, source_target_pairs={{0,8},{8,0},{16,24},{24,16},{1,9},{9,1},{17,25},{25,17},{2,10},{10... | collective-permute-start | bytes 3145736 | tf_op jit(solution)/shard_map/a1_dp0/ppermute | solution.py:73
  101.8 24.8 %all-to-all-start.2 = ((bf16[8,64,704]{2,1,0:T(8,128)(2,1)}), bf16[8,64,704]{2,1,0:T(8,128)(2,1)}, u32[]{:S(2)}, u32[]{:S(2)}) async-start(bf16[8,64,704]{2,1,0:T(8,128)(2,1)} %copy-done.15), calls=%async_computation.2 | async-start | bytes 1572864 | tf_op jit(solution)/shard_map/all_to_all | solution.py:807
  106.0 116.5 %all-gather.6.cloned.1.call-start = ((), (), s32[]{:S(2)}) async-start(), calls=%async_computation.8 | async-start | bytes 3604480 | tf_op jit(solution)/shard_map/all_gather | solution.py:828
  119.3 26.8 %collective-permute-start.13 = (bf16[256,2048]{1,0:T(8,128)(2,1)}, bf16[256,2048]{1,0:T(8,128)(2,1)}, u32[]{:S(2)}, u32[]{:S(2)}) collective-permute-start(bf16[256,2048]{1,0:T(8,128)(2,1)} %copy-done.61), channel_id=1, source_target_pairs={{0,1},{1,0},{2,3},{3,2},{4,5},{5,4},{6,7},{7,6},{8,9},{9,8},{10,11... | collective-permute-start | bytes 3145736 | tf_op jit(solution)/shard_map/out_ctx0/ppermute | solution.py:73
  134.8 118.2 %all-gather.8.cloned.1.call-start = ((), (), s32[]{:S(2)}) async-start(), calls=%async_computation.9 | async-start | bytes 3604480 | tf_op jit(solution)/shard_map/all_gather | solution.py:828
  184.4 17.1 %collective-permute-start.21 = (bf16[128,2048]{1,0:T(8,128)(2,1)}, bf16[128,2048]{1,0:T(8,128)(2,1)}, u32[]{:S(2)}, u32[]{:S(2)}) collective-permute-start(bf16[128,2048]{1,0:T(8,128)(2,1)} %order_kernel.1), channel_id=1, source_target_pairs={{0,16},{8,24},{16,0},{24,8},{1,17},{9,25},{17,1},{25,9},{2,18},{10... | collective-permute-start | bytes 1572872 | tf_op jit(solution)/shard_map/gb_dp1/ppermute | solution.py:73
  185.9 24.3 %collective-permute-start.17 = (bf16[128,2048]{1,0:T(8,128)(2,1)}, bf16[128,2048]{1,0:T(8,128)(2,1)}, u32[]{:S(2)}, u32[]{:S(2)}) collective-permute-start(bf16[128,2048]{1,0:T(8,128)(2,1)} %get-tuple-element.73), channel_id=1, source_target_pairs={{0,1},{1,0},{2,3},{3,2},{4,5},{5,4},{6,7},{7,6},{8,9},{9,8},{10,11... | collective-permute-start | bytes 1572872 | tf_op jit(solution)/shard_map/a2_ctx0/ppermute | solution.py:73
  187.3 25.4 %collective-permute-start.16 = (bf16[128,2048]{1,0:T(8,128)(2,1)}, bf16[128,2048]{1,0:T(8,128)(2,1)}, u32[]{:S(2)}, u32[]{:S(2)}) collective-permute-start(bf16[128,2048]{1,0:T(8,128)(2,1)} %get-tuple-element.73), channel_id=1, source_target_pairs={{0,16},{8,24},{16,0},{24,8},{1,17},{9,25},{17,1},{25,9},{2,18},{10... | collective-permute-start | bytes 1572872 | tf_op jit(solution)/shard_map/a2_dp1/ppermute | solution.py:73
  187.9 204.6 %reduce-scatter.3.cloned.1.call-start = ((), (), s32[]{:S(2)}) async-start(), calls=%async_computation.10 | async-start | bytes 3604480 | tf_op jit(solution)/shard_map/reduce_scatter | solution.py:831
  199.9 20.6 %collective-permute-start.23 = (bf16[64,2048]{1,0:T(8,128)(2,1)S(1)}, bf16[64,2048]{1,0:T(8,128)(2,1)S(1)}, u32[]{:S(2)}, u32[]{:S(2)}) collective-permute-start(bf16[64,2048]{1,0:T(8,128)(2,1)S(1)} %slice.260), channel_id=1, source_target_pairs={{0,16},{8,24},{16,0},{24,8},{1,17},{9,25},{17,1},{25,9},{2,18},{10... | collective-permute-start | bytes 786440 | tf_op jit(solution)/shard_map/gb_dp1/ppermute | solution.py:73
  202.5 18.8 %collective-permute-start.24 = (bf16[64,2048]{1,0:T(8,128)(2,1)S(1)}, bf16[64,2048]{1,0:T(8,128)(2,1)S(1)}, u32[]{:S(2)}, u32[]{:S(2)}) collective-permute-start(bf16[64,2048]{1,0:T(8,128)(2,1)S(1)} %slice.261), channel_id=1, source_target_pairs={{0,1},{1,0},{2,3},{3,2},{4,5},{5,4},{6,7},{7,6},{8,9},{9,8},{10,11... | collective-permute-start | bytes 786440 | tf_op jit(solution)/shard_map/gb_ctx0/ppermute | solution.py:73
  244.2 205.7 %reduce-scatter.5.cloned.1.call-start = ((), (), s32[]{:S(2)}) async-start(), calls=%async_computation.11 | async-start | bytes 7208960 | tf_op jit(solution)/shard_map/reduce_scatter | solution.py:831
  287.9 26.6 %collective-permute-start.28 = (bf16[512,2048]{1,0:T(8,128)(2,1)}, bf16[512,2048]{1,0:T(8,128)(2,1)}, u32[]{:S(2)}, u32[]{:S(2)}) collective-permute-start(bf16[512,2048]{1,0:T(8,128)(2,1)} %slice.263), channel_id=1, source_target_pairs={{0,8},{8,0},{16,24},{24,16},{1,9},{9,1},{17,25},{25,17},{2,10},{10... | collective-permute-start | bytes 6291464 | tf_op jit(solution)/shard_map/result_dp0/ppermute | solution.py:73
  320.8 19.1 %collective-permute-start.36 = (bf16[128,2048]{1,0:T(8,128)(2,1)S(1)}, bf16[128,2048]{1,0:T(8,128)(2,1)S(1)}, u32[]{:S(2)}, u32[]{:S(2)}) collective-permute-start(bf16[128,2048]{1,0:T(8,128)(2,1)S(1)} %get-tuple-element.88), channel_id=1, source_target_pairs={{0,16},{8,24},{16,0},{24,8},{1,17},{9,25},{17,1},{25,9},{2,18},{10... | collective-permute-start | bytes 1572872 | tf_op jit(solution)/shard_map/db_dp1/ppermute | solution.py:73
  328.9 20.7 %collective-permute-start.33 = (bf16[128,2048]{1,0:T(8,128)(2,1)S(1)}, bf16[128,2048]{1,0:T(8,128)(2,1)S(1)}, u32[]{:S(2)}, u32[]{:S(2)}) collective-permute-start(bf16[128,2048]{1,0:T(8,128)(2,1)S(1)} %pad_maximum_fusion.12), channel_id=1, source_target_pairs={{0,16},{8,24},{16,0},{24,8},{1,17},{9,25},{17,1},{25,9},{2,18},{10... | collective-permute-start | bytes 1572872 | tf_op jit(solution)/shard_map/result_dp1/ppermute | solution.py:73
  392.4 18.9 %collective-permute-start.39 = (bf16[1024,128]{1,0:T(8,128)(2,1)S(1)}, bf16[1024,128]{1,0:T(8,128)(2,1)S(1)}, u32[]{:S(2)}, u32[]{:S(2)}) collective-permute-start(bf16[1024,128]{1,0:T(8,128)(2,1)S(1)} %slice.279), channel_id=1, source_target_pairs={{0,2},{1,3},{2,0},{3,1},{4,6},{5,7},{6,4},{7,5},{8,10},{9,11},{10,... | collective-permute-start | bytes 786440 | tf_op jit(solution)/shard_map/dkv_ctx1/ppermute | solution.py:73
  397.7 24.4 %collective-permute-start.40 = (bf16[1024,512]{0,1:T(8,128)(2,1)}, bf16[1024,512]{0,1:T(8,128)(2,1)}, u32[]{:S(2)}, u32[]{:S(2)}) collective-permute-start(bf16[1024,512]{0,1:T(8,128)(2,1)} %slice.281), channel_id=1, source_target_pairs={{0,1},{1,0},{2,3},{3,2},{4,5},{5,4},{6,7},{7,6},{8,9},{9,8},{10,11... | collective-permute-start | bytes 3145736 | tf_op jit(solution)/shard_map/dq_w_ctx0/ppermute | solution.py:73
  434.5 24.6 %collective-permute-start.49 = (bf16[256,2048]{1,0:T(8,128)(2,1)}, bf16[256,2048]{1,0:T(8,128)(2,1)}, u32[]{:S(2)}, u32[]{:S(2)}) collective-permute-start(bf16[256,2048]{1,0:T(8,128)(2,1)} %bitcast.24), channel_id=1, source_target_pairs={{0,1},{1,0},{2,3},{3,2},{4,5},{5,4},{6,7},{7,6},{8,9},{9,8},{10,11... | collective-permute-start | bytes 3145736 | tf_op jit(solution)/shard_map/dout_w_ctx0/ppermute | solution.py:73
  442.6 24.2 %collective-permute-start.45 = (bf16[256,512]{0,1:T(8,128)(2,1)}, bf16[256,512]{0,1:T(8,128)(2,1)}, u32[]{:S(2)}, u32[]{:S(2)}) collective-permute-start(bf16[256,512]{0,1:T(8,128)(2,1)} %slice.291), channel_id=1, source_target_pairs={{0,4},{1,5},{2,6},{3,7},{4,0},{5,1},{6,2},{7,3},{8,12},{9,13},{10,... | collective-permute-start | bytes 786440 | tf_op jit(solution)/shard_map/dq_w_ctx2/ppermute | solution.py:73
  445.4 16.4 %collective-permute-start.47 = (bf16[512,128]{0,1:T(8,128)(2,1)}, bf16[512,128]{0,1:T(8,128)(2,1)}, u32[]{:S(2)}, u32[]{:S(2)}) collective-permute-start(bf16[512,128]{0,1:T(8,128)(2,1)} %slice.295), channel_id=1, source_target_pairs={{0,2},{1,3},{2,0},{3,1},{4,6},{5,7},{6,4},{7,5},{8,10},{9,11},{10,... | collective-permute-start | bytes 393224 | tf_op jit(solution)/shard_map/dkv_w_ctx1/ppermute | solution.py:73
  448.6 20.3 %collective-permute-start.43 = (bf16[128,2048]{1,0:T(8,128)(2,1)}, bf16[128,2048]{1,0:T(8,128)(2,1)}, u32[]{:S(2)}, u32[]{:S(2)}) collective-permute-start(bf16[128,2048]{1,0:T(8,128)(2,1)} %get-tuple-element.131), channel_id=1, source_target_pairs={{0,16},{8,24},{16,0},{24,8},{1,17},{9,25},{17,1},{25,9},{2,18},{10... | collective-permute-start | bytes 1572872 | tf_op jit(solution)/shard_map/da1_dp1/ppermute | solution.py:73
  453.4 35.9 %all-to-all-start.3 = ((bf16[8,192,704]{2,1,0:T(8,128)(2,1)}), bf16[8,192,704]{2,1,0:T(8,128)(2,1)S(1)}, u32[]{:S(2)}, u32[]{:S(2)}) async-start(bf16[8,192,704]{2,1,0:T(8,128)(2,1)} %copy-done.3), calls=%async_computation.5 | async-start | bytes 4718592 | tf_op jit(solution)/shard_map/all_to_all | solution.py:807
  461.9 21.6 %collective-permute-start.50 = (bf16[128,2048]{1,0:T(8,128)(2,1)}, bf16[128,2048]{1,0:T(8,128)(2,1)}, u32[]{:S(2)}, u32[]{:S(2)}) collective-permute-start(bf16[128,2048]{1,0:T(8,128)(2,1)} %slice.299), channel_id=1, source_target_pairs={{0,2},{1,3},{2,0},{3,1},{4,6},{5,7},{6,4},{7,5},{8,10},{9,11},{10,... | collective-permute-start | bytes 1572872 | tf_op jit(solution)/shard_map/dout_w_ctx1/ppermute | solution.py:73
  469.0 19.4 %collective-permute-start.48 = (bf16[256,128]{0,1:T(8,128)(2,1)S(1)}, bf16[256,128]{0,1:T(8,128)(2,1)S(1)}, u32[]{:S(2)}, u32[]{:S(2)}) collective-permute-start(bf16[256,128]{0,1:T(8,128)(2,1)S(1)} %slice.297), channel_id=1, source_target_pairs={{0,4},{1,5},{2,6},{3,7},{4,0},{5,1},{6,2},{7,3},{8,12},{9,13},{10,... | collective-permute-start | bytes 196616 | tf_op jit(solution)/shard_map/dkv_w_ctx2/ppermute | solution.py:73
  489.3 17.1 %all-to-all-start.4 = ((bf16[4,64,640]{2,1,0:T(8,128)(2,1)}), bf16[4,64,640]{2,1,0:T(8,128)(2,1)S(1)}, u32[]{:S(2)}, u32[]{:S(2)}) async-start(bf16[4,64,640]{2,1,0:T(8,128)(2,1)} %bitcast.65), calls=%async_computation.6 | async-start | bytes 655360 | tf_op jit(solution)/shard_map/all_to_all | solution.py:972
  (102 other events, 871.0 us)
Sparse Core Ops, SparseCore 0:
  69.0 60.7 all-gather.3
  135.0 58.5 all-gather.5
  195.2 57.8 all-gather.7
  255.2 54.8 reduce-scatter.2
  312.3 108.8 reduce-scatter.4

commit v6 on v5

--- a/solution.py
+++ b/solution.py
@@ -969,7 +969,18 @@
     out_two = out_sum.finish()
     output_grad = out_two[0].astype(F32) + out_two[1].astype(F32)
     qkv_total = jnp.concatenate([add_low(*dq_two), add_low(*kv_two)], -1).reshape(dp, depth, qkv_cols)
-    qkv_back = lax.all_to_all(after(qkv_total, all_back), "dp", 0, 0, tiled=True)
+    def place(blocks):
+        return run(
+            functools.partial(place_kernel, dp),
+            [me] + blocks,
+            [shape_of((dp, depth, qkv_cols), BF)],
+            [SMEM] + [pl.BlockSpec(memory_space=pltpu.VMEM)] * dp,
+        )[0]
+
+    sent = place([qkv_total[r] for r in range(dp)])
+    qkv_back = place(
+        [sent[0]] + [swap_difference(sent[r], "dp", dp, r, "back") for r in range(1, dp)]
+    )
 
     wide_shape = shape_of(gate_weight.shape, F32)
     gate_grad, up_grad, down_grad, mlp_sum = run(

time: 520 us -> 520 us (level)
  waiting for transfers between devices: 213 us -> 228 us
  Pallas kernels: 101 us -> 93.3 us
  starting transfers between devices: 89.7 us -> 82.3 us
    ppermute x49, starting transfers between devices: 67.6 us -> 51.7 us  [swap(): return lax.ppermute(value, self.axis, self.pairs)]
    ppermute x3 -> x6, waiting for transfers between devices: 0.01 us -> 10.6 us  [swap_difference(): return lax.ppermute(value, axis, [(i, i ^ difference) for i in range(size)])]
    reduce_scatter x2, starting transfers between devices: 0.34 us -> 10.3 us  [far_reduce(): lax.psum_scatter(terms, 'ctx', scatter_dimension=0, tiled=True, axis_inde...]
    pallas_call x25 -> x27, Pallas kernels: 101 us -> 93.3 us  [run(): pl.pallas_call(kernel, name=name, out_shape=list(outs), in_specs=specs or...]
    unnamed x164 -> x172, local copies, waits for them, and re-layouts: 35.8 us -> 35.4 us
  transfers between devices with their start and end apart: 62 -> 64, of which waited for: 32 -> 35; matrix products, arithmetic and copies ran while one was open for 14% -> 13% of each run, Pallas kernels for 19% -> 17%
where the time goes in v6:
time: 520 us; the launch traced here: 511 us
  waiting for transfers between devices  228 us (44%)
  Pallas kernels  93.3 us (18%)
  starting transfers between devices  82.3 us (16%)
  local copies, waits for them, and re-layouts  57.3 us (11%)
  other arithmetic  24.4 us (5%)
  between operations  15.7 us (3%)
  matrix products  10.3 us (2%)
    ppermute x49, waiting for transfers between devices, swap(): return lax.ppermute(value, self.axis, self.pairs)  201 us
    pallas_call x27, Pallas kernels, run(): pl.pallas_call(kernel, name=name, out_shape=list(outs), in_specs=specs or...  93.3 us
    ppermute x49, starting transfers between devices, swap(): return lax.ppermute(value, self.axis, self.pairs)  51.7 us
    unnamed x172, local copies, waits for them, and re-layouts  35.4 us
    all_to_all x3, starting transfers between devices, mlp_trade(): lax.all_to_all(parts, ('dp', 'ctx'), 0, 0, axis_index_groups=team_groups,...  12.5 us
    convert_element_type x18, other arithmetic, add_low(): return (a.astype(F32) + b.astype(F32)).astype(BF)  11.6 us
    ppermute x6, waiting for transfers between devices, swap_difference(): return lax.ppermute(value, axis, [(i, i ^ difference) for i in range(size)])  10.6 us
  transfers between devices with their start and end apart: 64, of which 35 were waited for; matrix products, arithmetic and copies ran while one was open for 13% of the time, Pallas kernels for 17%

profile of v6, /device:TPU:0, one launch (start us, length us, event | category | flops | bytes accessed | tf_op | source)
XLA Modules:
  0.0 511.2 jit_solution(16527027117551715979)
XLA Ops:
  17.5 5.9 %collective-permute-done = bf16[64,2048]{1,0:T(8,128)(2,1)S(1)} collective-permute-done((bf16[64,2048]{1,0:T(8,128)(2,1)}, bf16[64,2048]{1,0:T(8,128)(2,1)S(1)}, u32[]{:S(2)}, u32[]{:S(2)}) %collective-permute-start) | collective-permute-done | bytes 262176 | tf_op jit(solution)/shard_map/out_ctx2/ppermute | solution.py:73
  30.6 4.4 all-to-all-start
  35.0 8.6 %collective-permute-done.4 = bf16[256,640]{1,0:T(8,128)(2,1)} collective-permute-done((bf16[256,640]{1,0:T(8,128)(2,1)S(1)}, bf16[256,640]{1,0:T(8,128)(2,1)}, u32[]{:S(2)}, u32[]{:S(2)}) %collective-permute-start.4) | collective-permute-done | bytes 327712 | tf_op jit(solution)/shard_map/qkv_ctx2/ppermute | solution.py:73
  50.0 14.3 %collective-permute-done.6 = bf16[512,640]{1,0:T(8,128)(2,1)S(1)} collective-permute-done((bf16[512,640]{1,0:T(8,128)(2,1)S(1)}, bf16[512,640]{1,0:T(8,128)(2,1)S(1)}, u32[]{:S(2)}, u32[]{:S(2)}) %collective-permute-start.6) | collective-permute-done | bytes 655392 | tf_op jit(solution)/shard_map/qkv_ctx1/ppermute | solution.py:73
  73.7 6.9 %all-to-all-done.1 = bf16[32,1,64]{2,1,0:T(2,128)(2,1)S(1)} async-done(((bf16[32,1,64]{2,1,0:T(2,128)(2,1)}), bf16[32,1,64]{2,1,0:T(2,128)(2,1)S(1)}, u32[]{:S(2)}, u32[]{:S(2)}) %all-to-all-start.1) | async-done | bytes 4128 | tf_op jit(solution)/shard_map/all_to_all | solution.py:865
  84.1 12.7 %collective-permute-done.7 = bf16[128,2048]{1,0:T(8,128)(2,1)S(1)} collective-permute-done((bf16[128,2048]{1,0:T(8,128)(2,1)}, bf16[128,2048]{1,0:T(8,128)(2,1)S(1)}, u32[]{:S(2)}, u32[]{:S(2)}) %collective-permute-start.7) | collective-permute-done | bytes 524320 | tf_op jit(solution)/shard_map/a1_dp1/ppermute | solution.py:73
  101.9 4.2 all-to-all-start.2
  107.4 11.9 %collective-permute-done.9.refs_4_.refs_1_ = bf16[1024,640]{1,0:T(8,128)(2,1)S(1)} collective-permute-done((bf16[1024,640]{1,0:T(8,128)(2,1)S(1)}, bf16[1024,640]{1,0:T(8,128)(2,1)S(1)}, u32[]{:S(2)}, u32[]{:S(2)}) %collective-permute-start.9) | collective-permute-done | bytes 1310752 | tf_op jit(solution)/shard_map/qkv_ctx0/ppermute | solution.py:73
  129.0 4.7 collective-permute-done.10
  134.9 6.1 %collective-permute-done.11 = bf16[1024,128]{1,0:T(8,128)(2,1)S(1)} collective-permute-done((bf16[1024,128]{1,0:T(8,128)(2,1)S(1)}, bf16[1024,128]{1,0:T(8,128)(2,1)S(1)}, u32[]{:S(2)}, u32[]{:S(2)}) %collective-permute-start.11) | collective-permute-done | bytes 262176 | tf_op jit(solution)/shard_map/kv_ctx1/ppermute | solution.py:73
  147.9 7.9 %collective-permute-done.12 = bf16[2048,128]{1,0:T(8,128)(2,1)S(1)} collective-permute-done((bf16[2048,128]{1,0:T(8,128)(2,1)S(1)}, bf16[2048,128]{1,0:T(8,128)(2,1)S(1)}, u32[]{:S(2)}, u32[]{:S(2)}) %collective-permute-start.12) | collective-permute-done | bytes 524320 | tf_op jit(solution)/shard_map/kv_ctx0/ppermute | solution.py:73
  155.9 5.2 %attend_kernel.1 = bf16[512,512]{1,0:T(8,128)(2,1)S(1)} custom-call(bf16[512,512]{1,0:T(8,128)(2,1)S(1)} %copy-done.25, bf16[8,8,64,128]{3,2,1,0:T(8,128)(2,1)S(1)} %bitcast.53, s32[1,512]{1,0:T(1,128)S(1)} %add.218.key_ref), custom_call_target="tpu_custom_call" | custom-call | tf_op jit(solution)/shard_map/attend_kernel/pallas_call | solution.py:47
  167.3 12.5 %collective-permute-done.15.b_ref = bf16[128,2048]{1,0:T(8,128)(2,1)S(1)} collective-permute-done((bf16[128,2048]{1,0:T(8,128)(2,1)S(1)}, bf16[128,2048]{1,0:T(8,128)(2,1)S(1)}, u32[]{:S(2)}, u32[]{:S(2)}) %collective-permute-start.15) | collective-permute-done | bytes 524320 | tf_op jit(solution)/shard_map/branch_dp1/ppermute | solution.py:73
  187.9 10.2 %reduce-scatter.3.cloned.1.call-start = ((), (), s32[]{:S(2)}) async-start(), calls=%async_computation.9 | async-start | bytes 3604480 | tf_op jit(solution)/shard_map/reduce_scatter | solution.py:831
  205.3 4.9 collective-permute-done.17
  224.8 11.7 %gate_kernel.1 = (bf16[1024,704]{1,0:T(8,128)(2,1)S(1)}, f32[1024,704]{1,0:T(8,128)}, f32[1024,704]{1,0:T(8,128)}) custom-call(bf16[512,2048]{1,0:T(8,128)(2,1)S(1)} %constant_dynamic-update-slice_fusion.7.first_ref, bf16[512,2048]{1,0:T(8,128)(2,1)} %collective-permute-done.20.second_ref, bf16[2816,512]{1,0:T(8,128)(2,1)} %all-gather.4.cloned.1.call-done.gate_ref, ...), custom_call_target="tpu_custom_call" | custom-call | tf_op jit(solution)/shard_map/gate_kernel/pallas_call | solution.py:47
  236.5 6.5 %weight_grad_kernel.2 = bf16[2816,512]{1,0:T(8,128)(2,1)} custom-call(bf16[1024,704]{1,0:T(8,128)(2,1)S(1)} %get-tuple-element.82.left_ref.h_ref, bf16[512,2048]{1,0:T(8,128)(2,1)} %constant_dynamic-update-slice_fusion.12.first_ref, bf16[512,2048]{1,0:T(8,128)(2,1)} %collective-permute-done.25.second_ref), custom_call_target="tpu_custom_call" | custom-call | tf_op jit(solution)/shard_map/weight_grad_kernel/pallas_call | solution.py:47
  244.2 8.9 %all-gather.8.cloned.1.call-done.down_ref = bf16[2816,512]{1,0:T(8,128)(2,1)} async-done(((bf16[704,512]{1,0:T(8,128)(2,1)}), bf16[2816,512]{1,0:T(8,128)(2,1)}) %all-gather.8.cloned.1.call-update) | async-done | bytes 2883600 | tf_op jit(solution)/shard_map/all_gather | solution.py:828
  253.1 16.6 %hidden_kernel.1 = (bf16[1024,1408]{1,0:T(8,128)(2,1)}, bf16[1024,2048]{1,0:T(8,128)(2,1)}) custom-call(bf16[512,2048]{1,0:T(8,128)(2,1)} %constant_dynamic-update-slice_fusion.12.first_ref, bf16[512,2048]{1,0:T(8,128)(2,1)} %collective-permute-done.25.second_ref, f32[1024,704]{1,0:T(8,128)} %get-tuple-element.78.one_ref, ...), custom_call_target="tpu_custom_call" | custom-call | tf_op jit(solution)/shard_map/hidden_kernel/pallas_call | solution.py:47
  289.4 10.0 %weight_grad_kernel.3 = bf16[5632,512]{1,0:T(8,128)(2,1)} custom-call(bf16[1024,1408]{1,0:T(8,128)(2,1)} %get-tuple-element.84.left_ref, bf16[512,2048]{1,0:T(8,128)(2,1)S(1)} %constant_dynamic-update-slice_fusion.7.first_ref, bf16[512,2048]{1,0:T(8,128)(2,1)} %collective-permute-done.20.second_ref), custom_call_target="tpu_custom_call" | custom-call | tf_op jit(solution)/shard_map/weight_grad_kernel/pallas_call | solution.py:47
  304.0 10.6 %collective-permute-done.31.b_ref = bf16[128,2048]{1,0:T(8,128)(2,1)S(1)} collective-permute-done((bf16[128,2048]{1,0:T(8,128)(2,1)S(1)}, bf16[128,2048]{1,0:T(8,128)(2,1)S(1)}, u32[]{:S(2)}, u32[]{:S(2)}) %collective-permute-start.31) | collective-permute-done | bytes 524320 | tf_op jit(solution)/shard_map/da2_ctx0/ppermute | solution.py:73
  321.4 5.0 collective-permute-done.32
  329.4 10.4 %collective-permute-done.36 = bf16[128,2048]{1,0:T(8,128)(2,1)S(1)} collective-permute-done((bf16[128,2048]{1,0:T(8,128)(2,1)S(1)}, bf16[128,2048]{1,0:T(8,128)(2,1)S(1)}, u32[]{:S(2)}, u32[]{:S(2)}) %collective-permute-start.36) | collective-permute-done | bytes 524320 | tf_op jit(solution)/shard_map/db_dp1/ppermute | solution.py:73
  341.7 7.5 %collective-permute-done.33 = bf16[128,2048]{1,0:T(8,128)(2,1)S(1)} collective-permute-done((bf16[128,2048]{1,0:T(8,128)(2,1)S(1)}, bf16[128,2048]{1,0:T(8,128)(2,1)S(1)}, u32[]{:S(2)}, u32[]{:S(2)}) %collective-permute-start.33) | collective-permute-done | bytes 524320 | tf_op jit(solution)/shard_map/result_dp1/ppermute | solution.py:73
  349.3 5.2 %collective-permute-done.35.b_ref = bf16[128,2048]{1,0:T(8,128)(2,1)S(1)} collective-permute-done((bf16[128,2048]{1,0:T(8,128)(2,1)S(1)}, bf16[128,2048]{1,0:T(8,128)(2,1)S(1)}, u32[]{:S(2)}, u32[]{:S(2)}) %collective-permute-start.35) | collective-permute-done | bytes 524320 | tf_op jit(solution)/shard_map/result_ctx0/ppermute | solution.py:73
  358.1 11.6 %attend_back_kernel.1 = (bf16[512,512]{1,0:T(8,128)(2,1)S(1)}, bf16[8,8,64,128]{3,2,1,0:T(8,128)(2,1)S(1)}) custom-call(bf16[512,512]{1,0:T(8,128)(2,1)S(1)} %copy-done.26, bf16[8,8,64,128]{3,2,1,0:T(8,128)(2,1)S(1)} %bitcast.54, s32[1,512]{1,0:T(1,128)S(1)} %add.218.key_ref, f32[512,512]{1,0:T(8,128)S(1)} %fusion.23.do_ref, f32[64,640]{1,0:T(8,128)S(1)} %copy-done.21, ...), custom_call_target="tpu_custom_call" | custom-call | tf_op jit(solution)/shard_map/attend_back_kernel/pallas_call | solution.py:47
  371.4 12.2 %collective-permute-done.38 = bf16[2048,128]{1,0:T(8,128)(2,1)S(1)} collective-permute-done((bf16[2048,128]{1,0:T(8,128)(2,1)S(1)}, bf16[2048,128]{1,0:T(8,128)(2,1)S(1)}, u32[]{:S(2)}, u32[]{:S(2)}) %collective-permute-start.38) | collective-permute-done | bytes 524320 | tf_op jit(solution)/shard_map/dkv_ctx0/ppermute | solution.py:73
  390.4 13.1 %collective-permute-done.39 = bf16[1024,128]{1,0:T(8,128)(2,1)S(1)} collective-permute-done((bf16[1024,128]{1,0:T(8,128)(2,1)S(1)}, bf16[1024,128]{1,0:T(8,128)(2,1)S(1)}, u32[]{:S(2)}, u32[]{:S(2)}) %collective-permute-start.39) | collective-permute-done | bytes 262176 | tf_op jit(solution)/shard_map/dkv_ctx1/ppermute | solution.py:73
  408.0 5.4 %collective-permute-done.40 = bf16[1024,512]{1,0:T(8,128)(2,1)} collective-permute-done((bf16[1024,512]{1,0:T(8,128)(2,1)}, bf16[1024,512]{1,0:T(8,128)(2,1)}, u32[]{:S(2)}, u32[]{:S(2)}) %collective-permute-start.40) | collective-permute-done | bytes 1048608 | tf_op jit(solution)/shard_map/dq_w_ctx0/ppermute | solution.py:73
  428.6 6.3 %collective-permute-done.44 = bf16[512,512]{1,0:T(8,128)(2,1)S(1)} collective-permute-done((bf16[512,512]{1,0:T(8,128)(2,1)S(1)}, bf16[512,512]{1,0:T(8,128)(2,1)S(1)}, u32[]{:S(2)}, u32[]{:S(2)}) %collective-permute-start.44) | collective-permute-done | bytes 524320 | tf_op jit(solution)/shard_map/dq_w_ctx1/ppermute | solution.py:73
  443.6 7.5 %collective-permute-done.52 = bf16[256,2048]{1,0:T(8,128)(2,1)S(1)} collective-permute-done((bf16[256,2048]{1,0:T(8,128)(2,1)S(1)}, bf16[256,2048]{1,0:T(8,128)(2,1)S(1)}, u32[]{:S(2)}, u32[]{:S(2)}) %collective-permute-start.52) | collective-permute-done | bytes 1048608 | tf_op jit(solution)/shard_map/dout_w_ctx0/ppermute | solution.py:73
  482.9 9.8 %collective-permute-done.50.refs_2_ = bf16[64,640]{1,0:T(8,128)(2,1)} collective-permute-done((bf16[64,640]{1,0:T(8,128)(2,1)}, bf16[64,640]{1,0:T(8,128)(2,1)}, u32[]{:S(2)}, u32[]{:S(2)}) %collective-permute-start.50) | collective-permute-done | bytes 81952 | tf_op jit(solution)/shard_map/back_dp/ppermute | solution.py:78
  (396 shorter events, 216.7 us)
Async XLA Ops:
  7.2 16.2 %collective-permute-start = (bf16[64,2048]{1,0:T(8,128)(2,1)}, bf16[64,2048]{1,0:T(8,128)(2,1)S(1)}, u32[]{:S(2)}, u32[]{:S(2)}) collective-permute-start(bf16[64,2048]{1,0:T(8,128)(2,1)} %param.17), channel_id=1, source_target_pairs={{0,4},{1,5},{2,6},{3,7},{4,0},{5,1},{6,2},{7,3},{8,12},{9,13},{10,... | collective-permute-start | bytes 786440 | tf_op jit(solution)/shard_map/out_ctx2/ppermute | solution.py:73
  24.2 20.5 %collective-permute-start.5 = (bf16[128,2048]{1,0:T(8,128)(2,1)}, bf16[128,2048]{1,0:T(8,128)(2,1)}, u32[]{:S(2)}, u32[]{:S(2)}) collective-permute-start(bf16[128,2048]{1,0:T(8,128)(2,1)} %get-tuple-element.150), channel_id=1, source_target_pairs={{0,2},{1,3},{2,0},{3,1},{4,6},{5,7},{6,4},{7,5},{8,10},{9,11},{10,... | collective-permute-start | bytes 1572872 | tf_op jit(solution)/shard_map/out_ctx1/ppermute | solution.py:73
  25.2 18.4 %collective-permute-start.4 = (bf16[256,640]{1,0:T(8,128)(2,1)S(1)}, bf16[256,640]{1,0:T(8,128)(2,1)}, u32[]{:S(2)}, u32[]{:S(2)}) collective-permute-start(bf16[256,640]{1,0:T(8,128)(2,1)S(1)} %bitcast.60), channel_id=1, source_target_pairs={{0,4},{1,5},{2,6},{3,7},{4,0},{5,1},{6,2},{7,3},{8,12},{9,13},{10,... | collective-permute-start | bytes 983048 | tf_op jit(solution)/shard_map/qkv_ctx2/ppermute | solution.py:73
  30.6 33.9 %all-to-all-start = ((bf16[8,128,704]{1,2,0:T(8,128)(2,1)}), bf16[8,128,704]{1,2,0:T(8,128)(2,1)}, u32[]{:S(2)}, u32[]{:S(2)}) async-start(bf16[8,128,704]{1,2,0:T(8,128)(2,1)} %copy.33), calls=%async_computation | async-start | bytes 2883584 | tf_op jit(solution)/shard_map/all_to_all | solution.py:807
  35.0 187.5 %all-gather.4.cloned.1.call-start = ((), (), s32[]{:S(2)}) async-start(), calls=%async_computation.6 | async-start | bytes 3604480 | tf_op jit(solution)/shard_map/all_gather | solution.py:828
  45.8 18.6 %collective-permute-start.6 = (bf16[512,640]{1,0:T(8,128)(2,1)S(1)}, bf16[512,640]{1,0:T(8,128)(2,1)S(1)}, u32[]{:S(2)}, u32[]{:S(2)}) collective-permute-start(bf16[512,640]{1,0:T(8,128)(2,1)S(1)} %pad_maximum_fusion.7), channel_id=1, source_target_pairs={{0,2},{1,3},{2,0},{3,1},{4,6},{5,7},{6,4},{7,5},{8,10},{9,11},{10,... | collective-permute-start | bytes 1966088 | tf_op jit(solution)/shard_map/qkv_ctx1/ppermute | solution.py:73
  83.5 35.9 %collective-permute-start.9 = (bf16[1024,640]{1,0:T(8,128)(2,1)S(1)}, bf16[1024,640]{1,0:T(8,128)(2,1)S(1)}, u32[]{:S(2)}, u32[]{:S(2)}) collective-permute-start(bf16[1024,640]{1,0:T(8,128)(2,1)S(1)} %constant_dynamic-update-slice_fusion.5.refs_3_.refs_0_), channel_id=1, source_target_pairs={{0,1},{1,0},{2,3},{3,2},{4,5},{5,4},{6,7},{7,6},{8,9},{9,8},{10,11... | collective-permute-start | bytes 3932168 | tf_op jit(solution)/shard_map/qkv_ctx0/ppermute | solution.py:73
  99.7 20.3 %collective-permute-start.8 = (bf16[256,2048]{1,0:T(8,128)(2,1)}, bf16[256,2048]{1,0:T(8,128)(2,1)}, u32[]{:S(2)}, u32[]{:S(2)}) collective-permute-start(bf16[256,2048]{1,0:T(8,128)(2,1)} %pad_maximum_fusion.2), channel_id=1, source_target_pairs={{0,8},{8,0},{16,24},{24,16},{1,9},{9,1},{17,25},{25,17},{2,10},{10... | collective-permute-start | bytes 3145736 | tf_op jit(solution)/shard_map/a1_dp0/ppermute | solution.py:73
  101.9 24.8 %all-to-all-start.2 = ((bf16[8,64,704]{2,1,0:T(8,128)(2,1)}), bf16[8,64,704]{2,1,0:T(8,128)(2,1)}, u32[]{:S(2)}, u32[]{:S(2)}) async-start(bf16[8,64,704]{2,1,0:T(8,128)(2,1)} %copy-done.15), calls=%async_computation.2 | async-start | bytes 1572864 | tf_op jit(solution)/shard_map/all_to_all | solution.py:807
  106.1 116.4 %all-gather.6.cloned.1.call-start = ((), (), s32[]{:S(2)}) async-start(), calls=%async_computation.7 | async-start | bytes 3604480 | tf_op jit(solution)/shard_map/all_gather | solution.py:828
  119.4 26.8 %collective-permute-start.13 = (bf16[256,2048]{1,0:T(8,128)(2,1)}, bf16[256,2048]{1,0:T(8,128)(2,1)}, u32[]{:S(2)}, u32[]{:S(2)}) collective-permute-start(bf16[256,2048]{1,0:T(8,128)(2,1)} %copy-done.66), channel_id=1, source_target_pairs={{0,1},{1,0},{2,3},{3,2},{4,5},{5,4},{6,7},{7,6},{8,9},{9,8},{10,11... | collective-permute-start | bytes 3145736 | tf_op jit(solution)/shard_map/out_ctx0/ppermute | solution.py:73
  134.9 118.2 %all-gather.8.cloned.1.call-start = ((), (), s32[]{:S(2)}) async-start(), calls=%async_computation.8 | async-start | bytes 3604480 | tf_op jit(solution)/shard_map/all_gather | solution.py:828
  183.8 17.3 %collective-permute-start.22 = (bf16[128,2048]{1,0:T(8,128)(2,1)}, bf16[128,2048]{1,0:T(8,128)(2,1)}, u32[]{:S(2)}, u32[]{:S(2)}) collective-permute-start(bf16[128,2048]{1,0:T(8,128)(2,1)} %order_kernel.1), channel_id=1, source_target_pairs={{0,1},{1,0},{2,3},{3,2},{4,5},{5,4},{6,7},{7,6},{8,9},{9,8},{10,11... | collective-permute-start | bytes 1572872 | tf_op jit(solution)/shard_map/gb_ctx0/ppermute | solution.py:73
  184.4 19.2 %collective-permute-start.21 = (bf16[128,2048]{1,0:T(8,128)(2,1)}, bf16[128,2048]{1,0:T(8,128)(2,1)}, u32[]{:S(2)}, u32[]{:S(2)}) collective-permute-start(bf16[128,2048]{1,0:T(8,128)(2,1)} %order_kernel.1), channel_id=1, source_target_pairs={{0,16},{8,24},{16,0},{24,8},{1,17},{9,25},{17,1},{25,9},{2,18},{10... | collective-permute-start | bytes 1572872 | tf_op jit(solution)/shard_map/gb_dp1/ppermute | solution.py:73
  185.9 24.3 %collective-permute-start.17 = (bf16[128,2048]{1,0:T(8,128)(2,1)}, bf16[128,2048]{1,0:T(8,128)(2,1)}, u32[]{:S(2)}, u32[]{:S(2)}) collective-permute-start(bf16[128,2048]{1,0:T(8,128)(2,1)} %get-tuple-element.72), channel_id=1, source_target_pairs={{0,1},{1,0},{2,3},{3,2},{4,5},{5,4},{6,7},{7,6},{8,9},{9,8},{10,11... | collective-permute-start | bytes 1572872 | tf_op jit(solution)/shard_map/a2_ctx0/ppermute | solution.py:73
  187.3 25.4 %collective-permute-start.16 = (bf16[128,2048]{1,0:T(8,128)(2,1)}, bf16[128,2048]{1,0:T(8,128)(2,1)}, u32[]{:S(2)}, u32[]{:S(2)}) collective-permute-start(bf16[128,2048]{1,0:T(8,128)(2,1)} %get-tuple-element.72), channel_id=1, source_target_pairs={{0,16},{8,24},{16,0},{24,8},{1,17},{9,25},{17,1},{25,9},{2,18},{10... | collective-permute-start | bytes 1572872 | tf_op jit(solution)/shard_map/a2_dp1/ppermute | solution.py:73
  187.9 195.9 %reduce-scatter.3.cloned.1.call-start = ((), (), s32[]{:S(2)}) async-start(), calls=%async_computation.9 | async-start | bytes 3604480 | tf_op jit(solution)/shard_map/reduce_scatter | solution.py:831
  202.1 18.4 %collective-permute-start.23 = (bf16[64,2048]{1,0:T(8,128)(2,1)S(1)}, bf16[64,2048]{1,0:T(8,128)(2,1)S(1)}, u32[]{:S(2)}, u32[]{:S(2)}) collective-permute-start(bf16[64,2048]{1,0:T(8,128)(2,1)S(1)} %slice.296), channel_id=1, source_target_pairs={{0,16},{8,24},{16,0},{24,8},{1,17},{9,25},{17,1},{25,9},{2,18},{10... | collective-permute-start | bytes 786440 | tf_op jit(solution)/shard_map/gb_dp1/ppermute | solution.py:73
  204.6 16.6 %collective-permute-start.24 = (bf16[64,2048]{1,0:T(8,128)(2,1)S(1)}, bf16[64,2048]{1,0:T(8,128)(2,1)S(1)}, u32[]{:S(2)}, u32[]{:S(2)}) collective-permute-start(bf16[64,2048]{1,0:T(8,128)(2,1)S(1)} %slice.297), channel_id=1, source_target_pairs={{0,1},{1,0},{2,3},{3,2},{4,5},{5,4},{6,7},{7,6},{8,9},{9,8},{10,11... | collective-permute-start | bytes 786440 | tf_op jit(solution)/shard_map/gb_ctx0/ppermute | solution.py:73
  244.2 210.3 %reduce-scatter.5.cloned.1.call-start = ((), (), s32[]{:S(2)}) async-start(), calls=%async_computation.10 | async-start | bytes 7208960 | tf_op jit(solution)/shard_map/reduce_scatter | solution.py:831
  288.0 16.0 %collective-permute-start.28 = (bf16[512,2048]{1,0:T(8,128)(2,1)}, bf16[512,2048]{1,0:T(8,128)(2,1)}, u32[]{:S(2)}, u32[]{:S(2)}) collective-permute-start(bf16[512,2048]{1,0:T(8,128)(2,1)} %slice.299), channel_id=1, source_target_pairs={{0,8},{8,0},{16,24},{24,16},{1,9},{9,1},{17,25},{25,17},{2,10},{10... | collective-permute-start | bytes 6291464 | tf_op jit(solution)/shard_map/result_dp0/ppermute | solution.py:73
  319.9 19.9 %collective-permute-start.36 = (bf16[128,2048]{1,0:T(8,128)(2,1)S(1)}, bf16[128,2048]{1,0:T(8,128)(2,1)S(1)}, u32[]{:S(2)}, u32[]{:S(2)}) collective-permute-start(bf16[128,2048]{1,0:T(8,128)(2,1)S(1)} %get-tuple-element.87), channel_id=1, source_target_pairs={{0,16},{8,24},{16,0},{24,8},{1,17},{9,25},{17,1},{25,9},{2,18},{10... | collective-permute-start | bytes 1572872 | tf_op jit(solution)/shard_map/db_dp1/ppermute | solution.py:73
  328.8 20.4 %collective-permute-start.33 = (bf16[128,2048]{1,0:T(8,128)(2,1)S(1)}, bf16[128,2048]{1,0:T(8,128)(2,1)S(1)}, u32[]{:S(2)}, u32[]{:S(2)}) collective-permute-start(bf16[128,2048]{1,0:T(8,128)(2,1)S(1)} %pad_maximum_fusion.12), channel_id=1, source_target_pairs={{0,16},{8,24},{16,0},{24,8},{1,17},{9,25},{17,1},{25,9},{2,18},{10... | collective-permute-start | bytes 1572872 | tf_op jit(solution)/shard_map/result_dp1/ppermute | solution.py:73
  383.8 19.7 %collective-permute-start.39 = (bf16[1024,128]{1,0:T(8,128)(2,1)S(1)}, bf16[1024,128]{1,0:T(8,128)(2,1)S(1)}, u32[]{:S(2)}, u32[]{:S(2)}) collective-permute-start(bf16[1024,128]{1,0:T(8,128)(2,1)S(1)} %slice.315), channel_id=1, source_target_pairs={{0,2},{1,3},{2,0},{3,1},{4,6},{5,7},{6,4},{7,5},{8,10},{9,11},{10,... | collective-permute-start | bytes 786440 | tf_op jit(solution)/shard_map/dkv_ctx1/ppermute | solution.py:73
  389.0 24.4 %collective-permute-start.40 = (bf16[1024,512]{1,0:T(8,128)(2,1)}, bf16[1024,512]{1,0:T(8,128)(2,1)}, u32[]{:S(2)}, u32[]{:S(2)}) collective-permute-start(bf16[1024,512]{1,0:T(8,128)(2,1)} %slice.317), channel_id=1, source_target_pairs={{0,1},{1,0},{2,3},{3,2},{4,5},{5,4},{6,7},{7,6},{8,9},{9,8},{10,11... | collective-permute-start | bytes 3145736 | tf_op jit(solution)/shard_map/dq_w_ctx0/ppermute | solution.py:73
  426.8 24.4 %collective-permute-start.52 = (bf16[256,2048]{1,0:T(8,128)(2,1)S(1)}, bf16[256,2048]{1,0:T(8,128)(2,1)S(1)}, u32[]{:S(2)}, u32[]{:S(2)}) collective-permute-start(bf16[256,2048]{1,0:T(8,128)(2,1)S(1)} %bitcast.72), channel_id=1, source_target_pairs={{0,1},{1,0},{2,3},{3,2},{4,5},{5,4},{6,7},{7,6},{8,9},{9,8},{10,11... | collective-permute-start | bytes 3145736 | tf_op jit(solution)/shard_map/dout_w_ctx0/ppermute | solution.py:73
  435.1 17.9 %collective-permute-start.45 = (bf16[256,512]{1,0:T(8,128)(2,1)S(1)}, bf16[256,512]{1,0:T(8,128)(2,1)S(1)}, u32[]{:S(2)}, u32[]{:S(2)}) collective-permute-start(bf16[256,512]{1,0:T(8,128)(2,1)S(1)} %slice.327), channel_id=1, source_target_pairs={{0,4},{1,5},{2,6},{3,7},{4,0},{5,1},{6,2},{7,3},{8,12},{9,13},{10,... | collective-permute-start | bytes 786440 | tf_op jit(solution)/shard_map/dq_w_ctx2/ppermute | solution.py:73
  437.2 15.9 %collective-permute-start.43 = (bf16[128,2048]{1,0:T(8,128)(2,1)S(1)}, bf16[128,2048]{1,0:T(8,128)(2,1)S(1)}, u32[]{:S(2)}, u32[]{:S(2)}) collective-permute-start(bf16[128,2048]{1,0:T(8,128)(2,1)S(1)} %get-tuple-element.129), channel_id=1, source_target_pairs={{0,16},{8,24},{16,0},{24,8},{1,17},{9,25},{17,1},{25,9},{2,18},{10... | collective-permute-start | bytes 1572872 | tf_op jit(solution)/shard_map/da1_dp1/ppermute | solution.py:73
  458.0 40.4 %all-to-all-start.3 = ((bf16[8,192,704]{2,1,0:T(8,128)(2,1)}), bf16[8,192,704]{2,1,0:T(8,128)(2,1)S(1)}, u32[]{:S(2)}, u32[]{:S(2)}) async-start(bf16[8,192,704]{2,1,0:T(8,128)(2,1)} %copy-done.3), calls=%async_computation.5 | async-start | bytes 4718592 | tf_op jit(solution)/shard_map/all_to_all | solution.py:807
  468.6 27.9 %collective-permute-start.54 = (bf16[64,2048]{1,0:T(8,128)(2,1)}, bf16[64,2048]{1,0:T(8,128)(2,1)}, u32[]{:S(2)}, u32[]{:S(2)}) collective-permute-start(bf16[64,2048]{1,0:T(8,128)(2,1)} %slice.347), channel_id=1, source_target_pairs={{0,4},{1,5},{2,6},{3,7},{4,0},{5,1},{6,2},{7,3},{8,12},{9,13},{10,... | collective-permute-start | bytes 786440 | tf_op jit(solution)/shard_map/dout_w_ctx2/ppermute | solution.py:73
  472.8 19.9 %collective-permute-start.50 = (bf16[64,640]{1,0:T(8,128)(2,1)}, bf16[64,640]{1,0:T(8,128)(2,1)}, u32[]{:S(2)}, u32[]{:S(2)}) collective-permute-start(bf16[64,640]{1,0:T(8,128)(2,1)} %get-tuple-element.136), channel_id=1, source_target_pairs={{0,16},{8,24},{16,0},{24,8},{1,17},{9,25},{17,1},{25,9},{2,18},{10... | collective-permute-start | bytes 245768 | tf_op jit(solution)/shard_map/back_dp/ppermute | solution.py:78
  474.3 19.2 %collective-permute-start.51 = (bf16[64,640]{1,0:T(8,128)(2,1)}, bf16[64,640]{1,0:T(8,128)(2,1)}, u32[]{:S(2)}, u32[]{:S(2)}) collective-permute-start(bf16[64,640]{1,0:T(8,128)(2,1)} %get-tuple-element.135), channel_id=1, source_target_pairs={{0,24},{8,16},{16,8},{24,0},{1,25},{9,17},{17,9},{25,1},{2,26},{10... | collective-permute-start | bytes 245768 | tf_op jit(solution)/shard_map/back_dp/ppermute | solution.py:78
  (108 other events, 1058.7 us)
Sparse Core Ops, SparseCore 0:
  69.1 60.7 all-gather.3
  135.0 58.5 all-gather.5
  195.2 57.8 all-gather.7
  255.3 54.8 reduce-scatter.2
  312.3 110.5 reduce-scatter.4

commit v7 on v5

--- a/solution.py
+++ b/solution.py
@@ -920,7 +920,7 @@
 
     grad_heads = dot_nt(grad_branch, out_full)
     dq, dkv = attend_back(
-        queries, kv, after(key_places, *result_two), grad_heads, cosine, sine, seq_dev
+        queries, kv, after(key_places, result_mark), grad_heads, cosine, sine, seq_dev
     )
 
     class Sum:
@@ -943,7 +943,7 @@
     dkv_first = dkv_sum.step()
     dq_sum = Sum(dot_tn(a1, after(dq, dkv_first)).astype(BF), "dq_w")
     dq_first = dq_sum.step()
-    dkv_sum.step(down_back)
+    dkv_sum.step(down_back, *result_two)
     dkv_two = dkv_sum.finish()
     dkv_low = run(
         functools.partial(turn_back_kernel, all_seqs),

time: 520 us -> 518 us (level)
  starting transfers between devices: 89.7 us -> 70.7 us
  waiting for transfers between devices: 213 us -> 231 us
    ppermute x49, starting transfers between devices: 67.6 us -> 48.5 us  [swap(): return lax.ppermute(value, self.axis, self.pairs)]
    ppermute x49, waiting for transfers between devices: 197 us -> 214 us  [swap(): return lax.ppermute(value, self.axis, self.pairs)]
    unnamed x164 -> x172, local copies, waits for them, and re-layouts: 35.8 us -> 36 us
  transfers between devices with their start and end apart: 62 -> 62, of which waited for: 32 -> 33; matrix products, arithmetic and copies ran while one was open for 14% -> 13% of each run, Pallas kernels for 19% -> 19%
where the time goes in v7:
time: 518 us; the launch traced here: 513 us
  waiting for transfers between devices  231 us (45%)
  Pallas kernels  101 us (19%)
  starting transfers between devices  70.7 us (14%)
  local copies, waits for them, and re-layouts  59.7 us (12%)
  other arithmetic  26 us (5%)
  between operations  15.4 us (3%)
  matrix products  10 us (2%)
    ppermute x49, waiting for transfers between devices, swap(): return lax.ppermute(value, self.axis, self.pairs)  214 us
    pallas_call x25, Pallas kernels, run(): pl.pallas_call(kernel, name=name, out_shape=list(outs), in_specs=specs or...  101 us
    ppermute x49, starting transfers between devices, swap(): return lax.ppermute(value, self.axis, self.pairs)  48.5 us
    unnamed x172, local copies, waits for them, and re-layouts  36 us
    all_to_all x3, starting transfers between devices, mlp_trade(): lax.all_to_all(parts, ('dp', 'ctx'), 0, 0, axis_index_groups=team_groups,...  12.2 us
    convert_element_type x18, other arithmetic, add_low(): return (a.astype(F32) + b.astype(F32)).astype(BF)  12.2 us
  transfers between devices with their start and end apart: 62, of which 33 were waited for; matrix products, arithmetic and copies ran while one was open for 13% of the time, Pallas kernels for 19%

profile of v7, /device:TPU:0, one launch (start us, length us, event | category | flops | bytes accessed | tf_op | source)
XLA Modules:
  0.0 513.2 jit_solution(8572934972149784074)
XLA Ops:
  7.2 4.1 collective-permute-start
  17.5 5.9 %collective-permute-done = bf16[64,2048]{1,0:T(8,128)(2,1)S(1)} collective-permute-done((bf16[64,2048]{1,0:T(8,128)(2,1)}, bf16[64,2048]{1,0:T(8,128)(2,1)S(1)}, u32[]{:S(2)}, u32[]{:S(2)}) %collective-permute-start) | collective-permute-done | bytes 262176 | tf_op jit(solution)/shard_map/out_ctx2/ppermute | solution.py:73
  31.2 4.4 all-to-all-start
  35.7 8.0 %collective-permute-done.4 = bf16[256,640]{1,0:T(8,128)(2,1)S(1)} collective-permute-done((bf16[256,640]{1,0:T(8,128)(2,1)}, bf16[256,640]{1,0:T(8,128)(2,1)S(1)}, u32[]{:S(2)}, u32[]{:S(2)}) %collective-permute-start.4) | collective-permute-done | bytes 327712 | tf_op jit(solution)/shard_map/qkv_ctx2/ppermute | solution.py:73
  50.8 14.3 %collective-permute-done.6 = bf16[512,640]{1,0:T(8,128)(2,1)S(1)} collective-permute-done((bf16[512,640]{1,0:T(8,128)(2,1)S(1)}, bf16[512,640]{1,0:T(8,128)(2,1)S(1)}, u32[]{:S(2)}, u32[]{:S(2)}) %collective-permute-start.6) | collective-permute-done | bytes 655392 | tf_op jit(solution)/shard_map/qkv_ctx1/ppermute | solution.py:73
  70.3 4.1 all-to-all-start.1
  74.5 6.9 %all-to-all-done.1 = bf16[32,1,64]{2,1,0:T(2,128)(2,1)S(1)} async-done(((bf16[32,1,64]{2,1,0:T(2,128)(2,1)}), bf16[32,1,64]{2,1,0:T(2,128)(2,1)S(1)}, u32[]{:S(2)}, u32[]{:S(2)}) %all-to-all-start.1) | async-done | bytes 4128 | tf_op jit(solution)/shard_map/all_to_all | solution.py:865
  84.3 12.5 %collective-permute-done.7 = bf16[128,2048]{1,0:T(8,128)(2,1)S(1)} collective-permute-done((bf16[128,2048]{1,0:T(8,128)(2,1)S(1)}, bf16[128,2048]{1,0:T(8,128)(2,1)S(1)}, u32[]{:S(2)}, u32[]{:S(2)}) %collective-permute-start.7) | collective-permute-done | bytes 524320 | tf_op jit(solution)/shard_map/a1_dp1/ppermute | solution.py:73
  100.1 4.2 all-to-all-start.2
  106.5 13.1 %collective-permute-done.9.refs_4_.refs_1_ = bf16[1024,640]{1,0:T(8,128)(2,1)S(1)} collective-permute-done((bf16[1024,640]{1,0:T(8,128)(2,1)S(1)}, bf16[1024,640]{1,0:T(8,128)(2,1)S(1)}, u32[]{:S(2)}, u32[]{:S(2)}) %collective-permute-start.9) | collective-permute-done | bytes 1310752 | tf_op jit(solution)/shard_map/qkv_ctx0/ppermute | solution.py:73
  129.3 4.6 collective-permute-done.10
  135.2 6.1 %collective-permute-done.11 = bf16[1024,128]{1,0:T(8,128)(2,1)S(1)} collective-permute-done((bf16[1024,128]{1,0:T(8,128)(2,1)S(1)}, bf16[1024,128]{1,0:T(8,128)(2,1)S(1)}, u32[]{:S(2)}, u32[]{:S(2)}) %collective-permute-start.11) | collective-permute-done | bytes 262176 | tf_op jit(solution)/shard_map/kv_ctx1/ppermute | solution.py:73
  148.2 7.8 %collective-permute-done.12 = bf16[2048,128]{1,0:T(8,128)(2,1)S(1)} collective-permute-done((bf16[2048,128]{1,0:T(8,128)(2,1)S(1)}, bf16[2048,128]{1,0:T(8,128)(2,1)S(1)}, u32[]{:S(2)}, u32[]{:S(2)}) %collective-permute-start.12) | collective-permute-done | bytes 524320 | tf_op jit(solution)/shard_map/kv_ctx0/ppermute | solution.py:73
  156.1 5.3 %attend_kernel.1 = bf16[512,512]{1,0:T(8,128)(2,1)S(1)} custom-call(bf16[512,512]{1,0:T(8,128)(2,1)S(1)} %copy-done.26, bf16[8,8,64,128]{3,2,1,0:T(8,128)(2,1)S(1)} %bitcast.46, s32[1,512]{1,0:T(1,128)S(1)} %add.218.key_ref), custom_call_target="tpu_custom_call" | custom-call | tf_op jit(solution)/shard_map/attend_kernel/pallas_call | solution.py:47
  167.5 12.5 %collective-permute-done.15.b_ref = bf16[128,2048]{1,0:T(8,128)(2,1)S(1)} collective-permute-done((bf16[128,2048]{1,0:T(8,128)(2,1)S(1)}, bf16[128,2048]{1,0:T(8,128)(2,1)S(1)}, u32[]{:S(2)}, u32[]{:S(2)}) %collective-permute-start.15) | collective-permute-done | bytes 524320 | tf_op jit(solution)/shard_map/branch_dp1/ppermute | solution.py:73
  189.7 8.7 %collective-permute-done.22 = bf16[128,2048]{1,0:T(8,128)(2,1)} collective-permute-done((bf16[128,2048]{1,0:T(8,128)(2,1)S(1)}, bf16[128,2048]{1,0:T(8,128)(2,1)}, u32[]{:S(2)}, u32[]{:S(2)}) %collective-permute-start.22) | collective-permute-done | bytes 524320 | tf_op jit(solution)/shard_map/gb_ctx0/ppermute | solution.py:73
  202.6 7.0 %collective-permute-done.17 = bf16[128,2048]{1,0:T(8,128)(2,1)} collective-permute-done((bf16[128,2048]{1,0:T(8,128)(2,1)}, bf16[128,2048]{1,0:T(8,128)(2,1)}, u32[]{:S(2)}, u32[]{:S(2)}) %collective-permute-start.17) | collective-permute-done | bytes 524320 | tf_op jit(solution)/shard_map/a2_ctx0/ppermute | solution.py:73
  224.2 11.7 %gate_kernel.1 = (bf16[1024,704]{1,0:T(8,128)(2,1)S(1)}, f32[1024,704]{1,0:T(8,128)}, f32[1024,704]{1,0:T(8,128)}) custom-call(bf16[512,2048]{1,0:T(8,128)(2,1)S(1)} %constant_dynamic-update-slice_fusion.7.first_ref, bf16[512,2048]{1,0:T(8,128)(2,1)} %collective-permute-done.20.second_ref, bf16[2816,512]{1,0:T(8,128)(2,1)} %all-gather.4.cloned.1.call-done.gate_ref, ...), custom_call_target="tpu_custom_call" | custom-call | tf_op jit(solution)/shard_map/gate_kernel/pallas_call | solution.py:47
  235.9 6.5 %weight_grad_kernel.2 = bf16[2816,512]{1,0:T(8,128)(2,1)} custom-call(bf16[1024,704]{1,0:T(8,128)(2,1)S(1)} %get-tuple-element.83.left_ref.h_ref, bf16[512,2048]{1,0:T(8,128)(2,1)} %constant_dynamic-update-slice_fusion.12.first_ref, bf16[512,2048]{1,0:T(8,128)(2,1)} %collective-permute-done.25.second_ref), custom_call_target="tpu_custom_call" | custom-call | tf_op jit(solution)/shard_map/weight_grad_kernel/pallas_call | solution.py:47
  243.6 9.7 %all-gather.8.cloned.1.call-done.down_ref = bf16[2816,512]{1,0:T(8,128)(2,1)} async-done(((bf16[704,512]{1,0:T(8,128)(2,1)}), bf16[2816,512]{1,0:T(8,128)(2,1)}) %all-gather.8.cloned.1.call-update) | async-done | bytes 2883600 | tf_op jit(solution)/shard_map/all_gather | solution.py:828
  253.4 16.5 %hidden_kernel.1 = (bf16[1024,1408]{1,0:T(8,128)(2,1)}, bf16[1024,2048]{1,0:T(8,128)(2,1)}) custom-call(bf16[512,2048]{1,0:T(8,128)(2,1)} %constant_dynamic-update-slice_fusion.12.first_ref, bf16[512,2048]{1,0:T(8,128)(2,1)} %collective-permute-done.25.second_ref, f32[1024,704]{1,0:T(8,128)} %get-tuple-element.79.one_ref, ...), custom_call_target="tpu_custom_call" | custom-call | tf_op jit(solution)/shard_map/hidden_kernel/pallas_call | solution.py:47
  271.9 4.1 collective-permute-done.26
  280.7 5.4 %collective-permute-done.27 = bf16[64,2048]{1,0:T(8,128)(2,1)S(1)} collective-permute-done((bf16[64,2048]{1,0:T(8,128)(2,1)S(1)}, bf16[64,2048]{1,0:T(8,128)(2,1)S(1)}, u32[]{:S(2)}, u32[]{:S(2)}) %collective-permute-start.27) | collective-permute-done | bytes 262176 | tf_op jit(solution)/shard_map/da2_ctx0/ppermute | solution.py:73
  289.0 10.0 %weight_grad_kernel.3 = bf16[5632,512]{1,0:T(8,128)(2,1)} custom-call(bf16[1024,1408]{1,0:T(8,128)(2,1)} %get-tuple-element.85.left_ref, bf16[512,2048]{1,0:T(8,128)(2,1)S(1)} %constant_dynamic-update-slice_fusion.7.first_ref, bf16[512,2048]{1,0:T(8,128)(2,1)} %collective-permute-done.20.second_ref), custom_call_target="tpu_custom_call" | custom-call | tf_op jit(solution)/shard_map/weight_grad_kernel/pallas_call | solution.py:47
  309.5 11.3 %collective-permute-done.29 = bf16[128,2048]{1,0:T(8,128)(2,1)S(1)} collective-permute-done((bf16[128,2048]{1,0:T(8,128)(2,1)S(1)}, bf16[128,2048]{1,0:T(8,128)(2,1)S(1)}, u32[]{:S(2)}, u32[]{:S(2)}) %collective-permute-start.29) | collective-permute-done | bytes 524320 | tf_op jit(solution)/shard_map/da2_dp1/ppermute | solution.py:73
  327.2 11.1 %collective-permute-done.36 = bf16[128,2048]{1,0:T(8,128)(2,1)S(1)} collective-permute-done((bf16[128,2048]{1,0:T(8,128)(2,1)S(1)}, bf16[128,2048]{1,0:T(8,128)(2,1)S(1)}, u32[]{:S(2)}, u32[]{:S(2)}) %collective-permute-start.36) | collective-permute-done | bytes 524320 | tf_op jit(solution)/shard_map/db_dp1/ppermute | solution.py:73
  346.6 20.2 %attend_back_kernel.1 = (bf16[512,512]{1,0:T(8,128)(2,1)S(1)}, bf16[8,8,64,128]{3,2,1,0:T(8,128)(2,1)S(1)}) custom-call(bf16[512,512]{1,0:T(8,128)(2,1)S(1)} %copy-done.27, bf16[8,8,64,128]{3,2,1,0:T(8,128)(2,1)S(1)} %bitcast.47, s32[1,512]{1,0:T(1,128)S(1)} %add.218.key_ref, f32[512,512]{1,0:T(8,128)S(1)} %fusion.20.do_ref, f32[64,640]{1,0:T(8,128)S(1)} %copy-done.22, ...), custom_call_target="tpu_custom_call" | custom-call | tf_op jit(solution)/shard_map/attend_back_kernel/pallas_call | solution.py:47
  369.3 12.6 %collective-permute-done.38 = bf16[2048,128]{1,0:T(8,128)(2,1)S(1)} collective-permute-done((bf16[2048,128]{1,0:T(8,128)(2,1)S(1)}, bf16[2048,128]{1,0:T(8,128)(2,1)S(1)}, u32[]{:S(2)}, u32[]{:S(2)}) %collective-permute-start.38) | collective-permute-done | bytes 524320 | tf_op jit(solution)/shard_map/dkv_ctx0/ppermute | solution.py:73
  382.8 7.0 %collective-permute-done.35.b_ref = bf16[128,2048]{1,0:T(8,128)(2,1)S(1)} collective-permute-done((bf16[128,2048]{1,0:T(8,128)(2,1)S(1)}, bf16[128,2048]{1,0:T(8,128)(2,1)S(1)}, u32[]{:S(2)}, u32[]{:S(2)}) %collective-permute-start.35) | collective-permute-done | bytes 524320 | tf_op jit(solution)/shard_map/result_ctx0/ppermute | solution.py:73
  396.5 16.4 %collective-permute-done.39 = bf16[1024,128]{1,0:T(8,128)(2,1)} collective-permute-done((bf16[1024,128]{1,0:T(8,128)(2,1)}, bf16[1024,128]{1,0:T(8,128)(2,1)}, u32[]{:S(2)}, u32[]{:S(2)}) %collective-permute-start.39) | collective-permute-done | bytes 262176 | tf_op jit(solution)/shard_map/dkv_ctx1/ppermute | solution.py:73
  448.3 15.8 %collective-permute-done.49 = bf16[256,2048]{1,0:T(8,128)(2,1)} collective-permute-done((bf16[256,2048]{1,0:T(8,128)(2,1)}, bf16[256,2048]{1,0:T(8,128)(2,1)}, u32[]{:S(2)}, u32[]{:S(2)}) %collective-permute-start.49) | collective-permute-done | bytes 1048608 | tf_op jit(solution)/shard_map/dout_w_ctx0/ppermute | solution.py:73
  488.1 7.6 %collective-permute-done.51 = bf16[64,2048]{1,0:T(8,128)(2,1)} collective-permute-done((bf16[64,2048]{1,0:T(8,128)(2,1)}, bf16[64,2048]{1,0:T(8,128)(2,1)}, u32[]{:S(2)}, u32[]{:S(2)}) %collective-permute-start.51) | collective-permute-done | bytes 262176 | tf_op jit(solution)/shard_map/dout_w_ctx2/ppermute | solution.py:73
  (390 shorter events, 202.2 us)
Async XLA Ops:
  7.2 16.2 %collective-permute-start = (bf16[64,2048]{1,0:T(8,128)(2,1)}, bf16[64,2048]{1,0:T(8,128)(2,1)S(1)}, u32[]{:S(2)}, u32[]{:S(2)}) collective-permute-start(bf16[64,2048]{1,0:T(8,128)(2,1)} %param.17), channel_id=1, source_target_pairs={{0,4},{1,5},{2,6},{3,7},{4,0},{5,1},{6,2},{7,3},{8,12},{9,13},{10,... | collective-permute-start | bytes 786440 | tf_op jit(solution)/shard_map/out_ctx2/ppermute | solution.py:73
  24.2 20.6 %collective-permute-start.5 = (bf16[128,2048]{1,0:T(8,128)(2,1)}, bf16[128,2048]{1,0:T(8,128)(2,1)}, u32[]{:S(2)}, u32[]{:S(2)}) collective-permute-start(bf16[128,2048]{1,0:T(8,128)(2,1)} %get-tuple-element.144), channel_id=1, source_target_pairs={{0,2},{1,3},{2,0},{3,1},{4,6},{5,7},{6,4},{7,5},{8,10},{9,11},{10,... | collective-permute-start | bytes 1572872 | tf_op jit(solution)/shard_map/out_ctx1/ppermute | solution.py:73
  25.9 17.8 %collective-permute-start.4 = (bf16[256,640]{1,0:T(8,128)(2,1)}, bf16[256,640]{1,0:T(8,128)(2,1)S(1)}, u32[]{:S(2)}, u32[]{:S(2)}) collective-permute-start(bf16[256,640]{1,0:T(8,128)(2,1)} %bitcast.9), channel_id=1, source_target_pairs={{0,4},{1,5},{2,6},{3,7},{4,0},{5,1},{6,2},{7,3},{8,12},{9,13},{10,... | collective-permute-start | bytes 983048 | tf_op jit(solution)/shard_map/qkv_ctx2/ppermute | solution.py:73
  31.2 34.0 %all-to-all-start = ((bf16[8,128,704]{1,2,0:T(8,128)(2,1)}), bf16[8,128,704]{1,2,0:T(8,128)(2,1)}, u32[]{:S(2)}, u32[]{:S(2)}) async-start(bf16[8,128,704]{1,2,0:T(8,128)(2,1)} %copy.31), calls=%async_computation | async-start | bytes 2883584 | tf_op jit(solution)/shard_map/all_to_all | solution.py:807
  35.6 186.2 %all-gather.4.cloned.1.call-start = ((), (), s32[]{:S(2)}) async-start(), calls=%async_computation.7 | async-start | bytes 3604480 | tf_op jit(solution)/shard_map/all_gather | solution.py:828
  46.8 18.3 %collective-permute-start.6 = (bf16[512,640]{1,0:T(8,128)(2,1)S(1)}, bf16[512,640]{1,0:T(8,128)(2,1)S(1)}, u32[]{:S(2)}, u32[]{:S(2)}) collective-permute-start(bf16[512,640]{1,0:T(8,128)(2,1)S(1)} %pad_maximum_fusion.7), channel_id=1, source_target_pairs={{0,2},{1,3},{2,0},{3,1},{4,6},{5,7},{6,4},{7,5},{8,10},{9,11},{10,... | collective-permute-start | bytes 1966088 | tf_op jit(solution)/shard_map/qkv_ctx1/ppermute | solution.py:73
  83.7 35.9 %collective-permute-start.9 = (bf16[1024,640]{1,0:T(8,128)(2,1)S(1)}, bf16[1024,640]{1,0:T(8,128)(2,1)S(1)}, u32[]{:S(2)}, u32[]{:S(2)}) collective-permute-start(bf16[1024,640]{1,0:T(8,128)(2,1)S(1)} %constant_dynamic-update-slice_fusion.5.refs_3_.refs_0_), channel_id=1, source_target_pairs={{0,1},{1,0},{2,3},{3,2},{4,5},{5,4},{6,7},{7,6},{8,9},{9,8},{10,11... | collective-permute-start | bytes 3932168 | tf_op jit(solution)/shard_map/qkv_ctx0/ppermute | solution.py:73
  97.9 22.3 %collective-permute-start.8 = (bf16[256,2048]{1,0:T(8,128)(2,1)}, bf16[256,2048]{1,0:T(8,128)(2,1)}, u32[]{:S(2)}, u32[]{:S(2)}) collective-permute-start(bf16[256,2048]{1,0:T(8,128)(2,1)} %pad_maximum_fusion.2), channel_id=1, source_target_pairs={{0,8},{8,0},{16,24},{24,16},{1,9},{9,1},{17,25},{25,17},{2,10},{10... | collective-permute-start | bytes 3145736 | tf_op jit(solution)/shard_map/a1_dp0/ppermute | solution.py:73
  100.1 26.9 %all-to-all-start.2 = ((bf16[8,64,704]{2,1,0:T(8,128)(2,1)}), bf16[8,64,704]{2,1,0:T(8,128)(2,1)}, u32[]{:S(2)}, u32[]{:S(2)}) async-start(bf16[8,64,704]{2,1,0:T(8,128)(2,1)} %copy-done.16), calls=%async_computation.2 | async-start | bytes 1572864 | tf_op jit(solution)/shard_map/all_to_all | solution.py:807
  104.3 117.5 %all-gather.6.cloned.1.call-start = ((), (), s32[]{:S(2)}) async-start(), calls=%async_computation.8 | async-start | bytes 3604480 | tf_op jit(solution)/shard_map/all_gather | solution.py:828
  119.6 26.8 %collective-permute-start.13 = (bf16[256,2048]{1,0:T(8,128)(2,1)}, bf16[256,2048]{1,0:T(8,128)(2,1)}, u32[]{:S(2)}, u32[]{:S(2)}) collective-permute-start(bf16[256,2048]{1,0:T(8,128)(2,1)} %copy-done.61), channel_id=1, source_target_pairs={{0,1},{1,0},{2,3},{3,2},{4,5},{5,4},{6,7},{7,6},{8,9},{9,8},{10,11... | collective-permute-start | bytes 3145736 | tf_op jit(solution)/shard_map/out_ctx0/ppermute | solution.py:73
  135.2 118.2 %all-gather.8.cloned.1.call-start = ((), (), s32[]{:S(2)}) async-start(), calls=%async_computation.9 | async-start | bytes 3604480 | tf_op jit(solution)/shard_map/all_gather | solution.py:828
  183.4 15.0 %collective-permute-start.22 = (bf16[128,2048]{1,0:T(8,128)(2,1)S(1)}, bf16[128,2048]{1,0:T(8,128)(2,1)}, u32[]{:S(2)}, u32[]{:S(2)}) collective-permute-start(bf16[128,2048]{1,0:T(8,128)(2,1)S(1)} %order_kernel.1), channel_id=1, source_target_pairs={{0,1},{1,0},{2,3},{3,2},{4,5},{5,4},{6,7},{7,6},{8,9},{9,8},{10,11... | collective-permute-start | bytes 1572872 | tf_op jit(solution)/shard_map/gb_ctx0/ppermute | solution.py:73
  184.0 16.9 %collective-permute-start.21 = (bf16[128,2048]{1,0:T(8,128)(2,1)S(1)}, bf16[128,2048]{1,0:T(8,128)(2,1)}, u32[]{:S(2)}, u32[]{:S(2)}) collective-permute-start(bf16[128,2048]{1,0:T(8,128)(2,1)S(1)} %order_kernel.1), channel_id=1, source_target_pairs={{0,16},{8,24},{16,0},{24,8},{1,17},{9,25},{17,1},{25,9},{2,18},{10... | collective-permute-start | bytes 1572872 | tf_op jit(solution)/shard_map/gb_dp1/ppermute | solution.py:73
  185.5 24.1 %collective-permute-start.17 = (bf16[128,2048]{1,0:T(8,128)(2,1)}, bf16[128,2048]{1,0:T(8,128)(2,1)}, u32[]{:S(2)}, u32[]{:S(2)}) collective-permute-start(bf16[128,2048]{1,0:T(8,128)(2,1)} %get-tuple-element.73), channel_id=1, source_target_pairs={{0,1},{1,0},{2,3},{3,2},{4,5},{5,4},{6,7},{7,6},{8,9},{9,8},{10,11... | collective-permute-start | bytes 1572872 | tf_op jit(solution)/shard_map/a2_ctx0/ppermute | solution.py:73
  186.9 25.2 %collective-permute-start.16 = (bf16[128,2048]{1,0:T(8,128)(2,1)}, bf16[128,2048]{1,0:T(8,128)(2,1)}, u32[]{:S(2)}, u32[]{:S(2)}) collective-permute-start(bf16[128,2048]{1,0:T(8,128)(2,1)} %get-tuple-element.73), channel_id=1, source_target_pairs={{0,16},{8,24},{16,0},{24,8},{1,17},{9,25},{17,1},{25,9},{2,18},{10... | collective-permute-start | bytes 1572872 | tf_op jit(solution)/shard_map/a2_dp1/ppermute | solution.py:73
  187.5 203.1 %reduce-scatter.3.cloned.1.call-start = ((), (), s32[]{:S(2)}) async-start(), calls=%async_computation.10 | async-start | bytes 3604480 | tf_op jit(solution)/shard_map/reduce_scatter | solution.py:831
  199.4 20.6 %collective-permute-start.23 = (bf16[64,2048]{1,0:T(8,128)(2,1)S(1)}, bf16[64,2048]{1,0:T(8,128)(2,1)S(1)}, u32[]{:S(2)}, u32[]{:S(2)}) collective-permute-start(bf16[64,2048]{1,0:T(8,128)(2,1)S(1)} %slice.260), channel_id=1, source_target_pairs={{0,16},{8,24},{16,0},{24,8},{1,17},{9,25},{17,1},{25,9},{2,18},{10... | collective-permute-start | bytes 786440 | tf_op jit(solution)/shard_map/gb_dp1/ppermute | solution.py:73
  201.9 18.8 %collective-permute-start.24 = (bf16[64,2048]{1,0:T(8,128)(2,1)S(1)}, bf16[64,2048]{1,0:T(8,128)(2,1)S(1)}, u32[]{:S(2)}, u32[]{:S(2)}) collective-permute-start(bf16[64,2048]{1,0:T(8,128)(2,1)S(1)} %slice.261), channel_id=1, source_target_pairs={{0,1},{1,0},{2,3},{3,2},{4,5},{5,4},{6,7},{7,6},{8,9},{9,8},{10,11... | collective-permute-start | bytes 786440 | tf_op jit(solution)/shard_map/gb_ctx0/ppermute | solution.py:73
  243.6 197.6 %reduce-scatter.5.cloned.1.call-start = ((), (), s32[]{:S(2)}) async-start(), calls=%async_computation.11 | async-start | bytes 7208960 | tf_op jit(solution)/shard_map/reduce_scatter | solution.py:831
  306.4 15.6 %collective-permute-start.28 = (bf16[512,2048]{1,0:T(8,128)(2,1)S(1)}, bf16[512,2048]{1,0:T(8,128)(2,1)S(1)}, u32[]{:S(2)}, u32[]{:S(2)}) collective-permute-start(bf16[512,2048]{1,0:T(8,128)(2,1)S(1)} %slice.263), channel_id=1, source_target_pairs={{0,8},{8,0},{16,24},{24,16},{1,9},{9,1},{17,25},{25,17},{2,10},{10... | collective-permute-start | bytes 6291464 | tf_op jit(solution)/shard_map/result_dp0/ppermute | solution.py:73
  326.6 15.2 %collective-permute-start.34 = (bf16[64,2048]{1,0:T(8,128)(2,1)S(1)}, bf16[64,2048]{1,0:T(8,128)(2,1)S(1)}, u32[]{:S(2)}, u32[]{:S(2)}) collective-permute-start(bf16[64,2048]{1,0:T(8,128)(2,1)S(1)} %get-tuple-element.121), channel_id=1, source_target_pairs={{0,16},{8,24},{16,0},{24,8},{1,17},{9,25},{17,1},{25,9},{2,18},{10... | collective-permute-start | bytes 786440 | tf_op jit(solution)/shard_map/result_dp1/ppermute | solution.py:73
  342.0 27.1 %collective-permute-start.33 = (bf16[128,2048]{1,0:T(8,128)(2,1)S(1)}, bf16[128,2048]{1,0:T(8,128)(2,1)S(1)}, u32[]{:S(2)}, u32[]{:S(2)}) collective-permute-start(bf16[128,2048]{1,0:T(8,128)(2,1)S(1)} %pad_maximum_fusion.12), channel_id=1, source_target_pairs={{0,16},{8,24},{16,0},{24,8},{1,17},{9,25},{17,1},{25,9},{2,18},{10... | collective-permute-start | bytes 1572872 | tf_op jit(solution)/shard_map/result_dp1/ppermute | solution.py:73
  367.7 22.1 %collective-permute-start.35 = (bf16[128,2048]{1,0:T(8,128)(2,1)S(1)}, bf16[128,2048]{1,0:T(8,128)(2,1)S(1)}, u32[]{:S(2)}, u32[]{:S(2)}) collective-permute-start(bf16[128,2048]{1,0:T(8,128)(2,1)S(1)} %pad_maximum_fusion.13), channel_id=1, source_target_pairs={{0,1},{1,0},{2,3},{3,2},{4,5},{5,4},{6,7},{7,6},{8,9},{9,8},{10,11... | collective-permute-start | bytes 1572872 | tf_op jit(solution)/shard_map/result_ctx0/ppermute | solution.py:73
  390.6 22.3 %collective-permute-start.39 = (bf16[1024,128]{1,0:T(8,128)(2,1)}, bf16[1024,128]{1,0:T(8,128)(2,1)}, u32[]{:S(2)}, u32[]{:S(2)}) collective-permute-start(bf16[1024,128]{1,0:T(8,128)(2,1)} %slice.279), channel_id=1, source_target_pairs={{0,2},{1,3},{2,0},{3,1},{4,6},{5,7},{6,4},{7,5},{8,10},{9,11},{10,... | collective-permute-start | bytes 786440 | tf_op jit(solution)/shard_map/dkv_ctx1/ppermute | solution.py:73
  395.8 22.3 %collective-permute-start.40 = (bf16[1024,512]{0,1:T(8,128)(2,1)}, bf16[1024,512]{0,1:T(8,128)(2,1)}, u32[]{:S(2)}, u32[]{:S(2)}) collective-permute-start(bf16[1024,512]{0,1:T(8,128)(2,1)} %slice.281), channel_id=1, source_target_pairs={{0,1},{1,0},{2,3},{3,2},{4,5},{5,4},{6,7},{7,6},{8,9},{9,8},{10,11... | collective-permute-start | bytes 3145736 | tf_op jit(solution)/shard_map/dq_w_ctx0/ppermute | solution.py:73
  431.4 32.6 %collective-permute-start.49 = (bf16[256,2048]{1,0:T(8,128)(2,1)}, bf16[256,2048]{1,0:T(8,128)(2,1)}, u32[]{:S(2)}, u32[]{:S(2)}) collective-permute-start(bf16[256,2048]{1,0:T(8,128)(2,1)} %bitcast.24), channel_id=1, source_target_pairs={{0,1},{1,0},{2,3},{3,2},{4,5},{5,4},{6,7},{7,6},{8,9},{9,8},{10,11... | collective-permute-start | bytes 3145736 | tf_op jit(solution)/shard_map/dout_w_ctx0/ppermute | solution.py:73
  437.0 36.1 %collective-permute-start.45 = (bf16[256,512]{0,1:T(8,128)(2,1)}, bf16[256,512]{0,1:T(8,128)(2,1)}, u32[]{:S(2)}, u32[]{:S(2)}) collective-permute-start(bf16[256,512]{0,1:T(8,128)(2,1)} %slice.291), channel_id=1, source_target_pairs={{0,4},{1,5},{2,6},{3,7},{4,0},{5,1},{6,2},{7,3},{8,12},{9,13},{10,... | collective-permute-start | bytes 786440 | tf_op jit(solution)/shard_map/dq_w_ctx2/ppermute | solution.py:73
  438.4 28.5 %collective-permute-start.47 = (bf16[512,128]{0,1:T(8,128)(2,1)}, bf16[512,128]{0,1:T(8,128)(2,1)S(1)}, u32[]{:S(2)}, u32[]{:S(2)}) collective-permute-start(bf16[512,128]{0,1:T(8,128)(2,1)} %slice.295), channel_id=1, source_target_pairs={{0,2},{1,3},{2,0},{3,1},{4,6},{5,7},{6,4},{7,5},{8,10},{9,11},{10,... | collective-permute-start | bytes 393224 | tf_op jit(solution)/shard_map/dkv_w_ctx1/ppermute | solution.py:73
  439.9 34.3 %collective-permute-start.43 = (bf16[128,2048]{1,0:T(8,128)(2,1)}, bf16[128,2048]{1,0:T(8,128)(2,1)}, u32[]{:S(2)}, u32[]{:S(2)}) collective-permute-start(bf16[128,2048]{1,0:T(8,128)(2,1)} %get-tuple-element.131), channel_id=1, source_target_pairs={{0,16},{8,24},{16,0},{24,8},{1,17},{9,25},{17,1},{25,9},{2,18},{10... | collective-permute-start | bytes 1572872 | tf_op jit(solution)/shard_map/da1_dp1/ppermute | solution.py:73
  444.6 40.0 %all-to-all-start.3 = ((bf16[8,192,704]{2,1,0:T(8,128)(2,1)}), bf16[8,192,704]{2,1,0:T(8,128)(2,1)S(1)}, u32[]{:S(2)}, u32[]{:S(2)}) async-start(bf16[8,192,704]{2,1,0:T(8,128)(2,1)} %copy-done.3), calls=%async_computation.5 | async-start | bytes 4718592 | tf_op jit(solution)/shard_map/all_to_all | solution.py:807
  484.7 19.8 %all-to-all-start.4 = ((bf16[4,64,640]{2,1,0:T(8,128)(2,1)}), bf16[4,64,640]{2,1,0:T(8,128)(2,1)S(1)}, u32[]{:S(2)}, u32[]{:S(2)}) async-start(bf16[4,64,640]{2,1,0:T(8,128)(2,1)} %bitcast.63), calls=%async_computation.6 | async-start | bytes 655360 | tf_op jit(solution)/shard_map/all_to_all | solution.py:972
  (106 other events, 806.8 us)
Sparse Core Ops, SparseCore 0:
  69.8 60.6 all-gather.3
  135.3 58.5 all-gather.5
  195.5 57.8 all-gather.7
  255.5 54.8 reduce-scatter.2
  312.6 110.5 reduce-scatter.4
